TPU v7x, 128 devices: a whole 4x4x4 slice. The times are simulated.
128 devices in a mesh: row: 8 (over x, core), col: 16 (over z, y).
Axes of the slice: x: 4, y: 4, z: 4, core: 2. Of those that a mesh axis runs over, the one named last changes fastest.
Arguments:
- points: float32 [3, 262144], P(None, ('row', 'col')), may hold values from 0 to 1
- targets: float32 [262144], P(('row', 'col')), may hold values from -0.75 to 3.75
- kd_order: int32 [262144], P(('row', 'col')), may hold values from 0 to 2047, as said below
- lengthscales: float32 [8], replicated, may hold values from 0.5 to 2.14, as said below
- noise_level: float32 [8], replicated, may hold values from 2 to 4
- block_owner: int32 [512], replicated, may hold values from 0 to 511, as said below
- block_pairs: int32 [3, 2048], replicated, may hold values from 0 to 511, as said below
Outputs:
- solution: float32 [8, 262144], P(None, ('row', 'col'))
- residual: float32 [8, 262144], P(None, ('row', 'col'))
Inputs may be any that keep to these rules, and one draw needn't show every extreme that they name: `kd_order`: each device's 2048 entries are a permutation of 0 to 2047. `block_owner`: A permutation: the slot of each block id; slot s is local block s % 4 of device s // 4. `block_pairs`: rows 0 and 1 are block ids, row 2 a lengthscale index below 8. Columns 16 d to 16 d + 15 are device d's pairs: the first block's slot lies on device d, the second block's on another device with the same row index. At most 2 of one device's pairs have their second block on one device, and exactly 2 on some device, for every device. `lengthscales`: Ascending.
All inputs are finite; a program needn't handle non-finite values.
Results may differ from a plain program's by a relative error of at most 0.00071.
Values may be sent and summed in bfloat16 or wider, within the bound.
No kernel may reach another device: no remote copies, remote signals or barrier semaphores. Data moves between devices by JAX's collectives and lax.ppermute only.
A program may use at most 256 MiB of HBM per device.

v0:
```python
import jax
import jax.numpy as jnp
from jax import lax
from jax.sharding import PartitionSpec as P

BLOCK = 512
LS = 8
CAP = 2


def squared_gap(first_pts, second_pts):
    summed = jnp.zeros((first_pts.shape[1], second_pts.shape[1]), jnp.float32)
    for component in range(3):
        differ = first_pts[component][:, None] - second_pts[component][None, :]
        summed = summed + differ * differ
    return summed


def wendland(squared, scales):
    radius = jnp.sqrt(squared)[None, :, :] / scales[:, None, None]
    remain = jnp.maximum(1.0 - radius, 0.0)
    return (remain * remain * remain * remain * (4.0 * radius + 1.0)).astype(jnp.bfloat16)


def widen(values):
    return values[None, :, None]


def curvature_of(local_sum):
    return lax.psum(local_sum, ("row", "col"))


def on_device(points, targets, kd_order, lengthscales, noise_level, block_owner, block_pairs):
    col_count = lax.axis_size("col")
    row_count = lax.axis_size("row")
    row_index = lax.axis_index("row")
    col_index = lax.axis_index("col")
    self_index = row_index * col_count + col_index
    block_count = points.shape[1] // BLOCK
    pair_count = block_pairs.shape[1] // (row_count * col_count)
    placed = points[:, kd_order]
    blocks = jnp.transpose(placed.reshape(3, block_count, BLOCK), (1, 0, 2))
    right_side = targets[kd_order].reshape(block_count, 1, BLOCK)
    listed = lax.dynamic_slice_in_dim(block_pairs, self_index * pair_count, pair_count, 1)
    first_slot = block_owner[listed[0]]
    second_slot = block_owner[listed[1]]
    first_local = first_slot % block_count
    partner_col = second_slot // block_count % col_count
    live_mask = (jnp.arange(LS)[None, :] >= listed[2][:, None]).astype(jnp.float32)
    serial = jnp.arange(pair_count)
    earlier = (partner_col[:, None] == partner_col[None, :]) & (serial[None, :] < serial[:, None])
    slot_place = partner_col * CAP + jnp.sum(earlier.astype(jnp.int32), axis=1)
    sources = row_index * col_count + jnp.arange(col_count)
    columns = sources[:, None] * pair_count + serial[None, :]
    their_slot = block_owner[block_pairs[1][columns]]
    wanted = their_slot // block_count == self_index
    wanted_count = wanted.astype(jnp.int32)
    before = jnp.cumsum(wanted_count, axis=1) - wanted_count
    picks = []
    flags = []
    for position in range(CAP):
        chosen = wanted & (before == position)
        picks.append(jnp.sum(jnp.where(chosen, their_slot % block_count, 0), axis=1))
        flags.append(jnp.any(chosen, axis=1))
    send_index = jnp.stack(picks, axis=1).reshape(col_count * CAP)
    send_flag = jnp.stack(flags, axis=1).reshape(col_count * CAP)
    collect = (jnp.arange(block_count)[:, None] == first_local[None, :]).astype(jnp.float32)
    near_points = jnp.take(blocks, first_local, axis=0)
    outgoing = jnp.take(blocks, send_index, axis=0) * send_flag.astype(jnp.float32)[:, None, None]
    incoming = lax.all_to_all(outgoing, "col", split_axis=0, concat_axis=0, tiled=True)
    far_points = jnp.take(incoming, slot_place, axis=0)

    def own_tile(block_pts):
        return wendland(squared_gap(block_pts, block_pts), lengthscales)

    def cross_tile(both_pts):
        return wendland(squared_gap(both_pts[0], both_pts[1]), lengthscales)

    residual = jnp.broadcast_to(right_side, (block_count, LS, BLOCK))
    solution = jnp.zeros((block_count, LS, BLOCK), jnp.float32)
    direction = residual
    norm_now = lax.psum(jnp.sum(residual * residual, axis=(0, 2)), ("row", "col"))
    for iteration in range(2):
        apply_rounded = direction.astype(jnp.bfloat16)
        sending = (
            jnp.take(apply_rounded, send_index, axis=0)
            * send_flag.astype(jnp.bfloat16)[:, None, None]
        )
        fetch_arriving = lax.all_to_all(sending, "col", split_axis=0, concat_axis=0, tiled=True)
        fetch_result = jnp.take(fetch_arriving, slot_place, axis=0)
        near_vec = jnp.take(apply_rounded, first_local, axis=0)

        def own_part(inputs):
            kernel = own_tile(inputs[0])
            return jnp.einsum("lij,lj->li", kernel, inputs[1], preferred_element_type=jnp.float32)

        def cross_part(inputs):
            kernel = cross_tile((inputs[0], inputs[1]))
            forward_one = (
                jnp.einsum("lij,lj->li", kernel, inputs[3], preferred_element_type=jnp.float32)
                * inputs[4][:, None]
            )
            backward_one = (
                jnp.einsum("lij,li->lj", kernel, inputs[2], preferred_element_type=jnp.float32)
                * inputs[4][:, None]
            )
            return (forward_one, backward_one)

        diagonal = lax.map(own_part, (blocks, apply_rounded))
        forward, apply_backward = lax.map(
            cross_part, (near_points, far_points, near_vec, fetch_result, live_mask)
        )
        spread = (jnp.arange(col_count * CAP)[:, None] == slot_place[None, :]).astype(jnp.float32)
        buffer = jnp.einsum("sp,plk->slk", spread, apply_backward, precision=lax.Precision.HIGHEST)
        arriving = lax.all_to_all(buffer, "col", split_axis=0, concat_axis=0, tiled=True)
        settle = (
            (jnp.arange(block_count)[:, None] == send_index[None, :]) & send_flag[None, :]
        ).astype(jnp.float32)
        result = jnp.einsum("bs,slk->blk", settle, arriving, precision=lax.Precision.HIGHEST)
        summed = (
            diagonal
            + jnp.einsum("bp,plk->blk", collect, forward, precision=lax.Precision.HIGHEST)
            + result
        )
        mapped = widen(noise_level) * direction + summed / (2.0 * BLOCK)
        local_curve = jnp.sum(direction * mapped, axis=(0, 2))
        if iteration == 0:
            curvature_sum = curvature_of(local_curve)
        else:
            curvature_sum = curvature_of(local_curve)
        step_size = norm_now / curvature_sum
        solution = solution + widen(step_size) * direction
        residual = residual - widen(step_size) * mapped
        if iteration == 0:
            norm_next = lax.psum(jnp.sum(residual * residual, axis=(0, 2)), ("row", "col"))
            direction = residual + widen(norm_next / norm_now) * direction
            norm_now = norm_next
    solution_out = jnp.transpose(solution, (1, 0, 2)).reshape(LS, block_count * BLOCK)
    residual_out = jnp.transpose(residual, (1, 0, 2)).reshape(LS, block_count * BLOCK)
    return (solution_out, residual_out)


def solution(mesh):
    placed = (P(None, ("row", "col")), P(("row", "col")), P(("row", "col")), P(), P(), P(), P())
    return jax.shard_map(
        on_device,
        mesh=mesh,
        in_specs=placed,
        out_specs=(P(None, ("row", "col")), P(None, ("row", "col"))),
        check_vma=False,
    )
```

profile of v0, /device:TPU:1, one launch (start us, length us, event | category | flops | bytes accessed | tf_op | source)
XLA Modules:
  0.0 536.8 jit_solution(586247790757583593)
XLA Ops:
  7.4 5.5 %gather_fusion.1 = f32[2048,3]{1,0:T(8,128)S(1)} fusion(f32[3,2048]{0,1:T(8,128)S(1)} %copy.52, s32[2048]{0:T(1024)S(1)} %fusion.57), kind=kCustom, calls=%fused_computation.7 | custom fusion | bytes 57344 | tf_op jit(solution)/shard_map/gather | solution.py:41
  14.8 8.6 %all-to-all-start = ((f32[32,3,512]{2,1,0:T(4,128)}), f32[32,3,512]{2,1,0:T(4,128)S(1)}, u32[]{:S(2)}, u32[]{:S(2)}) async-start(f32[32,3,512]{2,1,0:T(4,128)} %select_multiply_fusion.2), calls=%async_computation | async-start | bytes 524288 | tf_op jit(solution)/shard_map/all_to_all | solution.py:70
  25.9 11.8 %gather_fusion = f32[2048]{0:T(1024)S(1)} fusion(f32[2048]{0:T(1024)S(1)} %copy-done, s32[2048]{0:T(1024)S(1)} %fusion.57), kind=kCustom, calls=%fused_computation.6 | custom fusion | bytes 24576 | tf_op jit(solution)/shard_map/gather | solution.py:43
  41.3 6.7 %all-to-all-start.1 = ((bf16[32,8,512]{2,1,0:T(8,128)(2,1)}), bf16[32,8,512]{2,1,0:T(8,128)(2,1)S(1)}, u32[]{:S(2)}, u32[]{:S(2)}) async-start(bf16[32,8,512]{2,1,0:T(8,128)(2,1)} %select_multiply_fusion.1), calls=%async_computation.1 | async-start | bytes 524288 | tf_op jit(solution)/shard_map/all_to_all | solution.py:89
  48.8 6.8 %all-to-all-done.1 = bf16[32,8,512]{2,1,0:T(8,128)(2,1)S(1)} async-done(((bf16[32,8,512]{2,1,0:T(8,128)(2,1)}), bf16[32,8,512]{2,1,0:T(8,128)(2,1)S(1)}, u32[]{:S(2)}, u32[]{:S(2)}) %all-to-all-start.1) | async-done | bytes 262176 | tf_op jit(solution)/shard_map/all_to_all | solution.py:89
  56.3 111.4 %while.45 = (s32[]{:T(128)}, f32[16,8,512]{2,0,1:T(8,128)S(1)}, f32[16,8,512]{2,0,1:T(8,128)S(1)}, f32[16,3,512]{2,1,0:T(4,128)S(1)}, f32[16,3,512]{2,1,0:T(4,12...) while((s32[]{:T(128)}, f32[16,8,512]{2,0,1:T(8,128)S(1)}, ...), condition=%wide.region_11.15_spmd, body=%wide.region_10.14_spmd.sunk | while | flops 52436996 | bytes 3461457 | solution.py:110
  56.9 3.0 fusion.130
  63.9 3.0 fusion.130
  70.9 3.0 fusion.130
  77.8 3.0 fusion.130
  84.8 3.0 fusion.130
  91.7 3.0 fusion.130
  98.7 3.0 fusion.130
  105.7 3.0 fusion.130
  112.6 3.0 fusion.130
  119.6 3.0 fusion.130
  126.6 3.0 fusion.130
  140.5 3.0 fusion.130
  147.5 3.0 fusion.130
  154.4 3.0 fusion.130
  161.4 3.0 fusion.130
  169.3 3.6 all-to-all-start.2
  173.0 15.1 %while.44 = (s32[]{:T(128)}, f32[4,8,512]{2,0,1:T(4,128)S(1)}, f32[4,3,512]{2,1,0:T(4,128)S(1)}, f32[8]{0:T(128)S(1)}, bf16[4,8,512]{2,1,0:T(8,128)(2,1)S(1)}, /*index=5*/s32[]{:T(128)}, s32[]{:T(128)}, s32[]{}, s32[]{}) while((s32[]{:T(128)}, f32[4,8,512]{2,0,1:T(4,128)S(1)}, f32[4,3,512]{2,1,0:T(4,128)S(1)}, f32[8]{0:T(128)S(1)}, ...), condition=%wide.region_3.4_spmd, body=%wide.region_2.3_spmd.sunk | while | flops 27262980 | bytes 2255017 | solution.py:109
  177.4 3.0 fusion.123
  181.1 3.0 fusion.123
  184.9 3.0 fusion.123
  190.3 67.5 %all-reduce = (f32[8]{0:T(128)S(1)}, f32[8]{0:T(128)S(1)}) all-reduce(f32[8]{0:T(128)S(1)} %reduce_sum.68, f32[8]{0:T(128)S(1)} %get-tuple-element.311), channel_id=1, replica_groups=mesh['row'=8,'col'=16] {'row','col'}, use_global_device_ids=true, to_apply=%region_1.2 | all-reduce | flops 16 | bytes 128 | tf_op jit(solution)/shard_map/psum | solution.py:82
  258.0 63.8 %psum.30 = f32[8]{0:T(128)S(1)} all-reduce(f32[8]{0:T(128)S(1)} %multiply_reduce_fusion.1), channel_id=1, replica_groups=mesh['row'=8,'col'=16] {'row','col'}, use_global_device_ids=true, to_apply=%region_15.19 | all-reduce | flops 8 | bytes 64 | tf_op jit(solution)/shard_map/psum | solution.py:135
  324.1 3.7 all-to-all-start.3
  328.6 6.7 %all-to-all-done.3 = bf16[32,8,512]{2,1,0:T(8,128)(2,1)S(1)} async-done(((bf16[32,8,512]{2,1,0:T(8,128)(2,1)}), bf16[32,8,512]{2,1,0:T(8,128)(2,1)S(1)}, u32[]{:S(2)}, u32[]{:S(2)}) %all-to-all-start.3) | async-done | bytes 262176 | tf_op jit(solution)/shard_map/all_to_all | solution.py:89
  336.2 111.4 %while.47 = (s32[]{:T(128)}, f32[16,8,512]{2,0,1:T(8,128)S(1)}, f32[16,8,512]{2,0,1:T(8,128)S(1)}, f32[16,3,512]{2,1,0:T(4,128)S(1)}, f32[16,3,512]{2,1,0:T(4,12...) while((s32[]{:T(128)}, f32[16,8,512]{2,0,1:T(8,128)S(1)}, ...), condition=%wide.region_19.23_spmd, body=%wide.region_18.22_spmd.sunk | while | flops 52436996 | bytes 3461457 | solution.py:110
  343.8 3.0 fusion.141
  350.8 3.0 fusion.141
  364.7 3.0 fusion.141
  378.6 3.0 fusion.141
  385.6 3.0 fusion.141
  392.6 3.0 fusion.141
  399.5 3.0 fusion.141
  413.4 3.0 fusion.141
  427.4 3.0 fusion.141
  434.3 3.0 fusion.141
  441.3 3.0 fusion.141
  449.2 3.6 all-to-all-start.4
  452.9 15.1 %while.46 = (s32[]{:T(128)}, f32[4,8,512]{2,0,1:T(4,128)S(1)}, f32[4,3,512]{2,1,0:T(4,128)S(1)}, f32[8]{0:T(128)S(1)}, bf16[4,8,512]{2,1,0:T(8,128)(2,1)S(1)}, /*index=5*/s32[]{:T(128)}, s32[]{:T(128)}, s32[]{}, s32[]{}) while((s32[]{:T(128)}, f32[4,8,512]{2,0,1:T(4,128)S(1)}, f32[4,3,512]{2,1,0:T(4,128)S(1)}, f32[8]{0:T(128)S(1)}, ...), condition=%wide.region_17.21_spmd, body=%wide.region_16.20_spmd.sunk | while | flops 27262980 | bytes 2255017 | solution.py:109
  453.5 3.0 fusion.134
  457.3 3.0 fusion.134
  464.8 3.0 fusion.134
  469.0 66.4 %psum.31 = f32[8]{0:T(128)S(1)} all-reduce(f32[8]{0:T(128)S(1)} %get-tuple-element.313), channel_id=1, replica_groups=mesh['row'=8,'col'=16] {'row','col'}, use_global_device_ids=true, to_apply=%region_21.25 | all-reduce | flops 8 | bytes 64 | tf_op jit(solution)/shard_map/psum | solution.py:30
  (557 shorter events, 182.3 us)
Async XLA Ops:
  0.6 25.3 %copy-start = (f32[2048]{0:T(1024)S(1)}, f32[2048]{0:T(1024)}, u32[]{:S(2)}) copy-start(f32[2048]{0:T(1024)} %param.22) | copy-start | bytes 24580
  3.3 0.7 copy-start.1
  4.0 3.0 copy-start.11
  4.0 3.0 copy-start.10
  6.7 18.4 %copy-start.12 = (s32[32]{0:T(128)}, s32[32]{0:T(128)S(1)}, u32[]{:S(2)}) copy-start(s32[32]{0:T(128)S(1)} %reshape.869) | copy-start | bytes 388
  7.0 6.2 %copy-start.15 = (pred[32]{0:T(512)(128)(4,1)}, pred[32]{0:T(512)(128)(4,1)S(1)}, u32[]{:S(2)}) copy-start(pred[32]{0:T(512)(128)(4,1)S(1)} %reshape.871) | copy-start | bytes 100
  13.3 27.2 %copy-start.18 = (pred[32]{0:T(512)(128)(4,1)}, pred[32]{0:T(512)(128)(4,1)S(1)}, u32[]{:S(2)}) copy-start(pred[32]{0:T(512)(128)(4,1)S(1)} %get-tuple-element.317) | copy-start | bytes 100
  13.3 27.2 %copy-start.29 = (bf16[32]{0:T(256)(128)(2,1)}, bf16[32]{0:T(256)(128)(2,1)S(1)}, u32[]{:S(2)}) copy-start(bf16[32]{0:T(256)(128)(2,1)S(1)} %get-tuple-element.309) | copy-start | bytes 196
  14.8 26.5 %all-to-all-start = ((f32[32,3,512]{2,1,0:T(4,128)}), f32[32,3,512]{2,1,0:T(4,128)S(1)}, u32[]{:S(2)}, u32[]{:S(2)}) async-start(f32[32,3,512]{2,1,0:T(4,128)} %select_multiply_fusion.2), calls=%async_computation | async-start | bytes 524288 | tf_op jit(solution)/shard_map/all_to_all | solution.py:70
  25.1 142.6 %copy-start.31 = (s32[16]{0:T(128)}, s32[16]{0:T(128)S(1)}, u32[]{:S(2)}) copy-start(s32[16]{0:T(128)S(1)} %get-tuple-element.264) | copy-start | bytes 196
  25.8 13.7 %copy-start.33 = (s32[16]{0:T(128)}, s32[16]{0:T(128)S(1)}, u32[]{:S(2)}) copy-start(s32[16]{0:T(128)S(1)} %get-tuple-element.262) | copy-start | bytes 196
  25.9 12.4 %copy-start.21 = (s32[1024]{0:T(1024)}, s32[1024]{0:T(1024)S(1)}, u32[]{:S(2)}) copy-start(s32[1024]{0:T(1024)S(1)} %pad_clamp_fusion.2) | copy-start | bytes 12292
  37.7 0.6 copy-start.8
  37.7 0.6 copy-start.5
  38.3 1.2 copy-start.20
  39.5 9.1 %copy-start.23 = (pred[16]{0:T(512)(128)(4,1)}, pred[16]{0:T(512)(128)(4,1)S(1)}, u32[]{:S(2)}) copy-start(pred[16]{0:T(512)(128)(4,1)S(1)} %compare_and_fusion.4) | copy-start | bytes 52
  41.3 14.8 %copy-start.25 = (pred[16]{0:T(512)(128)(4,1)}, pred[16]{0:T(512)(128)(4,1)S(1)}, u32[]{:S(2)}) copy-start(pred[16]{0:T(512)(128)(4,1)S(1)} %compare_and_fusion.3) | copy-start | bytes 52
  41.3 15.0 %copy-start.38 = (f32[8]{0:T(128)S(1)}, f32[8]{0:T(128)}, u32[]{:S(2)}) copy-start(f32[8]{0:T(128)} %param.24) | copy-start | bytes 100
  41.3 14.2 %all-to-all-start.1 = ((bf16[32,8,512]{2,1,0:T(8,128)(2,1)}), bf16[32,8,512]{2,1,0:T(8,128)(2,1)S(1)}, u32[]{:S(2)}, u32[]{:S(2)}) async-start(bf16[32,8,512]{2,1,0:T(8,128)(2,1)} %select_multiply_fusion.1), calls=%async_computation.1 | async-start | bytes 524288 | tf_op jit(solution)/shard_map/all_to_all | solution.py:89
  48.0 8.3 %copy-start.22 = (s32[1024]{0:T(1024)}, s32[1024]{0:T(1024)S(1)}, u32[]{:S(2)}) copy-start(s32[1024]{0:T(1024)S(1)} %pad_clamp_fusion.1) | copy-start | bytes 12292
  169.3 19.6 %all-to-all-start.2 = ((f32[32,8,512]{2,1,0:T(8,128)}), f32[32,8,512]{2,1,0:T(8,128)S(1)}, u32[]{:S(2)}, u32[]{:S(2)}) async-start(f32[32,8,512]{2,1,0:T(8,128)} %copy.60), calls=%async_computation.2 | async-start | bytes 1048576 | tf_op jit(solution)/shard_map/all_to_all | solution.py:115
  172.9 15.2 %copy-start.9 = (f32[2048]{0:T(1024)S(1)}, f32[2048]{0:T(1024)}, u32[]{:S(2)}) copy-start(f32[2048]{0:T(1024)} %copy-done.8) | copy-start | bytes 24580
  172.9 15.8 %copy-start.34 = (s32[16]{0:T(128)S(1)}, s32[16]{0:T(128)}, u32[]{:S(2)}) copy-start(s32[16]{0:T(128)} %copy-done.33) | copy-start | bytes 196
  172.9 16.0 %copy-start.6 = (f32[4,512]{1,0:T(4,128)S(1)}, f32[4,512]{1,0:T(4,128)}, u32[]{:S(2)}) copy-start(f32[4,512]{1,0:T(4,128)} %copy-done.5) | copy-start | bytes 24580
  172.9 16.0 %copy-start.13 = (s32[32]{0:T(128)S(1)}, s32[32]{0:T(128)}, u32[]{:S(2)}) copy-start(s32[32]{0:T(128)} %copy-done.12) | copy-start | bytes 388
  172.9 16.0 %copy-start.16 = (pred[32]{0:T(512)(128)(4,1)S(1)}, pred[32]{0:T(512)(128)(4,1)}, u32[]{:S(2)}) copy-start(pred[32]{0:T(512)(128)(4,1)} %copy-done.15) | copy-start | bytes 100
  172.9 16.0 %copy-start.36 = (f32[8]{0:T(128)S(1)}, f32[8]{0:T(128)}, u32[]{:S(2)}) copy-start(f32[8]{0:T(128)} %param.25) | copy-start | bytes 100
  188.1 135.2 %copy-start.19 = (pred[32]{0:T(512)(128)(4,1)S(1)}, pred[32]{0:T(512)(128)(4,1)}, u32[]{:S(2)}) copy-start(pred[32]{0:T(512)(128)(4,1)} %copy-done.18) | copy-start | bytes 100
  188.1 135.2 %copy-start.30 = (bf16[32]{0:T(256)(128)(2,1)S(1)}, bf16[32]{0:T(256)(128)(2,1)}, u32[]{:S(2)}) copy-start(bf16[32]{0:T(256)(128)(2,1)} %copy-done.29) | copy-start | bytes 196
  189.7 138.8 %copy-start.2 = (f32[4,8,512]{2,0,1:T(4,128)}, f32[4,8,512]{2,0,1:T(4,128)S(1)}, u32[]{:S(2)}) copy-start(f32[4,8,512]{2,0,1:T(4,128)S(1)} %get-tuple-element.312) | copy-start | bytes 196612
  257.8 70.7 %copy-start.27 = (f32[8]{0:T(128)}, f32[8]{0:T(128)S(1)}, u32[]{:S(2)}) copy-start(f32[8]{0:T(128)S(1)} %div.112) | copy-start | bytes 100
  258.0 70.5 %copy-start.24 = (pred[16]{0:T(512)(128)(4,1)S(1)}, pred[16]{0:T(512)(128)(4,1)}, u32[]{:S(2)}) copy-start(pred[16]{0:T(512)(128)(4,1)} %copy-done.23) | copy-start | bytes 52
  321.8 6.8 %copy-start.39 = (f32[8]{0:T(128)}, f32[8]{0:T(128)S(1)}, u32[]{:S(2)}) copy-start(f32[8]{0:T(128)S(1)} %psum.30) | copy-start | bytes 100
  323.3 12.8 %copy-start.26 = (pred[16]{0:T(512)(128)(4,1)S(1)}, pred[16]{0:T(512)(128)(4,1)}, u32[]{:S(2)}) copy-start(pred[16]{0:T(512)(128)(4,1)} %copy-done.25) | copy-start | bytes 52
  324.1 11.2 %all-to-all-start.3 = ((bf16[32,8,512]{2,1,0:T(8,128)(2,1)}), bf16[32,8,512]{2,1,0:T(8,128)(2,1)S(1)}, u32[]{:S(2)}, u32[]{:S(2)}) async-start(bf16[32,8,512]{2,1,0:T(8,128)(2,1)} %select_multiply_fusion), calls=%async_computation.3 | async-start | bytes 524288 | tf_op jit(solution)/shard_map/all_to_all | solution.py:89
  336.2 111.4 %copy-start.32 = (s32[16]{0:T(128)S(1)}, s32[16]{0:T(128)}, u32[]{:S(2)}) copy-start(s32[16]{0:T(128)} %copy-done.31) | copy-start | bytes 196
  449.2 19.0 %all-to-all-start.4 = ((f32[32,8,512]{2,1,0:T(8,128)}), f32[32,8,512]{2,1,0:T(8,128)S(1)}, u32[]{:S(2)}, u32[]{:S(2)}) async-start(f32[32,8,512]{2,1,0:T(8,128)} %copy.68), calls=%async_computation.4 | async-start | bytes 1048576 | tf_op jit(solution)/shard_map/all_to_all | solution.py:115
  452.8 15.2 %copy-start.35 = (s32[16]{0:T(128)S(1)}, s32[16]{0:T(128)}, u32[]{:S(2)}) copy-start(s32[16]{0:T(128)} %copy-done.33) | copy-start | bytes 196
  452.8 15.4 %copy-start.4 = (f32[4,8,512]{2,0,1:T(4,128)S(1)}, f32[4,8,512]{2,0,1:T(4,128)}, u32[]{:S(2)}) copy-start(f32[4,8,512]{2,0,1:T(4,128)} %get-tuple-element.260) | copy-start | bytes 196612
  452.8 15.4 %copy-start.14 = (s32[32]{0:T(128)S(1)}, s32[32]{0:T(128)}, u32[]{:S(2)}) copy-start(s32[32]{0:T(128)} %copy-done.12) | copy-start | bytes 388
  452.8 15.4 %copy-start.17 = (pred[32]{0:T(512)(128)(4,1)S(1)}, pred[32]{0:T(512)(128)(4,1)}, u32[]{:S(2)}) copy-start(pred[32]{0:T(512)(128)(4,1)} %copy-done.15) | copy-start | bytes 100
  452.9 15.4 %copy-start.37 = (f32[8]{0:T(128)S(1)}, f32[8]{0:T(128)}, u32[]{:S(2)}) copy-start(f32[8]{0:T(128)} %param.25) | copy-start | bytes 100
  468.0 67.4 %copy-start.40 = (f32[8]{0:T(128)S(1)}, f32[8]{0:T(128)}, u32[]{:S(2)}) copy-start(f32[8]{0:T(128)} %copy-done.39) | copy-start | bytes 100
  468.0 67.4 %copy-start.3 = (f32[4,8,512]{2,0,1:T(4,128)S(1)}, f32[4,8,512]{2,0,1:T(4,128)}, u32[]{:S(2)}) copy-start(f32[4,8,512]{2,0,1:T(4,128)} %copy-done.2) | copy-start | bytes 196612
  468.0 67.4 %copy-start.7 = (f32[4,512]{1,0:T(4,128)S(1)}, f32[4,512]{1,0:T(4,128)}, u32[]{:S(2)}) copy-start(f32[4,512]{1,0:T(4,128)} %copy-done.5) | copy-start | bytes 24580
  468.0 67.4 %copy-start.28 = (f32[8]{0:T(128)S(1)}, f32[8]{0:T(128)}, u32[]{:S(2)}) copy-start(f32[8]{0:T(128)} %copy-done.27) | copy-start | bytes 100
where the time goes:
time: 538 us; the launch traced here: 537 us
  matrix products  217 us (40%)
  blocking collectives  198 us (37%)
  local copies, waits for them, and re-layouts  47 us (9%)
  other arithmetic  31.2 us (6%)
  starting transfers between devices  26.1 us (5%)
  waiting for transfers between devices  13.5 us (3%)
    psum x2, blocking collectives, on_device(): lax.psum(jnp.sum(residual * residual, axis=(0, 2)), ('row', 'col'))  131 us
    dot_general x32, matrix products, cross_part(): jnp.einsum('lij,lj->li', kernel, inputs[3], preferred_element_type=jnp.fl...  95.7 us
    dot_general x32, matrix products, cross_part(): jnp.einsum('lij,li->lj', kernel, inputs[2], preferred_element_type=jnp.fl...  94.6 us
    psum x1, blocking collectives, curvature_of(): return lax.psum(local_sum, ('row', 'col'))  66.4 us
    dot_general x8, matrix products, own_part(): jnp.einsum('lij,lj->li', kernel, inputs[1], preferred_element_type=jnp.fl...  23.9 us
    sqrt x40, other arithmetic, wendland(): radius = jnp.sqrt(squared)[None, :, :] / scales[:, None, None]  23.1 us
    all_to_all x2, waiting for transfers between devices, on_device(): lax.all_to_all(sending, 'col', split_axis=0, concat_axis=0, tiled=True)  13.5 us
    gather x1, local copies, waits for them, and re-layouts, on_device(): right_side = targets[kd_order].reshape(block_count, 1, BLOCK)  11.8 us
  transfers between devices with their start and end apart: 5, of which 2 were waited for; matrix products, arithmetic and copies ran while one was open for 9% of the time, Pallas kernels for 0%

commit v1 on v0

v1 whole, which is shorter than its diff:
```python
import jax
import jax.numpy as jnp
from jax import lax
from jax.experimental import pallas as pl
from jax.experimental.pallas import tpu as pltpu
from jax.sharding import PartitionSpec as P

BLOCK = 512
LS = 8
CAP = 2
LANES = 128
CHUNK = 16
F32 = jnp.float32
BF16 = jnp.bfloat16
VMEM = pltpu.VMEM
SMEM = pltpu.SMEM
LIMIT = 56 * 2**20


def vmem_spec():
    return pl.BlockSpec(memory_space=pltpu.VMEM)


def smem_spec():
    return pl.BlockSpec(memory_space=pltpu.SMEM)


def any_spec():
    return pl.BlockSpec(memory_space=pl.ANY)


def params():
    return pltpu.CompilerParams(vmem_limit_bytes=LIMIT)


def prepare_kernel(
    cols, count, pairs_dev, me_ref, pts_ref, tgt_ref, order_ref, owner_ref, pairs_ref,
    loc_ref, send_ref, meta_ref, asked_ref, used_ref,
):
    me = me_ref[0]
    row = me // cols

    def clear(i, _):
        asked_ref[i] = -1
        return 0

    lax.fori_loop(0, cols * CAP + 1, clear, 0)
    for c in range(cols):
        used_ref[c] = 0

    def own_pair(p, _):
        column = me * pairs_dev + p
        first = owner_ref[pairs_ref[0, column]]
        second = owner_ref[pairs_ref[1, column]]
        partner = (second // count) % cols
        seen = used_ref[partner]
        used_ref[partner] = seen + 1
        meta_ref[0, p] = first % count
        meta_ref[1, p] = partner * CAP + seen
        meta_ref[2, p] = pairs_ref[2, column]
        return 0

    lax.fori_loop(0, pairs_dev, own_pair, 0)

    def scan_source(c, _):
        base = (row * cols + c) * pairs_dev
        seen = jnp.int32(0)
        for j in range(pairs_dev):
            second = owner_ref[pairs_ref[1, base + j]]
            match = (second // count) == me
            place = jnp.where(match, c * CAP + seen, cols * CAP)
            asked_ref[place] = second % count
            seen = seen + match.astype(jnp.int32)
        return 0

    lax.fori_loop(0, cols, scan_source, 0)

    total = pts_ref.shape[1]
    pieces = total // LANES
    source = jnp.concatenate([pts_ref[...], tgt_ref[...], jnp.zeros((4, total), F32)], axis=0)
    for o in range(pieces):
        index = jnp.broadcast_to(order_ref[:, o * LANES:(o + 1) * LANES], (8, LANES))
        high = index // LANES
        low = index % LANES
        got = jnp.zeros((8, LANES), F32)
        for c in range(pieces):
            part = jnp.take_along_axis(
                source[:, c * LANES:(c + 1) * LANES], low, axis=1, mode="promise_in_bounds"
            )
            got = jnp.where(high == c, part, got)
        per = BLOCK // LANES
        loc_ref[o // per, :, (o % per) * LANES:(o % per + 1) * LANES] = got

    for q in range(cols * CAP):
        meta_ref[3, q] = asked_ref[q]
        where = jnp.maximum(asked_ref[q], 0)
        half = (q % CAP) * 4
        send_ref[q // CAP, half:half + 4, :] = loc_ref[where, 0:4, :]


def spread_columns(rows):
    turned = jnp.transpose(rows)
    return [jnp.broadcast_to(turned[:, k:k + 1], (BLOCK, LANES)) for k in range(8)]


def rounded(values):
    return values.astype(BF16).astype(F32)


def per_system(ref):
    which = lax.broadcasted_iota(jnp.int32, (LS, LANES), 0)
    out = jnp.zeros((LS, LANES), F32)
    for l in range(LS):
        out = jnp.where(which == l, ref[l], out)
    return out


def wide(column, width):
    return jnp.concatenate([column] * (width // LANES), axis=1)


def lane_fold(values):
    total = values[:, 0:LANES]
    for c in range(1, values.shape[1] // LANES):
        total = total + values[:, c * LANES:(c + 1) * LANES]
    return total


def distance(col_refs, row_vals, width):
    summed = None
    for k in range(3):
        differ = wide(col_refs[k], width) - row_vals[k]
        square = differ * differ
        summed = square if summed is None else summed + square
    summed = jnp.maximum(summed, 1e-30)
    return summed * lax.rsqrt(summed)


CREST = 4.0**0.2


def kernel_value(dist, slope):
    remain = jnp.maximum(CREST - dist * slope, 0.0)
    squared = remain * remain
    return ((squared * squared) * (5.0 / CREST**4 - remain)).astype(BF16)


def sub_fold(values):
    return values[0:8, :] + values[8:16, :]


def fold_forward(forward_ref, s):
    lane = lax.broadcasted_iota(jnp.int32, (LANES, LANES), 1)
    out = []
    for part in range(BLOCK // LANES):
        held = jnp.zeros((LANES, LANES), F32)
        for l in range(LS):
            block = forward_ref[s, l, part * LANES:(part + 1) * LANES, :]
            held = jnp.where(lane == l, jnp.sum(block, axis=1, keepdims=True), held)
        out.append(jnp.transpose(held)[0:LS, :])
    return jnp.concatenate(out, axis=1)


def own_kernel(common, ls_ref, loc_ref, vec_ref, out_ref, coord_ref, col_ref, dist_ref, forward_ref):
    count = loc_ref.shape[0]
    parts = BLOCK // LANES
    per = LANES // CHUNK

    def block(s, _):
        columns = spread_columns(loc_ref[s])
        for k in range(4):
            coord_ref[k] = columns[k]
        if common:
            coord_ref[3] = rounded(columns[3])
        else:
            columns = spread_columns(vec_ref[s])
            for l in range(LS):
                col_ref[l] = columns[l]
        for part in range(parts):
            low = part * LANES
            width = BLOCK - low
            rows = [loc_ref[s, k:k + 1, low:] for k in range(3)]

            def measure(c, _):
                at = pl.ds(pl.multiple_of(low + c * CHUNK, CHUNK), CHUNK)
                dist_ref[at, low:] = distance([coord_ref[k, at, :] for k in range(3)], rows, width)
                return 0

            lax.fori_loop(0, per, measure, 0, unroll=2)

        def two(t, _):
            back = [jnp.zeros((8, BLOCK), F32) for _ in range(2)]
            ids = [2 * t, 2 * t + 1]
            slopes = [ls_ref[l] for l in ids]
            for part in range(parts):
                low = part * LANES
                width = BLOCK - low
                if common:
                    rows = [rounded(loc_ref[s, 3:4, low:])] * 2
                else:
                    rows = [vec_ref[s, pl.ds(l, 1), :][:, low:] for l in ids]

                def step(c, held):
                    at = pl.ds(pl.multiple_of(low + c * CHUNK, CHUNK), CHUNK)
                    dist = dist_ref[at, low:]
                    fresh = []
                    for n in range(2):
                        value = kernel_value(dist, slopes[n]).astype(F32)
                        forward_ref[s, ids[n], at, :] = lane_fold(value * rows[n])
                        if width > LANES:
                            column = coord_ref[3, at, :] if common else col_ref[ids[n], at, :]
                            right = value[:, LANES:] * wide(column, width - LANES)
                            fresh.append(held[n] + sub_fold(right))
                    return tuple(fresh) if fresh else held

                start = max(width - LANES, LANES)
                held = tuple(jnp.zeros((8, start), F32) for _ in range(2))
                held = lax.fori_loop(0, per, step, held, unroll=2)
                if width > LANES:
                    for n in range(2):
                        back[n] = jnp.concatenate(
                            [back[n][:, :low + LANES], back[n][:, low + LANES:] + held[n]], axis=1
                        )
            for n in range(2):
                out_ref[s, pl.ds(ids[n], 1), :] = jnp.sum(back[n], axis=0, keepdims=True)
            return 0

        lax.fori_loop(0, LS // 2, two, 0)
        out_ref[s] = out_ref[s] + fold_forward(forward_ref, s)
        return 0

    lax.fori_loop(0, count, block, 0)


def first_kernel(
    ls_ref, meta_ref, loc_ref, far_ref,
    out_ref, back_ref, tiles_ref,
    coord_ref, dist_ref, forward_ref, stage_ref, sem_ref,
):
    count = loc_ref.shape[0]
    pairs_dev = tiles_ref.shape[0] // LS
    steps = BLOCK // CHUNK
    for s in range(count):
        columns = spread_columns(loc_ref[s])
        for k in range(3):
            coord_ref[s, k] = columns[k]
        coord_ref[s, 3] = rounded(columns[3])
    forward_ref[...] = jnp.zeros(forward_ref.shape, F32)

    def store_copy(slot, number):
        return pltpu.make_async_copy(stage_ref.at[slot], tiles_ref.at[number], sem_ref.at[slot])

    def pair(p, number):
        a = meta_ref[0, p]
        q = meta_ref[1, p]
        reach = meta_ref[2, p]
        both = far_ref[q // CAP]
        mine = jnp.where(q % CAP == 1, both[4:8, :], both[0:4, :])
        rows = [mine[k:k + 1, :] for k in range(3)]
        values = rounded(mine[3:4, :])

        def measure(c, _):
            at = pl.ds(pl.multiple_of(c * CHUNK, CHUNK), CHUNK)
            dist_ref[at, :] = distance([coord_ref[a, k, at, :] for k in range(3)], rows, BLOCK)
            return 0

        lax.fori_loop(0, steps, measure, 0, unroll=2)
        back_ref[q] = jnp.zeros((LS, BLOCK), F32)

        def sweep(ids, number):
            slopes = [ls_ref[l] for l in ids]
            slots = [(number + n) % 4 for n in range(len(ids))]
            for n in range(len(ids)):
                @pl.when(number + n >= 4)
                def _():
                    store_copy(slots[n], number + n).wait()

            def step(c, held):
                at = pl.ds(pl.multiple_of(c * CHUNK, CHUNK), CHUNK)
                dist = dist_ref[at, :]
                column = wide(coord_ref[a, 3, at, :], BLOCK)
                fresh = []
                for n in range(len(ids)):
                    value = kernel_value(dist, slopes[n])
                    stage_ref[slots[n], at, :] = value
                    value = value.astype(F32)
                    forward_ref[a, ids[n], at, :] += lane_fold(value * values)
                    fresh.append(held[n] + sub_fold(value * column))
                return tuple(fresh)

            held = tuple(jnp.zeros((8, BLOCK), F32) for _ in ids)
            held = lax.fori_loop(0, steps, step, held, unroll=2)
            for n in range(len(ids)):
                back_ref[q, pl.ds(ids[n], 1), :] = jnp.sum(held[n], axis=0, keepdims=True)
                store_copy(slots[n], number + n).start()
            return number + len(ids)

        live = LS - reach

        def two(t, number):
            return sweep([LS - 1 - 2 * t, LS - 2 - 2 * t], number)

        number = lax.fori_loop(0, live // 2, two, number)
        return lax.cond(live % 2 == 1, lambda m: sweep([reach], m), lambda m: m, number)

    number = lax.fori_loop(0, pairs_dev, pair, jnp.int32(0))
    for back in range(4):
        store_copy((number - 1 - back) % 4, number - 1 - back).wait()
    for s in range(count):
        out_ref[s] = fold_forward(forward_ref, s)


def combine_kernel(
    meta_ref, loc_ref, own_ref, fwd_ref, got_ref, w_ref, send_ref, dots_ref
):
    count = loc_ref.shape[0]
    slots = got_ref.shape[0]
    w_ref[...] = own_ref[...] + fwd_ref[...]
    for q in range(slots):
        where = meta_ref[3, q]

        @pl.when(where >= 0)
        def _():
            w_ref[where] = w_ref[where] + got_ref[q]

    unit = 1.0 / (2.0 * BLOCK)
    products = [jnp.zeros((LS, BLOCK), F32) for _ in range(3)]
    for s in range(count):
        value = w_ref[s] * unit
        w_ref[s] = value
        target = jnp.broadcast_to(loc_ref[s, 3:4, :], (LS, BLOCK))
        products[0] = products[0] + target * target
        products[1] = products[1] + target * value
        products[2] = products[2] + value * value
    for q in range(slots):
        send_ref[q] = w_ref[jnp.maximum(meta_ref[3, q], 0)]
    lane = lax.broadcasted_iota(jnp.int32, (LS, LANES), 1)
    held = jnp.zeros((LS, LANES), F32)
    for n in range(3):
        held = jnp.where(lane == n, jnp.sum(products[n], axis=1, keepdims=True), held)
    dots_ref[...] = held


def second_kernel(
    meta_ref, loc_ref, w_ref, own_ref, far_pts_ref, far_ref, dots_ref, tiles_ref,
    out_ref, back_ref,
    list_ref, col_ref, forward_ref, wz_ref, yz_ref, stage_ref, sem_ref,
):
    count = w_ref.shape[0]
    pairs_dev = tiles_ref.shape[0] // LS
    steps = BLOCK // CHUNK
    depth = stage_ref.shape[0]

    def list_pair(p, number):
        reach = meta_ref[2, p]
        live = LS - reach

        def two(t, number):
            list_ref[number] = p * LS + LS - 1 - t
            return number + 1

        return lax.fori_loop(0, live, two, number)

    number = lax.fori_loop(0, pairs_dev, list_pair, jnp.int32(0))

    def load_copy(t):
        slot = t % depth
        return pltpu.make_async_copy(tiles_ref.at[t], stage_ref.at[slot], sem_ref.at[slot])

    for t in range(depth - 1):
        load_copy(jnp.int32(t)).start()

    def clear(p, _):
        q = meta_ref[1, p]
        back_ref[q // CAP, pl.ds(pl.multiple_of((q % CAP) * LS, LS), LS), :] = jnp.zeros((LS, BLOCK), F32)
        return 0

    lax.fori_loop(0, pairs_dev, clear, 0)
    for s in range(count):
        columns = spread_columns(w_ref[s])
        for l in range(LS):
            col_ref[s, l] = columns[l]
    forward_ref[...] = jnp.zeros(forward_ref.shape, F32)
    wz_ref[...] = jnp.zeros(wz_ref.shape, F32)
    yz_ref[...] = jnp.zeros(yz_ref.shape, F32)

    def tile(t, _):
        entry = list_ref[t]
        p = entry // LS
        l = entry % LS
        a = meta_ref[0, p]
        q = meta_ref[1, p]
        slot = t % depth

        @pl.when(t + depth - 1 < number)
        def _():
            load_copy(t + depth - 1).start()

        load_copy(t).wait()
        row = far_ref[q, pl.ds(l, 1), :]

        def step(c, held):
            at = pl.ds(pl.multiple_of(c * CHUNK, CHUNK), CHUNK)
            value = stage_ref[slot, at, :].astype(F32)
            forward_ref[a, l, at, :] += lane_fold(value * row)
            return held + sub_fold(value * wide(col_ref[a, l, at, :], BLOCK))

        held = lax.fori_loop(0, steps, step, jnp.zeros((8, BLOCK), F32), unroll=4)
        result = jnp.sum(held, axis=0, keepdims=True)
        back_ref[q // CAP, pl.ds((q % CAP) * LS + l, 1), :] = result
        both = far_pts_ref[q // CAP]
        target = jnp.where(q % CAP == 1, both[7:8, :], both[3:4, :])
        wz_ref[pl.ds(l, 1), :] += result * row
        yz_ref[pl.ds(l, 1), :] += result * target
        return 0

    lax.fori_loop(0, number, tile, 0)
    wz = wz_ref[...]
    yz = yz_ref[...]
    for s in range(count):
        value = own_ref[s] + fold_forward(forward_ref, s)
        out_ref[s] = value
        wz = wz + value * w_ref[s]
        yz = yz + value * loc_ref[s, 3:4, :]
    unit = 1.0 / (2.0 * BLOCK)
    lane = lax.broadcasted_iota(jnp.int32, (LS, LANES), 1)
    held = jnp.where(lane == 3, jnp.sum(wz, axis=1, keepdims=True) * unit, dots_ref[...])
    held = jnp.where(lane == 4, jnp.sum(yz, axis=1, keepdims=True) * unit, held)
    padded = jnp.concatenate([held, jnp.zeros((LS, BLOCK - LANES), F32)], axis=1)
    for c in range(back_ref.shape[0]):
        back_ref[c, CAP * LS:(CAP + 1) * LS, :] = padded


def gather_kernel(meta_ref, part_ref, got_ref, z_ref, dots_ref):
    z_ref[...] = part_ref[...]
    held = jnp.zeros((LS, LANES), F32)
    for c in range(got_ref.shape[0]):
        held = held + got_ref[c, CAP * LS:(CAP + 1) * LS, 0:LANES]
        for k in range(CAP):
            where = meta_ref[3, c * CAP + k]

            @pl.when(where >= 0)
            def _():
                z_ref[where] = z_ref[where] + got_ref[c, k * LS:(k + 1) * LS, :]

    z_ref[...] = z_ref[...] * (1.0 / (2.0 * BLOCK))
    for c in range(dots_ref.shape[0]):
        dots_ref[c] = held


def finish_kernel(noise_ref, loc_ref, w_ref, z_ref, dots_ref, sol_ref, res_ref):
    dots = dots_ref[0]
    for c in range(1, dots_ref.shape[0]):
        dots = dots + dots_ref[c]
    noise = per_system(noise_ref)[:, 0:1]
    yy, yw, ww, wz, yz = [dots[:, n:n + 1] for n in range(5)]
    curve = noise * yy + yw
    first = yy / curve
    keep = yw / curve
    fresh = first * ((yy * ww - yw * yw) / curve)
    beta = fresh / yy
    gain = keep + beta
    bend = noise * fresh * (1.0 + beta) + gain * gain * yw - gain * first * (ww + yz) + first * first * wz
    second = fresh / bend
    sol_y = first + second * gain
    sol_w = second * first
    res_y = keep - second * noise * gain
    res_w = second * (noise * first - gain) - first
    for s in range(loc_ref.shape[0]):
        target = loc_ref[s, 3:4, :]
        value = w_ref[s]
        sol_ref[:, s * BLOCK:(s + 1) * BLOCK] = sol_y * target - sol_w * value
        res_ref[:, s * BLOCK:(s + 1) * BLOCK] = res_y * target + res_w * value + sol_w * z_ref[s]


def on_device(points, targets, kd_order, lengthscales, noise_level, block_owner, block_pairs):
    cols = lax.axis_size("col")
    rows = lax.axis_size("row")
    me = (lax.axis_index("row") * cols + lax.axis_index("col")).astype(jnp.int32).reshape(1)
    total = points.shape[1]
    count = total // BLOCK
    pairs_dev = block_pairs.shape[1] // (rows * cols)
    slots = cols * CAP
    field = jax.ShapeDtypeStruct((count, LS, BLOCK), F32)

    loc, send, meta = pl.pallas_call(
        lambda *refs: prepare_kernel(cols, count, pairs_dev, *refs),
        out_shape=(
            jax.ShapeDtypeStruct((count, 8, BLOCK), F32),
            jax.ShapeDtypeStruct((cols, CAP * 4, BLOCK), F32),
            jax.ShapeDtypeStruct((4, slots), jnp.int32),
        ),
        in_specs=[smem_spec(), vmem_spec(), vmem_spec(), vmem_spec(), smem_spec(), smem_spec()],
        out_specs=(vmem_spec(), vmem_spec(), smem_spec()),
        scratch_shapes=[SMEM((slots + 1,), jnp.int32), SMEM((cols,), jnp.int32)],
        compiler_params=params(),
        name="prepare",
    )(me, points, targets.reshape(1, total), kd_order.reshape(1, total), block_owner, block_pairs)

    slopes = CREST / lengthscales

    def own(vec, common):
        return pl.pallas_call(
            lambda *refs: own_kernel(common, *refs),
            out_shape=field,
            in_specs=[smem_spec(), vmem_spec(), vmem_spec()],
            out_specs=vmem_spec(),
            scratch_shapes=[
                VMEM((4, BLOCK, LANES), F32),
                VMEM((LS, BLOCK, LANES), F32),
                VMEM((BLOCK, BLOCK), F32),
                VMEM((count, LS, BLOCK, LANES), F32),
            ],
            compiler_params=params(),
            cost_estimate=pl.CostEstimate(flops=2 * 10**9, bytes_accessed=10**6, transcendentals=0),
            name="own_first" if common else "own_second",
        )(slopes, loc, vec)

    far = lax.all_to_all(send, "col", split_axis=0, concat_axis=0, tiled=True)
    own_one = own(loc, True)
    fwd_one, back_one, tiles = pl.pallas_call(
        first_kernel,
        out_shape=(
            field,
            jax.ShapeDtypeStruct((slots, LS, BLOCK), F32),
            jax.ShapeDtypeStruct((pairs_dev * LS, BLOCK, BLOCK), BF16),
        ),
        in_specs=[smem_spec(), smem_spec(), vmem_spec(), vmem_spec()],
        out_specs=(vmem_spec(), vmem_spec(), any_spec()),
        scratch_shapes=[
            VMEM((count, 4, BLOCK, LANES), F32),
            VMEM((BLOCK, BLOCK), F32),
            VMEM((count, LS, BLOCK, LANES), F32),
            VMEM((4, BLOCK, BLOCK), BF16),
            pltpu.SemaphoreType.DMA((4,)),
        ],
        compiler_params=params(),
        cost_estimate=pl.CostEstimate(flops=10**10, bytes_accessed=6 * 10**7, transcendentals=0),
        name="cross_first",
    )(slopes, meta, loc, far)
    got_one = lax.all_to_all(back_one, "col", split_axis=0, concat_axis=0, tiled=True)

    w, send_w, dots_one = pl.pallas_call(
        combine_kernel,
        out_shape=(
            field,
            jax.ShapeDtypeStruct((slots, LS, BLOCK), F32),
            jax.ShapeDtypeStruct((LS, LANES), F32),
        ),
        in_specs=[smem_spec()] + [vmem_spec()] * 4,
        out_specs=(vmem_spec(),) * 3,
        compiler_params=params(),
        name="combine",
    )(meta, loc, own_one, fwd_one, got_one)
    far_w = lax.all_to_all(send_w, "col", split_axis=0, concat_axis=0, tiled=True)
    own_two = own(w, False)
    fwd_two, back_two = pl.pallas_call(
        second_kernel,
        out_shape=(field, jax.ShapeDtypeStruct((cols, (CAP + 1) * LS, BLOCK), F32)),
        in_specs=[smem_spec()] + [vmem_spec()] * 6 + [any_spec()],
        out_specs=(vmem_spec(),) * 2,
        scratch_shapes=[
            SMEM((pairs_dev * LS,), jnp.int32),
            VMEM((count, LS, BLOCK, LANES), F32),
            VMEM((count, LS, BLOCK, LANES), F32),
            VMEM((LS, BLOCK), F32),
            VMEM((LS, BLOCK), F32),
            VMEM((8, BLOCK, BLOCK), BF16),
            pltpu.SemaphoreType.DMA((8,)),
        ],
        compiler_params=params(),
        cost_estimate=pl.CostEstimate(flops=5 * 10**9, bytes_accessed=6 * 10**7, transcendentals=0),
        name="cross_second",
    )(meta, loc, w, own_two, far, far_w, dots_one, tiles)
    got_two = lax.all_to_all(back_two, "col", split_axis=0, concat_axis=0, tiled=True)

    z, dots_two = pl.pallas_call(
        gather_kernel,
        out_shape=(field, jax.ShapeDtypeStruct((rows, LS, LANES), F32)),
        in_specs=[smem_spec()] + [vmem_spec()] * 2,
        out_specs=(vmem_spec(),) * 2,
        compiler_params=params(),
        name="gather",
    )(meta, fwd_two, got_two)
    dots = lax.all_to_all(dots_two, "row", split_axis=0, concat_axis=0, tiled=True)
    return pl.pallas_call(
        finish_kernel,
        out_shape=(jax.ShapeDtypeStruct((LS, total), F32),) * 2,
        in_specs=[smem_spec()] + [vmem_spec()] * 4,
        out_specs=(vmem_spec(),) * 2,
        compiler_params=params(),
        name="finish",
    )(noise_level, loc, w, z, dots)


def solution(mesh):
    placed = (P(None, ("row", "col")), P(("row", "col")), P(("row", "col")), P(), P(), P(), P())
    return jax.shard_map(
        on_device,
        mesh=mesh,
        in_specs=placed,
        out_specs=(P(None, ("row", "col")), P(None, ("row", "col"))),
        check_vma=False,
    )
```

time: 538 us -> 207 us (0.38)
  matrix products: 217 us -> 0 us
  blocking collectives: 198 us -> 40.3 us
  Pallas kernels: 0 us -> 131 us
  local copies, waits for them, and re-layouts: 47 us -> 2.31 us
  other arithmetic: 31.2 us -> 1.25 us
  waiting for transfers between devices: 13.5 us -> 6.29 us
    dot_general x78 -> x0, matrix products: 217 us -> none  [the longest x32 95.7 us: cross_part(): jnp.einsum('lij,lj->li', kernel, inputs[3], preferred_element_type=jnp.fl...]
    psum x3 -> x0, blocking collectives: 198 us -> none  [the longest x2 131 us: on_device(): lax.psum(jnp.sum(residual * residual, axis=(0, 2)), ('row', 'col'))]
    pallas_call x0 -> x8, Pallas kernels: none -> 131 us  [the longest x1 53.1 us: on_device(): pl.pallas_call(first_kernel, out_shape=(field, jax.ShapeDtypeStruct((slot...]
    all_to_all x0 -> x2, blocking collectives: none -> 40.3 us  [the longest x1 20.7 us: on_device(): lax.all_to_all(back_two, 'col', split_axis=0, concat_axis=0, tiled=True)]
    gather x17 -> x0, local copies, waits for them, and re-layouts: 28.1 us -> none  [the longest x1 11.8 us: on_device(): right_side = targets[kd_order].reshape(block_count, 1, BLOCK)]
    sqrt x40 -> x0, other arithmetic: 23.1 us -> none  [wendland(): radius = jnp.sqrt(squared)[None, :, :] / scales[:, None, None]]
    dynamic_update_slice x144 -> x0, local copies, waits for them, and re-layouts: 9.11 us -> none  [the longest x128 8.15 us: on_device(): lax.map(cross_part, (near_points, far_points, near_vec, fetch_result, liv...]
    all_to_all x5 -> x3, waiting for transfers between devices: 13.5 us -> 6.29 us  [the longest x1 6.29 us: on_device(): far = lax.all_to_all(send, 'col', split_axis=0, concat_axis=0, tiled=True)]
  transfers between devices with their start and end apart: 5 -> 3, of which waited for: 2 -> 1; matrix products, arithmetic and copies ran while one was open for 9% -> 1% of each run, Pallas kernels for 0% -> 18%
where the time goes in v1:
time: 207 us; the launch traced here: 206 us
  Pallas kernels  131 us (63%)
  blocking collectives  40.3 us (19%)
  starting transfers between devices  24.5 us (12%)
  waiting for transfers between devices  6.29 us (3%)
  local copies, waits for them, and re-layouts  2.31 us (1%)
    pallas_call x1, Pallas kernels, on_device(): pl.pallas_call(first_kernel, out_shape=(field, jax.ShapeDtypeStruct((slot...  53.1 us
    pallas_call x2, Pallas kernels, own(): pl.pallas_call(lambda *refs: own_kernel(common, *refs), out_shape=field,...  37.5 us
    pallas_call x1, Pallas kernels, on_device(): pl.pallas_call(second_kernel, out_shape=(field, jax.ShapeDtypeStruct((col...  28.2 us
    all_to_all x1, blocking collectives, on_device(): lax.all_to_all(back_two, 'col', split_axis=0, concat_axis=0, tiled=True)  20.7 us
    all_to_all x1, blocking collectives, on_device(): lax.all_to_all(dots_two, 'row', split_axis=0, concat_axis=0, tiled=True)  19.6 us
    all_to_all x1, starting transfers between devices, on_device(): lax.all_to_all(back_one, 'col', split_axis=0, concat_axis=0, tiled=True)  9.22 us
    all_to_all x1, starting transfers between devices, on_device(): far = lax.all_to_all(send, 'col', split_axis=0, concat_axis=0, tiled=True)  8.61 us
    all_to_all x1, starting transfers between devices, on_device(): lax.all_to_all(send_w, 'col', split_axis=0, concat_axis=0, tiled=True)  6.66 us
  transfers between devices with their start and end apart: 3, of which 1 were waited for; matrix products, arithmetic and copies ran while one was open for 1% of the time, Pallas kernels for 18%

profile of v1, /device:TPU:1, one launch (start us, length us, event | category | flops | bytes accessed | tf_op | source)
XLA Modules:
  0.0 206.0 jit_solution(10444133659045502999)
XLA Ops:
  0.6 5.6 %prepare.1 = (f32[4,8,512]{2,1,0:T(8,128)}, f32[16,8,512]{2,1,0:T(8,128)}, s32[4,32]{1,0:T(4,128)}) custom-call(s32[1]{0:T(128)} %bitcast.refs_0_, f32[3,2048]{1,0:T(4,128)} %refs_1_.1, f32[1,2048]{1,0:T(1,128)} %bitcast.3, s32[1,2048]{1,0:T(1,128)} %bitcast.4, s32[512]{0:T(512)} %refs_4_.1, s32[3,2048]{1,0:T(4,128)} %refs_5_.1), custom_call_target="tpu_custom_call" | custom-call | tf_op jit(solution)/shard_map/prepare/pallas_call | solution.py:486
  6.2 8.6 %all-to-all-start = ((f32[16,8,512]{2,1,0:T(8,128)}), f32[16,8,512]{2,1,0:T(8,128)S(1)}, u32[]{:S(2)}, u32[]{:S(2)}) async-start(f32[16,8,512]{2,1,0:T(8,128)} %get-tuple-element.17), calls=%async_computation | async-start | bytes 524288 | tf_op jit(solution)/shard_map/all_to_all | solution.py:519
  14.8 1.3 broadcast_divide_fusion.refs_0_.ls_ref
  16.1 6.3 %all-to-all-done.far_ref.far_pts_ref = f32[16,8,512]{2,1,0:T(8,128)S(1)} async-done(((f32[16,8,512]{2,1,0:T(8,128)}), f32[16,8,512]{2,1,0:T(8,128)S(1)}, u32[]{:S(2)}, u32[]{:S(2)}) %all-to-all-start) | async-done | bytes 262176 | tf_op jit(solution)/shard_map/all_to_all | solution.py:519
  22.4 0.0 copy-start.2
  22.4 0.7 copy-done.2
  23.1 53.1 %cross_first.1 = (f32[4,8,512]{2,1,0:T(8,128)}, f32[32,8,512]{2,1,0:T(8,128)}, bf16[128,512,512]{2,1,0:T(8,128)(2,1)}) custom-call(f32[8]{0:T(128)} %broadcast_divide_fusion.refs_0_.ls_ref, s32[4,32]{1,0:T(4,128)} %get-tuple-element.16.meta_ref, f32[4,8,512]{2,1,0:T(8,128)} %get-tuple-element.15.refs_1_.refs_2_.loc_ref, f32[16,8,512]{2,1,0:T(8,128)} %copy-done.2), custom_call_target="tpu_custom_call" | custom-call | flops 10000000000 | bytes 60000000 | tf_op jit(solution)/shard_map/cross_first/pallas_call | solution.py:521
  76.3 9.2 %all-to-all-start.1 = ((f32[32,8,512]{2,1,0:T(8,128)}), f32[32,8,512]{2,1,0:T(8,128)S(1)}, u32[]{:S(2)}, u32[]{:S(2)}) async-start(f32[32,8,512]{2,1,0:T(8,128)} %get-tuple-element.19), calls=%async_computation.1 | async-start | bytes 1048576 | tf_op jit(solution)/shard_map/all_to_all | solution.py:541
  85.5 17.5 %own_first.1.own_ref = f32[4,8,512]{2,1,0:T(8,128)} custom-call(f32[8]{0:T(128)} %broadcast_divide_fusion.refs_0_.ls_ref, f32[4,8,512]{2,1,0:T(8,128)} %get-tuple-element.15.refs_1_.refs_2_.loc_ref, f32[4,8,512]{2,1,0:T(8,128)} %get-tuple-element.15.refs_1_.refs_2_.loc_ref), custom_call_target="tpu_custom_call" | custom-call | flops 2000000000 | bytes 1000000 | tf_op jit(solution)/shard_map/own_first/pallas_call | solution.py:503
  103.0 0.0 all-to-all-done.1.got_ref
  103.0 0.0 copy-start.1
  103.0 0.8 copy-done.1
  103.8 2.3 %combine.1 = (f32[4,8,512]{2,1,0:T(8,128)}, f32[32,8,512]{2,1,0:T(8,128)}, f32[8,128]{1,0:T(8,128)}) custom-call(s32[4,32]{1,0:T(4,128)} %get-tuple-element.16.meta_ref, f32[4,8,512]{2,1,0:T(8,128)} %get-tuple-element.15.refs_1_.refs_2_.loc_ref, f32[4,8,512]{2,1,0:T(8,128)} %own_first.1.own_ref, f32[4,8,512]{2,1,0:T(8,128)} %get-tuple-element.18.fwd_ref, ...), custom_call_target="tpu_custom_call" | custom-call | tf_op jit(solution)/shard_map/combine/pallas_call | solution.py:543
  106.1 6.7 %all-to-all-start.2 = ((f32[32,8,512]{2,1,0:T(8,128)}), f32[32,8,512]{2,1,0:T(8,128)S(1)}, u32[]{:S(2)}, u32[]{:S(2)}) async-start(f32[32,8,512]{2,1,0:T(8,128)} %get-tuple-element.21), calls=%async_computation.2 | async-start | bytes 1048576 | tf_op jit(solution)/shard_map/all_to_all | solution.py:555
  112.7 20.0 %own_second.1.own_ref = f32[4,8,512]{2,1,0:T(8,128)} custom-call(f32[8]{0:T(128)} %broadcast_divide_fusion.refs_0_.ls_ref, f32[4,8,512]{2,1,0:T(8,128)} %get-tuple-element.15.refs_1_.refs_2_.loc_ref, f32[4,8,512]{2,1,0:T(8,128)} %get-tuple-element.20.refs_2_.w_ref), custom_call_target="tpu_custom_call" | custom-call | flops 2000000000 | bytes 1000000 | tf_op jit(solution)/shard_map/own_second/pallas_call | solution.py:503
  132.7 0.0 all-to-all-done.2.far_ref
  132.7 0.0 copy-start
  132.7 0.8 copy-done
  133.5 28.2 %cross_second.1 = (f32[4,8,512]{2,1,0:T(8,128)}, f32[16,24,512]{2,1,0:T(8,128)}) custom-call(s32[4,32]{1,0:T(4,128)} %get-tuple-element.16.meta_ref, f32[4,8,512]{2,1,0:T(8,128)} %get-tuple-element.15.refs_1_.refs_2_.loc_ref, f32[4,8,512]{2,1,0:T(8,128)} %get-tuple-element.20.refs_2_.w_ref, f32[4,8,512]{2,1,0:T(8,128)} %own_second.1.own_ref, ...), custom_call_target="tpu_custom_call" | custom-call | flops 5000000000 | bytes 60000000 | tf_op jit(solution)/shard_map/cross_second/pallas_call | solution.py:557
  161.7 20.7 %all_to_all.25.got_ref = f32[16,24,512]{2,1,0:T(8,128)} all-to-all(f32[16,24,512]{2,1,0:T(8,128)} %get-tuple-element.25), channel_id=1, replica_groups=mesh['row'=8,'col'=16] {'col'}, dimensions={0} | all-to-all | bytes 1572864 | tf_op jit(solution)/shard_map/all_to_all | solution.py:575
  182.4 2.1 %gather.1 = (f32[4,8,512]{2,1,0:T(8,128)}, f32[8,8,128]{2,1,0:T(8,128)}) custom-call(s32[4,32]{1,0:T(4,128)} %get-tuple-element.16.meta_ref, f32[4,8,512]{2,1,0:T(8,128)} %get-tuple-element.24.part_ref, f32[16,24,512]{2,1,0:T(8,128)} %all_to_all.25.got_ref), custom_call_target="tpu_custom_call" | custom-call | tf_op jit(solution)/shard_map/gather/pallas_call | solution.py:577
  184.5 19.6 %all_to_all.26.dots_ref = f32[8,8,128]{2,1,0:T(8,128)} all-to-all(f32[8,8,128]{2,1,0:T(8,128)} %get-tuple-element.27), channel_id=1, replica_groups=mesh['row'=8,'col'=16] {'row'}, dimensions={0} | all-to-all | bytes 65536 | tf_op jit(solution)/shard_map/all_to_all | solution.py:585
  204.1 1.9 finish.1
Async XLA Ops:
  6.2 16.2 %all-to-all-start = ((f32[16,8,512]{2,1,0:T(8,128)}), f32[16,8,512]{2,1,0:T(8,128)S(1)}, u32[]{:S(2)}, u32[]{:S(2)}) async-start(f32[16,8,512]{2,1,0:T(8,128)} %get-tuple-element.17), calls=%async_computation | async-start | bytes 524288 | tf_op jit(solution)/shard_map/all_to_all | solution.py:519
  22.4 0.7 copy-start.2
  76.3 26.7 %all-to-all-start.1 = ((f32[32,8,512]{2,1,0:T(8,128)}), f32[32,8,512]{2,1,0:T(8,128)S(1)}, u32[]{:S(2)}, u32[]{:S(2)}) async-start(f32[32,8,512]{2,1,0:T(8,128)} %get-tuple-element.19), calls=%async_computation.1 | async-start | bytes 1048576 | tf_op jit(solution)/shard_map/all_to_all | solution.py:541
  103.0 0.8 copy-start.1
  106.1 26.6 %all-to-all-start.2 = ((f32[32,8,512]{2,1,0:T(8,128)}), f32[32,8,512]{2,1,0:T(8,128)S(1)}, u32[]{:S(2)}, u32[]{:S(2)}) async-start(f32[32,8,512]{2,1,0:T(8,128)} %get-tuple-element.21), calls=%async_computation.2 | async-start | bytes 1048576 | tf_op jit(solution)/shard_map/all_to_all | solution.py:555
  132.7 0.8 copy-start

commit v2 on v1

--- a/solution.py
+++ b/solution.py
@@ -10,6 +10,7 @@
 CAP = 2
 LANES = 128
 CHUNK = 16
+DOTS = 5
 F32 = jnp.float32
 BF16 = jnp.bfloat16
 VMEM = pltpu.VMEM
@@ -33,69 +34,119 @@
     return pltpu.CompilerParams(vmem_limit_bytes=LIMIT)
 
 
-def prepare_kernel(
-    cols, count, pairs_dev, me_ref, pts_ref, tgt_ref, order_ref, owner_ref, pairs_ref,
-    loc_ref, send_ref, meta_ref, asked_ref, used_ref,
-):
-    me = me_ref[0]
-    row = me // cols
-
-    def clear(i, _):
-        asked_ref[i] = -1
-        return 0
-
-    lax.fori_loop(0, cols * CAP + 1, clear, 0)
-    for c in range(cols):
-        used_ref[c] = 0
-
-    def own_pair(p, _):
-        column = me * pairs_dev + p
-        first = owner_ref[pairs_ref[0, column]]
-        second = owner_ref[pairs_ref[1, column]]
-        partner = (second // count) % cols
-        seen = used_ref[partner]
-        used_ref[partner] = seen + 1
-        meta_ref[0, p] = first % count
-        meta_ref[1, p] = partner * CAP + seen
-        meta_ref[2, p] = pairs_ref[2, column]
-        return 0
-
-    lax.fori_loop(0, pairs_dev, own_pair, 0)
-
-    def scan_source(c, _):
-        base = (row * cols + c) * pairs_dev
-        seen = jnp.int32(0)
-        for j in range(pairs_dev):
-            second = owner_ref[pairs_ref[1, base + j]]
-            match = (second // count) == me
-            place = jnp.where(match, c * CAP + seen, cols * CAP)
-            asked_ref[place] = second % count
-            seen = seen + match.astype(jnp.int32)
-        return 0
-
-    lax.fori_loop(0, cols, scan_source, 0)
-
+def over(value, size):
+    return value >> (size.bit_length() - 1) if size & (size - 1) == 0 else value // size
+
+
+def rest(value, size):
+    return value & (size - 1) if size & (size - 1) == 0 else value % size
+
+
+def order_kernel(pts_ref, tgt_ref, order_ref, loc_ref, send_ref):
     total = pts_ref.shape[1]
     pieces = total // LANES
+    per = BLOCK // LANES
     source = jnp.concatenate([pts_ref[...], tgt_ref[...], jnp.zeros((4, total), F32)], axis=0)
     for o in range(pieces):
         index = jnp.broadcast_to(order_ref[:, o * LANES:(o + 1) * LANES], (8, LANES))
-        high = index // LANES
-        low = index % LANES
+        high = over(index, LANES)
+        low = rest(index, LANES)
         got = jnp.zeros((8, LANES), F32)
         for c in range(pieces):
             part = jnp.take_along_axis(
                 source[:, c * LANES:(c + 1) * LANES], low, axis=1, mode="promise_in_bounds"
             )
             got = jnp.where(high == c, part, got)
-        per = BLOCK // LANES
         loc_ref[o // per, :, (o % per) * LANES:(o % per + 1) * LANES] = got
-
+    halves = []
+    for h in range(loc_ref.shape[0] // 2):
+        halves.append(jnp.concatenate([loc_ref[2 * h, 0:4, :], loc_ref[2 * h + 1, 0:4, :]], axis=0))
+    for c in range(send_ref.shape[0] // len(halves)):
+        for h in range(len(halves)):
+            send_ref[c * len(halves) + h] = halves[h]
+
+
+SPARE = 63
+
+
+def plan_kernel(cols, count, pairs_dev, me_ref, owner_ref, pairs_ref, meta_ref, near_ref, far_ref, peer_ref, reach_ref, turn_ref, load_ref, have_ref, used_ref):
+    row = over(me_ref[0], cols)
+    mine = rest(me_ref[0], cols)
+    start = row * (cols * pairs_dev)
+
+    def clear(i, _):
+        for c in range(cols):
+            have_ref[i * cols + c] = 0
+            used_ref[i * cols + c] = 0
+        return 0
+
+    lax.fori_loop(0, cols, clear, 0)
     for q in range(cols * CAP):
-        meta_ref[3, q] = asked_ref[q]
-        where = jnp.maximum(asked_ref[q], 0)
-        half = (q % CAP) * 4
-        send_ref[q // CAP, half:half + 4, :] = loc_ref[where, 0:4, :]
+        meta_ref[4, q] = -1
+
+    def cost_of(reach):
+        return 4 * (LS - reach) + 3
+
+    def read(d, _):
+        total = jnp.int32(0)
+        for j in range(pairs_dev):
+            p = d * pairs_dev + j
+            first = owner_ref[pairs_ref[0, start + p]]
+            second = owner_ref[pairs_ref[1, start + p]]
+            reach = pairs_ref[2, start + p]
+            e = rest(over(second, count), cols)
+            near_ref[p] = rest(first, count)
+            far_ref[p] = rest(second, count)
+            peer_ref[p] = e
+            reach_ref[p] = reach
+            total = total + cost_of(reach)
+            have_ref[d * cols + e] = have_ref[d * cols + e] + 1
+        load_ref[d] = total
+        return 0
+
+    lax.fori_loop(0, cols, read, 0)
+
+    def weigh(j, _):
+        for d in range(cols):
+            p = d * pairs_dev + j
+            e = peer_ref[p]
+            cost = cost_of(reach_ref[p])
+            here = load_ref[d]
+            there = load_ref[e]
+            back = have_ref[e * cols + d]
+            turn = jnp.logical_and(here - there > cost, back < CAP).astype(jnp.int32)
+            load_ref[d] = here - turn * cost
+            load_ref[e] = there + turn * cost
+            have_ref[e * cols + d] = back + turn
+            turn_ref[p] = turn
+        return 0
+
+    lax.fori_loop(0, pairs_dev, weigh, 0)
+
+    def lay(d, number):
+        for j in range(pairs_dev):
+            p = d * pairs_dev + j
+            turn = turn_ref[p] == 1
+            e = peer_ref[p]
+            x = jnp.where(turn, e, d)
+            y = jnp.where(turn, d, e)
+            near = near_ref[p]
+            far = far_ref[p]
+            block_x = jnp.where(turn, far, near)
+            block_y = jnp.where(turn, near, far)
+            seen = used_ref[x * cols + y]
+            used_ref[x * cols + y] = seen + 1
+            ours = x == mine
+            at = jnp.where(ours, number, SPARE)
+            meta_ref[0, at] = block_x
+            meta_ref[1, at] = y * CAP + seen
+            meta_ref[2, at] = reach_ref[p]
+            meta_ref[3, at] = y * count + block_y
+            meta_ref[4, jnp.where(y == mine, x * CAP + seen, SPARE)] = block_y
+            number = number + ours.astype(jnp.int32)
+        return number
+
+    meta_ref[5, 0] = lax.fori_loop(0, cols, lay, jnp.int32(0))
 
 
 def spread_columns(rows):
@@ -159,6 +210,11 @@
             held = jnp.where(lane == l, jnp.sum(block, axis=1, keepdims=True), held)
         out.append(jnp.transpose(held)[0:LS, :])
     return jnp.concatenate(out, axis=1)
+
+
+def partner_rows(far_ref, which):
+    both = far_ref[over(which, 2)]
+    return jnp.where(rest(which, 2) == 1, both[4:8, :], both[0:4, :])
 
 
 def own_kernel(common, ls_ref, loc_ref, vec_ref, out_ref, coord_ref, col_ref, dist_ref, forward_ref):
@@ -186,7 +242,7 @@
                 dist_ref[at, low:] = distance([coord_ref[k, at, :] for k in range(3)], rows, width)
                 return 0
 
-            lax.fori_loop(0, per, measure, 0, unroll=2)
+            lax.fori_loop(0, per, measure, 0, unroll=8)
 
         def two(t, _):
             back = [jnp.zeros((8, BLOCK), F32) for _ in range(2)]
@@ -215,7 +271,7 @@
 
                 start = max(width - LANES, LANES)
                 held = tuple(jnp.zeros((8, start), F32) for _ in range(2))
-                held = lax.fori_loop(0, per, step, held, unroll=2)
+                held = lax.fori_loop(0, per, step, held, unroll=8)
                 if width > LANES:
                     for n in range(2):
                         back[n] = jnp.concatenate(
@@ -238,7 +294,7 @@
     coord_ref, dist_ref, forward_ref, stage_ref, sem_ref,
 ):
     count = loc_ref.shape[0]
-    pairs_dev = tiles_ref.shape[0] // LS
+    pair_count = meta_ref[5, 0]
     steps = BLOCK // CHUNK
     for s in range(count):
         columns = spread_columns(loc_ref[s])
@@ -254,8 +310,7 @@
         a = meta_ref[0, p]
         q = meta_ref[1, p]
         reach = meta_ref[2, p]
-        both = far_ref[q // CAP]
-        mine = jnp.where(q % CAP == 1, both[4:8, :], both[0:4, :])
+        mine = partner_rows(far_ref, meta_ref[3, p])
         rows = [mine[k:k + 1, :] for k in range(3)]
         values = rounded(mine[3:4, :])
 
@@ -264,7 +319,7 @@
             dist_ref[at, :] = distance([coord_ref[a, k, at, :] for k in range(3)], rows, BLOCK)
             return 0
 
-        lax.fori_loop(0, steps, measure, 0, unroll=2)
+        lax.fori_loop(0, steps, measure, 0, unroll=8)
         back_ref[q] = jnp.zeros((LS, BLOCK), F32)
 
         def sweep(ids, number):
@@ -289,7 +344,7 @@
                 return tuple(fresh)
 
             held = tuple(jnp.zeros((8, BLOCK), F32) for _ in ids)
-            held = lax.fori_loop(0, steps, step, held, unroll=2)
+            held = lax.fori_loop(0, steps, step, held, unroll=8)
             for n in range(len(ids)):
                 back_ref[q, pl.ds(ids[n], 1), :] = jnp.sum(held[n], axis=0, keepdims=True)
                 store_copy(slots[n], number + n).start()
@@ -303,9 +358,12 @@
         number = lax.fori_loop(0, live // 2, two, number)
         return lax.cond(live % 2 == 1, lambda m: sweep([reach], m), lambda m: m, number)
 
-    number = lax.fori_loop(0, pairs_dev, pair, jnp.int32(0))
+    number = lax.fori_loop(0, pair_count, pair, jnp.int32(0))
     for back in range(4):
-        store_copy((number - 1 - back) % 4, number - 1 - back).wait()
+        @pl.when(number > back)
+        def _():
+            store_copy((number - 1 - back) % 4, number - 1 - back).wait()
+
     for s in range(count):
         out_ref[s] = fold_forward(forward_ref, s)
 
@@ -317,7 +375,7 @@
     slots = got_ref.shape[0]
     w_ref[...] = own_ref[...] + fwd_ref[...]
     for q in range(slots):
-        where = meta_ref[3, q]
+        where = meta_ref[4, q]
 
         @pl.when(where >= 0)
         def _():
@@ -333,7 +391,7 @@
         products[1] = products[1] + target * value
         products[2] = products[2] + value * value
     for q in range(slots):
-        send_ref[q] = w_ref[jnp.maximum(meta_ref[3, q], 0)]
+        send_ref[q] = w_ref[jnp.maximum(meta_ref[4, q], 0)]
     lane = lax.broadcasted_iota(jnp.int32, (LS, LANES), 1)
     held = jnp.zeros((LS, LANES), F32)
     for n in range(3):
@@ -347,7 +405,7 @@
     list_ref, col_ref, forward_ref, wz_ref, yz_ref, stage_ref, sem_ref,
 ):
     count = w_ref.shape[0]
-    pairs_dev = tiles_ref.shape[0] // LS
+    pair_count = meta_ref[5, 0]
     steps = BLOCK // CHUNK
     depth = stage_ref.shape[0]
 
@@ -361,21 +419,24 @@
 
         return lax.fori_loop(0, live, two, number)
 
-    number = lax.fori_loop(0, pairs_dev, list_pair, jnp.int32(0))
+    number = lax.fori_loop(0, pair_count, list_pair, jnp.int32(0))
 
     def load_copy(t):
         slot = t % depth
         return pltpu.make_async_copy(tiles_ref.at[t], stage_ref.at[slot], sem_ref.at[slot])
 
     for t in range(depth - 1):
-        load_copy(jnp.int32(t)).start()
+        @pl.when(t < number)
+        def _():
+            load_copy(jnp.int32(t)).start()
+
 
     def clear(p, _):
         q = meta_ref[1, p]
-        back_ref[q // CAP, pl.ds(pl.multiple_of((q % CAP) * LS, LS), LS), :] = jnp.zeros((LS, BLOCK), F32)
+        back_ref[over(q, CAP), pl.ds(pl.multiple_of(rest(q, CAP) * LS, LS), LS), :BLOCK] = jnp.zeros((LS, BLOCK), F32)
         return 0
 
-    lax.fori_loop(0, pairs_dev, clear, 0)
+    lax.fori_loop(0, pair_count, clear, 0)
     for s in range(count):
         columns = spread_columns(w_ref[s])
         for l in range(LS):
@@ -386,8 +447,8 @@
 
     def tile(t, _):
         entry = list_ref[t]
-        p = entry // LS
-        l = entry % LS
+        p = over(entry, LS)
+        l = rest(entry, LS)
         a = meta_ref[0, p]
         q = meta_ref[1, p]
         slot = t % depth
@@ -405,11 +466,10 @@
             forward_ref[a, l, at, :] += lane_fold(value * row)
             return held + sub_fold(value * wide(col_ref[a, l, at, :], BLOCK))
 
-        held = lax.fori_loop(0, steps, step, jnp.zeros((8, BLOCK), F32), unroll=4)
+        held = lax.fori_loop(0, steps, step, jnp.zeros((8, BLOCK), F32), unroll=32)
         result = jnp.sum(held, axis=0, keepdims=True)
-        back_ref[q // CAP, pl.ds((q % CAP) * LS + l, 1), :] = result
-        both = far_pts_ref[q // CAP]
-        target = jnp.where(q % CAP == 1, both[7:8, :], both[3:4, :])
+        back_ref[over(q, CAP), pl.ds(rest(q, CAP) * LS + l, 1), :BLOCK] = result
+        target = partner_rows(far_pts_ref, meta_ref[3, p])[3:4, :]
         wz_ref[pl.ds(l, 1), :] += result * row
         yz_ref[pl.ds(l, 1), :] += result * target
         return 0
@@ -426,34 +486,50 @@
     lane = lax.broadcasted_iota(jnp.int32, (LS, LANES), 1)
     held = jnp.where(lane == 3, jnp.sum(wz, axis=1, keepdims=True) * unit, dots_ref[...])
     held = jnp.where(lane == 4, jnp.sum(yz, axis=1, keepdims=True) * unit, held)
-    padded = jnp.concatenate([held, jnp.zeros((LS, BLOCK - LANES), F32)], axis=1)
     for c in range(back_ref.shape[0]):
-        back_ref[c, CAP * LS:(CAP + 1) * LS, :] = padded
-
-
-def gather_kernel(meta_ref, part_ref, got_ref, z_ref, dots_ref):
+        back_ref[c, 0:LS, BLOCK:] = held
+
+
+SPAN = LANES // LS
+
+
+def system_lanes(n):
+    sub = lax.broadcasted_iota(jnp.int32, (LS, LANES), 0)
+    lane = lax.broadcasted_iota(jnp.int32, (LS, LANES), 1)
+    return lane == sub * SPAN + n
+
+
+def dots_kernel(got_ref, dots_ref):
+    held = got_ref[0, 0:LS, :]
+    for c in range(1, got_ref.shape[0]):
+        held = held + got_ref[c, 0:LS, :]
+    row = jnp.zeros((LS, LANES), F32)
+    for n in range(DOTS):
+        row = jnp.where(system_lanes(n), held[:, n:n + 1], row)
+    row = jnp.sum(row, axis=0, keepdims=True)
+    dots_ref[...] = jnp.broadcast_to(row, dots_ref.shape)
+
+
+def gather_kernel(meta_ref, part_ref, got_ref, z_ref):
     z_ref[...] = part_ref[...]
-    held = jnp.zeros((LS, LANES), F32)
     for c in range(got_ref.shape[0]):
-        held = held + got_ref[c, CAP * LS:(CAP + 1) * LS, 0:LANES]
         for k in range(CAP):
-            where = meta_ref[3, c * CAP + k]
+            where = meta_ref[4, c * CAP + k]
 
             @pl.when(where >= 0)
             def _():
-                z_ref[where] = z_ref[where] + got_ref[c, k * LS:(k + 1) * LS, :]
+                z_ref[where] = z_ref[where] + got_ref[c, k * LS:(k + 1) * LS, :BLOCK]
 
     z_ref[...] = z_ref[...] * (1.0 / (2.0 * BLOCK))
-    for c in range(dots_ref.shape[0]):
-        dots_ref[c] = held
 
 
 def finish_kernel(noise_ref, loc_ref, w_ref, z_ref, dots_ref, sol_ref, res_ref):
-    dots = dots_ref[0]
-    for c in range(1, dots_ref.shape[0]):
-        dots = dots + dots_ref[c]
+    row = jnp.sum(dots_ref[...], axis=0, keepdims=True)
+    spread = jnp.broadcast_to(row, (LS, LANES))
     noise = per_system(noise_ref)[:, 0:1]
-    yy, yw, ww, wz, yz = [dots[:, n:n + 1] for n in range(5)]
+    yy, yw, ww, wz, yz = [
+        jnp.sum(jnp.where(system_lanes(n), spread, 0.0), axis=1, keepdims=True) for n in range(DOTS)
+    ]
     curve = noise * yy + yw
     first = yy / curve
     keep = yw / curve
@@ -481,21 +557,35 @@
     count = total // BLOCK
     pairs_dev = block_pairs.shape[1] // (rows * cols)
     slots = cols * CAP
+    most = (cols - 1) * CAP * LS
     field = jax.ShapeDtypeStruct((count, LS, BLOCK), F32)
 
-    loc, send, meta = pl.pallas_call(
-        lambda *refs: prepare_kernel(cols, count, pairs_dev, *refs),
+    loc, send = pl.pallas_call(
+        order_kernel,
         out_shape=(
             jax.ShapeDtypeStruct((count, 8, BLOCK), F32),
-            jax.ShapeDtypeStruct((cols, CAP * 4, BLOCK), F32),
-            jax.ShapeDtypeStruct((4, slots), jnp.int32),
+            jax.ShapeDtypeStruct((cols * (count // 2), 8, BLOCK), F32),
         ),
-        in_specs=[smem_spec(), vmem_spec(), vmem_spec(), vmem_spec(), smem_spec(), smem_spec()],
-        out_specs=(vmem_spec(), vmem_spec(), smem_spec()),
-        scratch_shapes=[SMEM((slots + 1,), jnp.int32), SMEM((cols,), jnp.int32)],
+        in_specs=[vmem_spec()] * 3,
+        out_specs=(vmem_spec(),) * 2,
         compiler_params=params(),
-        name="prepare",
-    )(me, points, targets.reshape(1, total), kd_order.reshape(1, total), block_owner, block_pairs)
+        name="order",
+    )(points, targets.reshape(1, total), kd_order.reshape(1, total))
+    meta = pl.pallas_call(
+        lambda *refs: plan_kernel(cols, count, pairs_dev, *refs),
+        out_shape=jax.ShapeDtypeStruct((8, SPARE + 1), jnp.int32),
+        in_specs=[smem_spec()] * 3,
+        out_specs=smem_spec(),
+        scratch_shapes=[
+            *[SMEM((cols * pairs_dev,), jnp.int32)] * 5,
+            SMEM((cols,), jnp.int32),
+            SMEM((cols * cols,), jnp.int32),
+            SMEM((cols * cols,), jnp.int32),
+        ],
+        compiler_params=params(),
+        cost_estimate=pl.CostEstimate(flops=10**9, bytes_accessed=10**6, transcendentals=0),
+        name="plan",
+    )(me, block_owner, block_pairs)
 
     slopes = CREST / lengthscales
 
@@ -523,7 +613,7 @@
         out_shape=(
             field,
             jax.ShapeDtypeStruct((slots, LS, BLOCK), F32),
-            jax.ShapeDtypeStruct((pairs_dev * LS, BLOCK, BLOCK), BF16),
+            jax.ShapeDtypeStruct((most, BLOCK, BLOCK), BF16),
         ),
         in_specs=[smem_spec(), smem_spec(), vmem_spec(), vmem_spec()],
         out_specs=(vmem_spec(), vmem_spec(), any_spec()),
@@ -556,11 +646,11 @@
     own_two = own(w, False)
     fwd_two, back_two = pl.pallas_call(
         second_kernel,
-        out_shape=(field, jax.ShapeDtypeStruct((cols, (CAP + 1) * LS, BLOCK), F32)),
+        out_shape=(field, jax.ShapeDtypeStruct((cols, CAP * LS, BLOCK + LANES), F32)),
         in_specs=[smem_spec()] + [vmem_spec()] * 6 + [any_spec()],
         out_specs=(vmem_spec(),) * 2,
         scratch_shapes=[
-            SMEM((pairs_dev * LS,), jnp.int32),
+            SMEM((most,), jnp.int32),
             VMEM((count, LS, BLOCK, LANES), F32),
             VMEM((count, LS, BLOCK, LANES), F32),
             VMEM((LS, BLOCK), F32),
@@ -574,15 +664,25 @@
     )(meta, loc, w, own_two, far, far_w, dots_one, tiles)
     got_two = lax.all_to_all(back_two, "col", split_axis=0, concat_axis=0, tiled=True)
 
-    z, dots_two = pl.pallas_call(
+    dots_two = pl.pallas_call(
+        dots_kernel,
+        out_shape=jax.ShapeDtypeStruct((rows, LANES), F32),
+        in_specs=[pl.BlockSpec((cols, LS, LANES), lambda i: (0, 0, BLOCK // LANES))],
+        out_specs=pl.BlockSpec((rows, LANES), lambda i: (0, 0)),
+        grid=(1,),
+        compiler_params=params(),
+        name="dots",
+    )(got_two)
+    dots = lax.all_to_all(dots_two, "row", split_axis=0, concat_axis=0, tiled=True)
+    z = pl.pallas_call(
         gather_kernel,
-        out_shape=(field, jax.ShapeDtypeStruct((rows, LS, LANES), F32)),
+        out_shape=field,
         in_specs=[smem_spec()] + [vmem_spec()] * 2,
-        out_specs=(vmem_spec(),) * 2,
+        out_specs=vmem_spec(),
         compiler_params=params(),
+        cost_estimate=pl.CostEstimate(flops=10**8, bytes_accessed=2 * 10**6, transcendentals=0),
         name="gather",
     )(meta, fwd_two, got_two)
-    dots = lax.all_to_all(dots_two, "row", split_axis=0, concat_axis=0, tiled=True)
     return pl.pallas_call(
         finish_kernel,
         out_shape=(jax.ShapeDtypeStruct((LS, total), F32),) * 2,

time: 207 us -> 181 us (0.87)
  blocking collectives: 40.3 us -> 20.2 us
  Pallas kernels: 131 us -> 126 us
  waiting for transfers between devices: 6.29 us -> 2.49 us
  starting transfers between devices: 24.5 us -> 27.2 us
    all_to_all x1 -> x0, blocking collectives: 19.6 us -> none  [on_device(): lax.all_to_all(dots_two, 'row', split_axis=0, concat_axis=0, tiled=True)]
    pallas_call x2 -> x4, Pallas kernels: 7.66 us -> 16.8 us  [the longest x1 11.3 us: on_device(): pl.pallas_call(lambda *refs: plan_kernel(cols, count, pairs_dev, *refs),...]
    all_to_all x1, waiting for transfers between devices: 6.29 us -> 0.01 us  [on_device(): far = lax.all_to_all(send, 'col', split_axis=0, concat_axis=0, tiled=True)]
    pallas_call x2, Pallas kernels: 37.5 us -> 31.4 us  [own(): pl.pallas_call(lambda *refs: own_kernel(common, *refs), out_shape=field,...]
    pallas_call x1, Pallas kernels: 28.2 us -> 23.4 us  [on_device(): pl.pallas_call(second_kernel, out_shape=(field, jax.ShapeDtypeStruct((col...]
    all_to_all x0 -> x1, starting transfers between devices: none -> 4.36 us  [on_device(): lax.all_to_all(dots_two, 'row', split_axis=0, concat_axis=0, tiled=True)]
    pallas_call x1, Pallas kernels: 53.1 us -> 50.1 us  [on_device(): pl.pallas_call(first_kernel, out_shape=(field, jax.ShapeDtypeStruct((slot...]
    all_to_all x0 -> x1, waiting for transfers between devices: none -> 2.49 us  [on_device(): lax.all_to_all(dots_two, 'row', split_axis=0, concat_axis=0, tiled=True)]
  transfers between devices with their start and end apart: 3 -> 4, of which waited for: 1 -> 1; matrix products, arithmetic and copies ran while one was open for 1% -> 1% of each run, Pallas kernels for 18% -> 25%
where the time goes in v2:
time: 181 us; the launch traced here: 180 us
  Pallas kernels  126 us (70%)
  starting transfers between devices  27.2 us (15%)
  blocking collectives  20.2 us (11%)
  local copies, waits for them, and re-layouts  2.99 us (2%)
  waiting for transfers between devices  2.49 us (1%)
    pallas_call x1, Pallas kernels, on_device(): pl.pallas_call(first_kernel, out_shape=(field, jax.ShapeDtypeStruct((slot...  50.1 us
    pallas_call x2, Pallas kernels, own(): pl.pallas_call(lambda *refs: own_kernel(common, *refs), out_shape=field,...  31.4 us
    pallas_call x1, Pallas kernels, on_device(): pl.pallas_call(second_kernel, out_shape=(field, jax.ShapeDtypeStruct((col...  23.4 us
    all_to_all x1, blocking collectives, on_device(): lax.all_to_all(back_two, 'col', split_axis=0, concat_axis=0, tiled=True)  20.2 us
    pallas_call x1, Pallas kernels, on_device(): pl.pallas_call(lambda *refs: plan_kernel(cols, count, pairs_dev, *refs),...  11.3 us
    all_to_all x1, starting transfers between devices, on_device(): far = lax.all_to_all(send, 'col', split_axis=0, concat_axis=0, tiled=True)  8.6 us
    all_to_all x1, starting transfers between devices, on_device(): lax.all_to_all(back_one, 'col', split_axis=0, concat_axis=0, tiled=True)  7.58 us
    all_to_all x1, starting transfers between devices, on_device(): lax.all_to_all(send_w, 'col', split_axis=0, concat_axis=0, tiled=True)  6.66 us
  transfers between devices with their start and end apart: 4, of which 1 were waited for; matrix products, arithmetic and copies ran while one was open for 1% of the time, Pallas kernels for 25%

profile of v2, /device:TPU:1, one launch (start us, length us, event | category | flops | bytes accessed | tf_op | source)
XLA Modules:
  0.0 180.5 jit_solution(1298239790411938410)
XLA Ops:
  0.6 2.0 %order.1 = (f32[4,8,512]{2,1,0:T(8,128)}, f32[32,8,512]{2,1,0:T(8,128)}) custom-call(f32[3,2048]{1,0:T(4,128)} %pts_ref.1, f32[1,2048]{1,0:T(1,128)} %bitcast.9, s32[1,2048]{1,0:T(1,128)} %bitcast.10), custom_call_target="tpu_custom_call" | custom-call | tf_op jit(solution)/shard_map/order/pallas_call | solution.py:563
  2.6 8.6 %all-to-all-start = ((f32[32,8,512]{2,1,0:T(8,128)}), f32[32,8,512]{2,1,0:T(8,128)S(1)}, u32[]{:S(2)}, u32[]{:S(2)}) async-start(f32[32,8,512]{2,1,0:T(8,128)} %get-tuple-element.13), calls=%async_computation | async-start | bytes 1048576 | tf_op jit(solution)/shard_map/all_to_all | solution.py:609
  11.2 11.3 %plan.1.meta_ref = s32[8,64]{1,0:T(8,128)} custom-call(s32[1]{0:T(128)} %bitcast.2.refs_0_, s32[512]{0:T(512)} %refs_1_.1, s32[3,2048]{1,0:T(4,128)} %refs_2_.1), custom_call_target="tpu_custom_call" | custom-call | flops 1000000000 | bytes 1000000 | tf_op jit(solution)/shard_map/plan/pallas_call | solution.py:574
  22.5 1.1 broadcast_divide_fusion.refs_0_.ls_ref
  23.7 0.0 all-to-all-done.far_ref.far_pts_ref
  23.7 0.0 copy-start
  23.7 0.8 copy-done
  24.5 50.1 %cross_first.1 = (f32[4,8,512]{2,1,0:T(8,128)}, f32[32,8,512]{2,1,0:T(8,128)}, bf16[240,512,512]{2,1,0:T(8,128)(2,1)}) custom-call(f32[8]{0:T(128)} %broadcast_divide_fusion.refs_0_.ls_ref, s32[8,64]{1,0:T(8,128)} %plan.1.meta_ref, f32[4,8,512]{2,1,0:T(8,128)} %get-tuple-element.12.refs_1_.refs_2_.loc_ref, f32[32,8,512]{2,1,0:T(8,128)} %copy-done), custom_call_target="tpu_custom_call" | custom-call | flops 10000000000 | bytes 60000000 | tf_op jit(solution)/shard_map/cross_first/pallas_call | solution.py:611
  74.6 7.6 %all-to-all-start.1 = ((f32[32,8,512]{2,1,0:T(8,128)}), f32[32,8,512]{2,1,0:T(8,128)S(1)}, u32[]{:S(2)}, u32[]{:S(2)}) async-start(f32[32,8,512]{2,1,0:T(8,128)} %get-tuple-element.15), calls=%async_computation.1 | async-start | bytes 1048576 | tf_op jit(solution)/shard_map/all_to_all | solution.py:631
  82.2 14.8 %own_first.1.own_ref = f32[4,8,512]{2,1,0:T(8,128)} custom-call(f32[8]{0:T(128)} %broadcast_divide_fusion.refs_0_.ls_ref, f32[4,8,512]{2,1,0:T(8,128)} %get-tuple-element.12.refs_1_.refs_2_.loc_ref, f32[4,8,512]{2,1,0:T(8,128)} %get-tuple-element.12.refs_1_.refs_2_.loc_ref), custom_call_target="tpu_custom_call" | custom-call | flops 2000000000 | bytes 1000000 | tf_op jit(solution)/shard_map/own_first/pallas_call | solution.py:593
  97.0 0.0 all-to-all-done.1.got_ref
  97.0 0.0 copy-start.2
  97.0 0.8 copy-done.2
  97.8 2.3 %combine.1 = (f32[4,8,512]{2,1,0:T(8,128)}, f32[32,8,512]{2,1,0:T(8,128)}, f32[8,128]{1,0:T(8,128)}) custom-call(s32[8,64]{1,0:T(8,128)} %plan.1.meta_ref, f32[4,8,512]{2,1,0:T(8,128)} %get-tuple-element.12.refs_1_.refs_2_.loc_ref, f32[4,8,512]{2,1,0:T(8,128)} %own_first.1.own_ref, f32[4,8,512]{2,1,0:T(8,128)} %get-tuple-element.14.fwd_ref, ...), custom_call_target="tpu_custom_call" | custom-call | tf_op jit(solution)/shard_map/combine/pallas_call | solution.py:633
  100.1 6.7 %all-to-all-start.2 = ((f32[32,8,512]{2,1,0:T(8,128)}), f32[32,8,512]{2,1,0:T(8,128)S(1)}, u32[]{:S(2)}, u32[]{:S(2)}) async-start(f32[32,8,512]{2,1,0:T(8,128)} %get-tuple-element.17), calls=%async_computation.2 | async-start | bytes 1048576 | tf_op jit(solution)/shard_map/all_to_all | solution.py:645
  106.8 16.6 %own_second.1.own_ref = f32[4,8,512]{2,1,0:T(8,128)} custom-call(f32[8]{0:T(128)} %broadcast_divide_fusion.refs_0_.ls_ref, f32[4,8,512]{2,1,0:T(8,128)} %get-tuple-element.12.refs_1_.refs_2_.loc_ref, f32[4,8,512]{2,1,0:T(8,128)} %get-tuple-element.16.refs_2_.w_ref), custom_call_target="tpu_custom_call" | custom-call | flops 2000000000 | bytes 1000000 | tf_op jit(solution)/shard_map/own_second/pallas_call | solution.py:593
  123.4 0.0 all-to-all-done.2.far_ref
  123.4 0.0 copy-start.1
  123.4 0.8 copy-done.1
  124.2 23.4 %cross_second.1 = (f32[4,8,512]{2,1,0:T(8,128)}, f32[16,16,640]{2,1,0:T(8,128)}) custom-call(s32[8,64]{1,0:T(8,128)} %plan.1.meta_ref, f32[4,8,512]{2,1,0:T(8,128)} %get-tuple-element.12.refs_1_.refs_2_.loc_ref, f32[4,8,512]{2,1,0:T(8,128)} %get-tuple-element.16.refs_2_.w_ref, f32[4,8,512]{2,1,0:T(8,128)} %own_second.1.own_ref, f32[32,8,512]{2,1,0:T(8,128)} %copy-done, ...), custom_call_target="tpu_custom_call" | custom-call | flops 5000000000 | bytes 60000000 | tf_op jit(solution)/shard_map/cross_second/pallas_call | solution.py:647
  147.6 20.2 %all_to_all.31.got_ref = f32[16,16,640]{2,1,0:T(8,128)} all-to-all(f32[16,16,640]{2,1,0:T(8,128)} %get-tuple-element.21), channel_id=1, replica_groups=mesh['row'=8,'col'=16] {'col'}, dimensions={0} | all-to-all | bytes 1310720 | tf_op jit(solution)/shard_map/all_to_all | solution.py:665
  167.8 1.5 dots.1
  169.3 4.4 %all-to-all-start.4 = ((f32[8,1,128]{2,1,0:T(1,128)}), f32[8,1,128]{2,1,0:T(1,128)S(1)}, u32[]{:S(2)}, u32[]{:S(2)}) async-start(f32[8,1,128]{2,1,0:T(1,128)} %bitcast.7), calls=%async_computation.4 | async-start | bytes 8192 | tf_op jit(solution)/shard_map/all_to_all | solution.py:676
  173.7 2.0 %gather.1.z_ref = f32[4,8,512]{2,1,0:T(8,128)} custom-call(s32[8,64]{1,0:T(8,128)} %plan.1.meta_ref, f32[4,8,512]{2,1,0:T(8,128)} %get-tuple-element.20.part_ref, f32[16,16,640]{2,1,0:T(8,128)} %all_to_all.31.got_ref), custom_call_target="tpu_custom_call" | custom-call | flops 100000000 | bytes 2000000 | tf_op jit(solution)/shard_map/gather/pallas_call | solution.py:677
  175.7 2.5 %all-to-all-done.4 = f32[8,1,128]{2,1,0:T(1,128)S(1)} async-done(((f32[8,1,128]{2,1,0:T(1,128)}), f32[8,1,128]{2,1,0:T(1,128)S(1)}, u32[]{:S(2)}, u32[]{:S(2)}) %all-to-all-start.4) | async-done | bytes 4128 | tf_op jit(solution)/shard_map/all_to_all | solution.py:676
  178.2 0.0 copy-start.3
  178.2 0.6 copy-done.3
  178.8 1.7 finish.1
Async XLA Ops:
  2.6 21.0 %all-to-all-start = ((f32[32,8,512]{2,1,0:T(8,128)}), f32[32,8,512]{2,1,0:T(8,128)S(1)}, u32[]{:S(2)}, u32[]{:S(2)}) async-start(f32[32,8,512]{2,1,0:T(8,128)} %get-tuple-element.13), calls=%async_computation | async-start | bytes 1048576 | tf_op jit(solution)/shard_map/all_to_all | solution.py:609
  23.7 0.8 copy-start
  74.6 22.4 %all-to-all-start.1 = ((f32[32,8,512]{2,1,0:T(8,128)}), f32[32,8,512]{2,1,0:T(8,128)S(1)}, u32[]{:S(2)}, u32[]{:S(2)}) async-start(f32[32,8,512]{2,1,0:T(8,128)} %get-tuple-element.15), calls=%async_computation.1 | async-start | bytes 1048576 | tf_op jit(solution)/shard_map/all_to_all | solution.py:631
  97.0 0.8 copy-start.2
  100.1 23.3 %all-to-all-start.2 = ((f32[32,8,512]{2,1,0:T(8,128)}), f32[32,8,512]{2,1,0:T(8,128)S(1)}, u32[]{:S(2)}, u32[]{:S(2)}) async-start(f32[32,8,512]{2,1,0:T(8,128)} %get-tuple-element.17), calls=%async_computation.2 | async-start | bytes 1048576 | tf_op jit(solution)/shard_map/all_to_all | solution.py:645
  123.4 0.8 copy-start.1
  169.3 8.9 %all-to-all-start.4 = ((f32[8,1,128]{2,1,0:T(1,128)}), f32[8,1,128]{2,1,0:T(1,128)S(1)}, u32[]{:S(2)}, u32[]{:S(2)}) async-start(f32[8,1,128]{2,1,0:T(1,128)} %bitcast.7), calls=%async_computation.4 | async-start | bytes 8192 | tf_op jit(solution)/shard_map/all_to_all | solution.py:676
  178.2 0.6 copy-start.3

commit v3 on v2

--- a/solution.py
+++ b/solution.py
@@ -15,7 +15,6 @@
 BF16 = jnp.bfloat16
 VMEM = pltpu.VMEM
 SMEM = pltpu.SMEM
-LIMIT = 56 * 2**20
 
 
 def vmem_spec():
@@ -30,8 +29,19 @@
     return pl.BlockSpec(memory_space=pl.ANY)
 
 
-def params():
-    return pltpu.CompilerParams(vmem_limit_bytes=LIMIT)
+def hbm_spec():
+    return pl.BlockSpec(memory_space=pltpu.HBM)
+
+
+def start_copies(sources, targets, sems):
+    copies = [pltpu.make_async_copy(a, b, sems.at[n]) for n, (a, b) in enumerate(zip(sources, targets))]
+    for copy in copies:
+        copy.start()
+    return copies
+
+
+def params(mebibytes):
+    return pltpu.CompilerParams(vmem_limit_bytes=mebibytes * 2**20)
 
 
 def over(value, size):
@@ -42,7 +52,9 @@
     return value & (size - 1) if size & (size - 1) == 0 else value % size
 
 
-def order_kernel(pts_ref, tgt_ref, order_ref, loc_ref, send_ref):
+def order_kernel(pts_hbm, tgt_hbm, order_hbm, loc_ref, send_ref, pts_ref, tgt_ref, order_ref, sems):
+    for copy in start_copies((pts_hbm, tgt_hbm, order_hbm), (pts_ref, tgt_ref, order_ref), sems):
+        copy.wait()
     total = pts_ref.shape[1]
     pieces = total // LANES
     per = BLOCK // LANES
@@ -69,48 +81,46 @@
 SPARE = 63
 
 
-def plan_kernel(cols, count, pairs_dev, me_ref, owner_ref, pairs_ref, meta_ref, near_ref, far_ref, peer_ref, reach_ref, turn_ref, load_ref, have_ref, used_ref):
-    row = over(me_ref[0], cols)
+def plan_kernel(cols, count, pairs_dev, me_ref, owner_hbm, pairs_hbm, meta_ref, peer_ref, cost_ref, turn_ref, load_ref, have_ref, asking_ref, used_ref, owner_ref, pairs_ref, sems):
+    copies = start_copies((owner_hbm, pairs_hbm), (owner_ref, pairs_ref), sems)
     mine = rest(me_ref[0], cols)
-    start = row * (cols * pairs_dev)
+    start = over(me_ref[0], cols) * (cols * pairs_dev)
 
     def clear(i, _):
         for c in range(cols):
             have_ref[i * cols + c] = 0
-            used_ref[i * cols + c] = 0
+        for c in range(4):
+            used_ref[c * cols + i] = 0
         return 0
 
     lax.fori_loop(0, cols, clear, 0)
     for q in range(cols * CAP):
         meta_ref[4, q] = -1
-
-    def cost_of(reach):
-        return 4 * (LS - reach) + 3
-
-    def read(d, _):
+    for copy in copies:
+        copy.wait()
+
+    def read(d, asking):
         total = jnp.int32(0)
         for j in range(pairs_dev):
             p = d * pairs_dev + j
-            first = owner_ref[pairs_ref[0, start + p]]
-            second = owner_ref[pairs_ref[1, start + p]]
-            reach = pairs_ref[2, start + p]
-            e = rest(over(second, count), cols)
-            near_ref[p] = rest(first, count)
-            far_ref[p] = rest(second, count)
+            e = rest(over(owner_ref[pairs_ref[1, start + p]], count), cols)
+            cost = 4 * (LS - pairs_ref[2, start + p]) + 3
             peer_ref[p] = e
-            reach_ref[p] = reach
-            total = total + cost_of(reach)
+            cost_ref[p] = cost
+            total = total + cost
             have_ref[d * cols + e] = have_ref[d * cols + e] + 1
+            asking_ref[asking] = p
+            asking = asking + (e == mine).astype(jnp.int32)
         load_ref[d] = total
-        return 0
-
-    lax.fori_loop(0, cols, read, 0)
+        return asking
+
+    asking = lax.fori_loop(0, cols, read, jnp.int32(0))
 
     def weigh(j, _):
         for d in range(cols):
             p = d * pairs_dev + j
             e = peer_ref[p]
-            cost = cost_of(reach_ref[p])
+            cost = cost_ref[p]
             here = load_ref[d]
             there = load_ref[e]
             back = have_ref[e * cols + d]
@@ -123,30 +133,35 @@
 
     lax.fori_loop(0, pairs_dev, weigh, 0)
 
-    def lay(d, number):
-        for j in range(pairs_dev):
-            p = d * pairs_dev + j
-            turn = turn_ref[p] == 1
-            e = peer_ref[p]
-            x = jnp.where(turn, e, d)
-            y = jnp.where(turn, d, e)
-            near = near_ref[p]
-            far = far_ref[p]
-            block_x = jnp.where(turn, far, near)
-            block_y = jnp.where(turn, near, far)
-            seen = used_ref[x * cols + y]
-            used_ref[x * cols + y] = seen + 1
-            ours = x == mine
-            at = jnp.where(ours, number, SPARE)
-            meta_ref[0, at] = block_x
-            meta_ref[1, at] = y * CAP + seen
-            meta_ref[2, at] = reach_ref[p]
-            meta_ref[3, at] = y * count + block_y
-            meta_ref[4, jnp.where(y == mine, x * CAP + seen, SPARE)] = block_y
-            number = number + ours.astype(jnp.int32)
-        return number
-
-    meta_ref[5, 0] = lax.fori_loop(0, cols, lay, jnp.int32(0))
+    def lay(p, other, here, number):
+        turn = turn_ref[p]
+        turned = turn == 1
+        near = rest(owner_ref[pairs_ref[0, start + p]], count)
+        far = rest(owner_ref[pairs_ref[1, start + p]], count)
+        at_used = (2 * here + turn) * cols + other
+        seen = used_ref[at_used]
+        used_ref[at_used] = seen + 1
+        slot = other * CAP + jnp.where(turned, CAP - 1 - seen, seen)
+        ours = turn == here
+        mine_block, their_block = (far, near) if here else (near, far)
+        at = jnp.where(ours, number, SPARE)
+        meta_ref[0, at] = mine_block
+        meta_ref[1, at] = slot
+        meta_ref[2, at] = pairs_ref[2, start + p]
+        meta_ref[3, at] = other * count + their_block
+        meta_ref[4, jnp.where(ours, SPARE, slot)] = mine_block
+        return number + ours.astype(jnp.int32)
+
+    number = jnp.int32(0)
+    for j in range(pairs_dev):
+        p = mine * pairs_dev + j
+        number = lay(p, peer_ref[p], 0, number)
+
+    def lay_asking(i, number):
+        p = asking_ref[i]
+        return lay(p, over(p, pairs_dev), 1, number)
+
+    meta_ref[5, 0] = lax.fori_loop(0, asking, lay_asking, number)
 
 
 def spread_columns(rows):
@@ -190,8 +205,13 @@
 CREST = 4.0**0.2
 
 
+def slope_of(scale):
+    one = CREST / jnp.full((8, LANES), scale, F32)
+    return jnp.concatenate([one] * (CHUNK // 8), axis=0)
+
+
 def kernel_value(dist, slope):
-    remain = jnp.maximum(CREST - dist * slope, 0.0)
+    remain = jnp.maximum(CREST - dist * wide(slope, dist.shape[1]), 0.0)
     squared = remain * remain
     return ((squared * squared) * (5.0 / CREST**4 - remain)).astype(BF16)
 
@@ -217,91 +237,105 @@
     return jnp.where(rest(which, 2) == 1, both[4:8, :], both[0:4, :])
 
 
-def own_kernel(common, ls_ref, loc_ref, vec_ref, out_ref, coord_ref, col_ref, dist_ref, forward_ref):
-    count = loc_ref.shape[0]
+def own_tiles(common, s, ls_ref, loc_ref, vec_ref, coord_ref, col_ref, dist_ref, forward_ref, out_ref):
     parts = BLOCK // LANES
     per = LANES // CHUNK
-
-    def block(s, _):
-        columns = spread_columns(loc_ref[s])
-        for k in range(4):
-            coord_ref[k] = columns[k]
-        if common:
-            coord_ref[3] = rounded(columns[3])
-        else:
-            columns = spread_columns(vec_ref[s])
-            for l in range(LS):
-                col_ref[l] = columns[l]
+    turns = LS // 2
+    for part in range(parts):
+        low = part * LANES
+        width = BLOCK - low
+        rows = [loc_ref[s, k:k + 1, low:] for k in range(3)]
+
+        def measure(c, _):
+            at = pl.ds(pl.multiple_of(low + c * CHUNK, CHUNK), CHUNK)
+            dist_ref[at, low:] = distance([coord_ref[k, at, :] for k in range(3)], rows, width)
+            return 0
+
+        lax.fori_loop(0, per, measure, 0, unroll=8)
+
+    def two(t, _):
+        back = [jnp.zeros((8, BLOCK), F32) for _ in range(2)]
+        ids = [2 * t, 2 * t + 1]
+        slopes = [slope_of(ls_ref[l]) for l in ids]
         for part in range(parts):
             low = part * LANES
             width = BLOCK - low
-            rows = [loc_ref[s, k:k + 1, low:] for k in range(3)]
-
-            def measure(c, _):
-                at = pl.ds(pl.multiple_of(low + c * CHUNK, CHUNK), CHUNK)
-                dist_ref[at, low:] = distance([coord_ref[k, at, :] for k in range(3)], rows, width)
-                return 0
-
-            lax.fori_loop(0, per, measure, 0, unroll=8)
-
-        def two(t, _):
-            back = [jnp.zeros((8, BLOCK), F32) for _ in range(2)]
-            ids = [2 * t, 2 * t + 1]
-            slopes = [ls_ref[l] for l in ids]
-            for part in range(parts):
-                low = part * LANES
-                width = BLOCK - low
-                if common:
-                    rows = [rounded(loc_ref[s, 3:4, low:])] * 2
-                else:
-                    rows = [vec_ref[s, pl.ds(l, 1), :][:, low:] for l in ids]
-
-                def step(c, held):
-                    at = pl.ds(pl.multiple_of(low + c * CHUNK, CHUNK), CHUNK)
-                    dist = dist_ref[at, low:]
-                    fresh = []
-                    for n in range(2):
-                        value = kernel_value(dist, slopes[n]).astype(F32)
-                        forward_ref[s, ids[n], at, :] = lane_fold(value * rows[n])
-                        if width > LANES:
-                            column = coord_ref[3, at, :] if common else col_ref[ids[n], at, :]
-                            right = value[:, LANES:] * wide(column, width - LANES)
-                            fresh.append(held[n] + sub_fold(right))
-                    return tuple(fresh) if fresh else held
-
-                start = max(width - LANES, LANES)
-                held = tuple(jnp.zeros((8, start), F32) for _ in range(2))
-                held = lax.fori_loop(0, per, step, held, unroll=8)
-                if width > LANES:
-                    for n in range(2):
-                        back[n] = jnp.concatenate(
-                            [back[n][:, :low + LANES], back[n][:, low + LANES:] + held[n]], axis=1
-                        )
-            for n in range(2):
-                out_ref[s, pl.ds(ids[n], 1), :] = jnp.sum(back[n], axis=0, keepdims=True)
-            return 0
-
-        lax.fori_loop(0, LS // 2, two, 0)
-        out_ref[s] = out_ref[s] + fold_forward(forward_ref, s)
+            if common:
+                rows = [rounded(loc_ref[s, 3:4, low:])] * 2
+            else:
+                rows = [vec_ref[s, pl.ds(l, 1), :][:, low:] for l in ids]
+
+            def step(c, held):
+                at = slice(low + c * CHUNK, low + (c + 1) * CHUNK)
+                dist = dist_ref[at, low:]
+                fresh = []
+                for n in range(2):
+                    value = kernel_value(dist, slopes[n]).astype(F32)
+                    forward_ref[ids[n], at, :] = lane_fold(value * rows[n])
+                    if width > LANES:
+                        column = coord_ref[3, at, :] if common else col_ref[ids[n], at, :]
+                        right = value[:, LANES:] * wide(column, width - LANES)
+                        fresh.append(held[n] + sub_fold(right))
+                return tuple(fresh) if fresh else held
+
+            start = max(width - LANES, LANES)
+            held = tuple(jnp.zeros((8, start), F32) for _ in range(2))
+            for c in range(per):
+                held = step(c, held)
+            if width > LANES:
+                for n in range(2):
+                    back[n] = jnp.concatenate(
+                        [back[n][:, :low + LANES], back[n][:, low + LANES:] + held[n]], axis=1
+                    )
+        for n in range(2):
+            out_ref[pl.ds(ids[n], 1), :] = jnp.sum(back[n], axis=0, keepdims=True)
         return 0
 
-    lax.fori_loop(0, count, block, 0)
+    lax.fori_loop(0, turns, two, 0)
+
+
+def own_kernel(common, ls_hbm, loc_ref, vec_ref, out_ref, coord_ref, col_ref, dist_ref, forward_ref, ls_ref, sems):
+    (ls_copy,) = start_copies((ls_hbm,), (ls_ref,), sems)
+    columns = spread_columns(loc_ref[0])
+    for k in range(4):
+        coord_ref[k] = columns[k]
+    if common:
+        coord_ref[3] = rounded(columns[3])
+    else:
+        columns = spread_columns(vec_ref[0])
+        for l in range(LS):
+            col_ref[l] = columns[l]
+    ls_copy.wait()
+    own_tiles(common, 0, ls_ref, loc_ref, vec_ref, coord_ref, col_ref, dist_ref, forward_ref.at[0], out_ref.at[0])
+    out_ref[0] = out_ref[0] + fold_forward(forward_ref, 0)
 
 
 def first_kernel(
-    ls_ref, meta_ref, loc_ref, far_ref,
+    ls_hbm, meta_ref, loc_ref, far_hbm_ref,
     out_ref, back_ref, tiles_ref,
-    coord_ref, dist_ref, forward_ref, stage_ref, sem_ref,
+    coord_ref, dist_ref, forward_ref, stage_ref, far_ref, ls_ref, sem_ref, far_sem,
 ):
     count = loc_ref.shape[0]
     pair_count = meta_ref[5, 0]
     steps = BLOCK // CHUNK
+    far_copy, ls_copy = start_copies((far_hbm_ref, ls_hbm), (far_ref, ls_ref), far_sem)
     for s in range(count):
         columns = spread_columns(loc_ref[s])
         for k in range(3):
             coord_ref[s, k] = columns[k]
         coord_ref[s, 3] = rounded(columns[3])
-    forward_ref[...] = jnp.zeros(forward_ref.shape, F32)
+    forward_ref[0] = jnp.zeros(forward_ref.shape[1:], F32)
+    out_ref[0] = jnp.zeros(out_ref.shape[1:], F32)
+
+    def own(s, _):
+        own_tiles(
+            True, s, ls_ref, loc_ref, None, coord_ref.at[s], None, dist_ref, forward_ref.at[s], out_ref.at[s]
+        )
+        return 0
+
+    ls_copy.wait()
+    lax.fori_loop(1, count, own, 0)
+    far_copy.wait()
 
     def store_copy(slot, number):
         return pltpu.make_async_copy(stage_ref.at[slot], tiles_ref.at[number], sem_ref.at[slot])
@@ -323,7 +357,7 @@
         back_ref[q] = jnp.zeros((LS, BLOCK), F32)
 
         def sweep(ids, number):
-            slopes = [ls_ref[l] for l in ids]
+            slopes = [slope_of(ls_ref[l]) for l in ids]
             slots = [(number + n) % 4 for n in range(len(ids))]
             for n in range(len(ids)):
                 @pl.when(number + n >= 4)
@@ -365,7 +399,7 @@
             store_copy((number - 1 - back) % 4, number - 1 - back).wait()
 
     for s in range(count):
-        out_ref[s] = fold_forward(forward_ref, s)
+        out_ref[s] = out_ref[s] + fold_forward(forward_ref, s)
 
 
 def combine_kernel(
@@ -373,7 +407,8 @@
 ):
     count = loc_ref.shape[0]
     slots = got_ref.shape[0]
-    w_ref[...] = own_ref[...] + fwd_ref[...]
+    w_ref[...] = fwd_ref[...]
+    w_ref[0] = w_ref[0] + own_ref[0]
     for q in range(slots):
         where = meta_ref[4, q]
 
@@ -400,14 +435,18 @@
 
 
 def second_kernel(
-    meta_ref, loc_ref, w_ref, own_ref, far_pts_ref, far_ref, dots_ref, tiles_ref,
+    ls_hbm, meta_ref, loc_ref, w_ref, own_ref, dots_ref, far_pts_hbm_ref, far_hbm_ref, tiles_ref,
     out_ref, back_ref,
-    list_ref, col_ref, forward_ref, wz_ref, yz_ref, stage_ref, sem_ref,
+    list_ref, coord_ref, col_ref, dist_ref, forward_ref, wz_ref, yz_ref, stage_ref, far_pts_ref, far_ref,
+    ls_ref, sem_ref, far_sem,
 ):
     count = w_ref.shape[0]
     pair_count = meta_ref[5, 0]
     steps = BLOCK // CHUNK
     depth = stage_ref.shape[0]
+    *copies, ls_copy = start_copies(
+        (far_pts_hbm_ref, far_hbm_ref, ls_hbm), (far_pts_ref, far_ref, ls_ref), far_sem
+    )
 
     def list_pair(p, number):
         reach = meta_ref[2, p]
@@ -441,7 +480,22 @@
         columns = spread_columns(w_ref[s])
         for l in range(LS):
             col_ref[s, l] = columns[l]
-    forward_ref[...] = jnp.zeros(forward_ref.shape, F32)
+    forward_ref[0] = jnp.zeros(forward_ref.shape[1:], F32)
+    out_ref[0] = own_ref[0]
+
+    def own(s, _):
+        columns = spread_columns(loc_ref[s])
+        for k in range(3):
+            coord_ref[k] = columns[k]
+        own_tiles(
+            False, s, ls_ref, loc_ref, w_ref, coord_ref, col_ref.at[s], dist_ref, forward_ref.at[s], out_ref.at[s]
+        )
+        return 0
+
+    ls_copy.wait()
+    lax.fori_loop(1, count, own, 0)
+    for copy in copies:
+        copy.wait()
     wz_ref[...] = jnp.zeros(wz_ref.shape, F32)
     yz_ref[...] = jnp.zeros(yz_ref.shape, F32)
 
@@ -478,7 +532,7 @@
     wz = wz_ref[...]
     yz = yz_ref[...]
     for s in range(count):
-        value = own_ref[s] + fold_forward(forward_ref, s)
+        value = out_ref[s] + fold_forward(forward_ref, s)
         out_ref[s] = value
         wz = wz + value * w_ref[s]
         yz = yz + value * loc_ref[s, 3:4, :]
@@ -566,47 +620,54 @@
             jax.ShapeDtypeStruct((count, 8, BLOCK), F32),
             jax.ShapeDtypeStruct((cols * (count // 2), 8, BLOCK), F32),
         ),
-        in_specs=[vmem_spec()] * 3,
+        in_specs=[hbm_spec()] * 3,
         out_specs=(vmem_spec(),) * 2,
-        compiler_params=params(),
+        scratch_shapes=[
+            VMEM((3, total), F32),
+            VMEM((1, total), F32),
+            VMEM((1, total), jnp.int32),
+            pltpu.SemaphoreType.DMA((3,)),
+        ],
+        compiler_params=params(8),
         name="order",
     )(points, targets.reshape(1, total), kd_order.reshape(1, total))
-    meta = pl.pallas_call(
-        lambda *refs: plan_kernel(cols, count, pairs_dev, *refs),
-        out_shape=jax.ShapeDtypeStruct((8, SPARE + 1), jnp.int32),
-        in_specs=[smem_spec()] * 3,
-        out_specs=smem_spec(),
-        scratch_shapes=[
-            *[SMEM((cols * pairs_dev,), jnp.int32)] * 5,
-            SMEM((cols,), jnp.int32),
-            SMEM((cols * cols,), jnp.int32),
-            SMEM((cols * cols,), jnp.int32),
-        ],
-        compiler_params=params(),
-        cost_estimate=pl.CostEstimate(flops=10**9, bytes_accessed=10**6, transcendentals=0),
-        name="plan",
-    )(me, block_owner, block_pairs)
-
-    slopes = CREST / lengthscales
-
     def own(vec, common):
         return pl.pallas_call(
             lambda *refs: own_kernel(common, *refs),
-            out_shape=field,
-            in_specs=[smem_spec(), vmem_spec(), vmem_spec()],
+            out_shape=jax.ShapeDtypeStruct((1, LS, BLOCK), F32),
+            in_specs=[hbm_spec(), vmem_spec(), vmem_spec()],
             out_specs=vmem_spec(),
             scratch_shapes=[
                 VMEM((4, BLOCK, LANES), F32),
                 VMEM((LS, BLOCK, LANES), F32),
                 VMEM((BLOCK, BLOCK), F32),
-                VMEM((count, LS, BLOCK, LANES), F32),
+                VMEM((1, LS, BLOCK, LANES), F32),
+                SMEM((LS,), F32),
+                pltpu.SemaphoreType.DMA((1,)),
             ],
-            compiler_params=params(),
+            compiler_params=params(16),
             cost_estimate=pl.CostEstimate(flops=2 * 10**9, bytes_accessed=10**6, transcendentals=0),
             name="own_first" if common else "own_second",
-        )(slopes, loc, vec)
+        )(lengthscales, loc, vec)
 
     far = lax.all_to_all(send, "col", split_axis=0, concat_axis=0, tiled=True)
+    meta = pl.pallas_call(
+        lambda *refs: plan_kernel(cols, count, pairs_dev, *refs),
+        out_shape=jax.ShapeDtypeStruct((8, SPARE + 1), jnp.int32),
+        in_specs=[smem_spec(), hbm_spec(), hbm_spec()],
+        out_specs=smem_spec(),
+        scratch_shapes=[
+            SMEM((n,), jnp.int32)
+            for n in [cols * pairs_dev] * 3 + [cols, cols * cols, cols * pairs_dev + 1, 4 * cols]
+        ] + [
+            SMEM(block_owner.shape, jnp.int32),
+            SMEM(block_pairs.shape, jnp.int32),
+            pltpu.SemaphoreType.DMA((2,)),
+        ],
+        compiler_params=params(8),
+        cost_estimate=pl.CostEstimate(flops=10**9, bytes_accessed=10**6, transcendentals=0),
+        name="plan",
+    )(me, block_owner, block_pairs)
     own_one = own(loc, True)
     fwd_one, back_one, tiles = pl.pallas_call(
         first_kernel,
@@ -615,19 +676,22 @@
             jax.ShapeDtypeStruct((slots, LS, BLOCK), F32),
             jax.ShapeDtypeStruct((most, BLOCK, BLOCK), BF16),
         ),
-        in_specs=[smem_spec(), smem_spec(), vmem_spec(), vmem_spec()],
+        in_specs=[hbm_spec(), smem_spec(), vmem_spec(), any_spec()],
         out_specs=(vmem_spec(), vmem_spec(), any_spec()),
         scratch_shapes=[
             VMEM((count, 4, BLOCK, LANES), F32),
             VMEM((BLOCK, BLOCK), F32),
             VMEM((count, LS, BLOCK, LANES), F32),
             VMEM((4, BLOCK, BLOCK), BF16),
+            VMEM((slots, LS, BLOCK), F32),
+            SMEM((LS,), F32),
             pltpu.SemaphoreType.DMA((4,)),
+            pltpu.SemaphoreType.DMA((2,)),
         ],
-        compiler_params=params(),
+        compiler_params=params(28),
         cost_estimate=pl.CostEstimate(flops=10**10, bytes_accessed=6 * 10**7, transcendentals=0),
         name="cross_first",
-    )(slopes, meta, loc, far)
+    )(lengthscales, meta, loc, far)
     got_one = lax.all_to_all(back_one, "col", split_axis=0, concat_axis=0, tiled=True)
 
     w, send_w, dots_one = pl.pallas_call(
@@ -639,7 +703,7 @@
         ),
         in_specs=[smem_spec()] + [vmem_spec()] * 4,
         out_specs=(vmem_spec(),) * 3,
-        compiler_params=params(),
+        compiler_params=params(8),
         name="combine",
     )(meta, loc, own_one, fwd_one, got_one)
     far_w = lax.all_to_all(send_w, "col", split_axis=0, concat_axis=0, tiled=True)
@@ -647,21 +711,27 @@
     fwd_two, back_two = pl.pallas_call(
         second_kernel,
         out_shape=(field, jax.ShapeDtypeStruct((cols, CAP * LS, BLOCK + LANES), F32)),
-        in_specs=[smem_spec()] + [vmem_spec()] * 6 + [any_spec()],
+        in_specs=[hbm_spec(), smem_spec()] + [vmem_spec()] * 4 + [any_spec()] * 3,
         out_specs=(vmem_spec(),) * 2,
         scratch_shapes=[
             SMEM((most,), jnp.int32),
+            VMEM((3, BLOCK, LANES), F32),
             VMEM((count, LS, BLOCK, LANES), F32),
+            VMEM((BLOCK, BLOCK), F32),
             VMEM((count, LS, BLOCK, LANES), F32),
             VMEM((LS, BLOCK), F32),
             VMEM((LS, BLOCK), F32),
             VMEM((8, BLOCK, BLOCK), BF16),
+            VMEM((slots, LS, BLOCK), F32),
+            VMEM((slots, LS, BLOCK), F32),
+            SMEM((LS,), F32),
             pltpu.SemaphoreType.DMA((8,)),
+            pltpu.SemaphoreType.DMA((3,)),
         ],
-        compiler_params=params(),
+        compiler_params=params(40),
         cost_estimate=pl.CostEstimate(flops=5 * 10**9, bytes_accessed=6 * 10**7, transcendentals=0),
         name="cross_second",
-    )(meta, loc, w, own_two, far, far_w, dots_one, tiles)
+    )(lengthscales, meta, loc, w, own_two, dots_one, far, far_w, tiles)
     got_two = lax.all_to_all(back_two, "col", split_axis=0, concat_axis=0, tiled=True)
 
     dots_two = pl.pallas_call(
@@ -670,7 +740,7 @@
         in_specs=[pl.BlockSpec((cols, LS, LANES), lambda i: (0, 0, BLOCK // LANES))],
         out_specs=pl.BlockSpec((rows, LANES), lambda i: (0, 0)),
         grid=(1,),
-        compiler_params=params(),
+        compiler_params=params(4),
         name="dots",
     )(got_two)
     dots = lax.all_to_all(dots_two, "row", split_axis=0, concat_axis=0, tiled=True)
@@ -679,7 +749,7 @@
         out_shape=field,
         in_specs=[smem_spec()] + [vmem_spec()] * 2,
         out_specs=vmem_spec(),
-        compiler_params=params(),
+        compiler_params=params(8),
         cost_estimate=pl.CostEstimate(flops=10**8, bytes_accessed=2 * 10**6, transcendentals=0),
         name="gather",
     )(meta, fwd_two, got_two)
@@ -688,7 +758,7 @@
         out_shape=(jax.ShapeDtypeStruct((LS, total), F32),) * 2,
         in_specs=[smem_spec()] + [vmem_spec()] * 4,
         out_specs=(vmem_spec(),) * 2,
-        compiler_params=params(),
+        compiler_params=params(8),
         name="finish",
     )(noise_level, loc, w, z, dots)
 

time: 181 us -> 171 us (0.945)
  Pallas kernels: 126 us -> 106 us
  waiting for transfers between devices: 2.49 us -> 14.1 us
  blocking collectives: 20.2 us -> 12.3 us
  local copies, waits for them, and re-layouts: 2.99 us -> 6.2 us
  starting transfers between devices: 27.2 us -> 30.2 us
    pallas_call x2, Pallas kernels: 31.4 us -> 7.9 us  [own(): pl.pallas_call(lambda *refs: own_kernel(common, *refs), out_shape=jax.Sha...]
    all_to_all x1, starting transfers between devices: 4.36 us -> 14.3 us  [on_device(): lax.all_to_all(dots_two, 'row', split_axis=0, concat_axis=0, tiled=True)]
    all_to_all x1, blocking collectives: 20.2 us -> 12.3 us  [on_device(): lax.all_to_all(back_two, 'col', split_axis=0, concat_axis=0, tiled=True)]
    pallas_call x1, Pallas kernels: 23.4 us -> 29.6 us  [on_device(): pl.pallas_call(second_kernel, out_shape=(field, jax.ShapeDtypeStruct((col...]
    pallas_call x1, Pallas kernels: 50.1 us -> 55.7 us  [on_device(): pl.pallas_call(first_kernel, out_shape=(field, jax.ShapeDtypeStruct((slot...]
    all_to_all x1, waiting for transfers between devices: 0.01 us -> 4.75 us  [on_device(): lax.all_to_all(back_one, 'col', split_axis=0, concat_axis=0, tiled=True)]
    all_to_all x1, waiting for transfers between devices: 0.01 us -> 4.13 us  [on_device(): lax.all_to_all(send_w, 'col', split_axis=0, concat_axis=0, tiled=True)]
    all_to_all x1, starting transfers between devices: 7.58 us -> 3.67 us  [on_device(): lax.all_to_all(back_one, 'col', split_axis=0, concat_axis=0, tiled=True)]
  transfers between devices with their start and end apart: 4 -> 4, of which waited for: 1 -> 4; matrix products, arithmetic and copies ran while one was open for 1% -> 0% of each run, Pallas kernels for 25% -> 10%
where the time goes in v3:
time: 171 us; the launch traced here: 170 us
  Pallas kernels  106 us (62%)
  starting transfers between devices  30.2 us (18%)
  waiting for transfers between devices  14.1 us (8%)
  blocking collectives  12.3 us (7%)
  local copies, waits for them, and re-layouts  6.2 us (4%)
    pallas_call x1, Pallas kernels, on_device(): pl.pallas_call(first_kernel, out_shape=(field, jax.ShapeDtypeStruct((slot...  55.7 us
    pallas_call x1, Pallas kernels, on_device(): pl.pallas_call(second_kernel, out_shape=(field, jax.ShapeDtypeStruct((col...  29.6 us
    all_to_all x1, starting transfers between devices, on_device(): lax.all_to_all(dots_two, 'row', split_axis=0, concat_axis=0, tiled=True)  14.3 us
    all_to_all x1, blocking collectives, on_device(): lax.all_to_all(back_two, 'col', split_axis=0, concat_axis=0, tiled=True)  12.3 us
    all_to_all x1, starting transfers between devices, on_device(): far = lax.all_to_all(send, 'col', split_axis=0, concat_axis=0, tiled=True)  8.61 us
    pallas_call x2, Pallas kernels, own(): pl.pallas_call(lambda *refs: own_kernel(common, *refs), out_shape=jax.Sha...  7.9 us
    pallas_call x1, Pallas kernels, on_device(): pl.pallas_call(lambda *refs: plan_kernel(cols, count, pairs_dev, *refs),...  7.4 us
    unnamed x20, local copies, waits for them, and re-layouts  6.2 us
  transfers between devices with their start and end apart: 4, of which 4 were waited for; matrix products, arithmetic and copies ran while one was open for 0% of the time, Pallas kernels for 10%

profile of v3, /device:TPU:1, one launch (start us, length us, event | category | flops | bytes accessed | tf_op | source)
XLA Modules:
  0.0 170.0 jit_solution(2484475432099638794)
XLA Ops:
  0.6 0.0 copy-start.3
  0.6 0.0 copy-start
  0.7 0.8 copy-done
  1.4 0.0 copy-start.1
  1.4 0.7 copy-done.1
  2.1 0.0 copy-start.2
  2.1 0.7 copy-done.2
  2.8 1.3 order.1
  4.1 8.6 %all-to-all-start = ((f32[32,8,512]{2,1,0:T(8,128)}), f32[32,8,512]{2,1,0:T(8,128)S(1)}, u32[]{:S(2)}, u32[]{:S(2)}) async-start(f32[32,8,512]{2,1,0:T(8,128)} %get-tuple-element.13), calls=%async_computation | async-start | bytes 1048576 | tf_op jit(solution)/shard_map/all_to_all | solution.py:653
  12.7 0.0 copy-start.8
  12.7 0.7 copy-done.8
  13.5 0.0 copy-start.9
  13.5 0.7 copy-done.9
  14.2 7.4 %plan.1.meta_ref = s32[8,64]{1,0:T(8,128)S(1)} custom-call(s32[1]{0:T(128)} %bitcast.2.refs_0_, s32[512]{0:T(512)S(1)} %copy-done.9, s32[3,2048]{1,0:T(4,128)S(1)} %copy-done.8), custom_call_target="tpu_custom_call" | custom-call | flops 1000000000 | bytes 1000000 | tf_op jit(solution)/shard_map/plan/pallas_call | solution.py:654
  21.6 1.6 all-to-all-done.far_hbm_ref.far_pts_hbm_ref
  23.2 0.0 copy-start.4
  23.2 0.7 copy-done.4
  23.9 55.7 %cross_first.1 = (f32[4,8,512]{2,1,0:T(8,128)S(1)}, f32[32,8,512]{2,1,0:T(8,128)}, bf16[240,512,512]{2,1,0:T(8,128)(2,1)}) custom-call(f32[8]{0:T(128)S(1)} %copy-done.4, s32[8,64]{1,0:T(8,128)S(1)} %plan.1.meta_ref, f32[4,8,512]{2,1,0:T(8,128)S(1)} %get-tuple-element.12.refs_1_.refs_2_.loc_ref, f32[32,8,512]{2,1,0:T(8,128)S(1)} %all-to-all-done.far_hbm_ref.far_pts_hbm_ref), custom_call_target="tpu_custom_call" | custom-call | flops 10000000000 | bytes 60000000 | tf_op jit(solution)/shard_map/cross_first/pallas_call | solution.py:672
  79.6 3.7 %all-to-all-start.1 = ((f32[32,8,512]{2,1,0:T(8,128)}), f32[32,8,512]{2,1,0:T(8,128)S(1)}, u32[]{:S(2)}, u32[]{:S(2)}) async-start(f32[32,8,512]{2,1,0:T(8,128)} %get-tuple-element.15), calls=%async_computation.1 | async-start | bytes 1048576 | tf_op jit(solution)/shard_map/all_to_all | solution.py:695
  83.3 0.0 copy-start.5
  83.3 0.6 copy-done.5
  83.9 3.7 %own_first.1.own_ref = f32[1,8,512]{2,1,0:T(8,128)S(1)} custom-call(f32[8]{0:T(128)S(1)} %copy-done.5, f32[4,8,512]{2,1,0:T(8,128)S(1)} %get-tuple-element.12.refs_1_.refs_2_.loc_ref, f32[4,8,512]{2,1,0:T(8,128)S(1)} %get-tuple-element.12.refs_1_.refs_2_.loc_ref), custom_call_target="tpu_custom_call" | custom-call | flops 2000000000 | bytes 1000000 | tf_op jit(solution)/shard_map/own_first/pallas_call | solution.py:635
  87.7 4.7 %all-to-all-done.1.got_ref = f32[32,8,512]{2,1,0:T(8,128)S(1)} async-done(((f32[32,8,512]{2,1,0:T(8,128)}), f32[32,8,512]{2,1,0:T(8,128)S(1)}, u32[]{:S(2)}, u32[]{:S(2)}) %all-to-all-start.1) | async-done | bytes 524320 | tf_op jit(solution)/shard_map/all_to_all | solution.py:695
  92.4 1.7 %combine.1 = (f32[4,8,512]{2,1,0:T(8,128)S(1)}, f32[32,8,512]{2,1,0:T(8,128)}, f32[8,128]{1,0:T(8,128)S(1)}) custom-call(s32[8,64]{1,0:T(8,128)S(1)} %plan.1.meta_ref, f32[4,8,512]{2,1,0:T(8,128)S(1)} %get-tuple-element.12.refs_1_.refs_2_.loc_ref, f32[1,8,512]{2,1,0:T(8,128)S(1)} %own_first.1.own_ref, f32[4,8,512]{2,1,0:T(8,128)S(1)} %get-tuple-element.14.fwd_ref, ...), custom_call_target="tpu_custom_call" | custom-call | tf_op jit(solution)/shard_map/combine/pallas_call | solution.py:697
  94.1 3.6 %all-to-all-start.2 = ((f32[32,8,512]{2,1,0:T(8,128)}), f32[32,8,512]{2,1,0:T(8,128)S(1)}, u32[]{:S(2)}, u32[]{:S(2)}) async-start(f32[32,8,512]{2,1,0:T(8,128)} %get-tuple-element.18), calls=%async_computation.2 | async-start | bytes 1048576 | tf_op jit(solution)/shard_map/all_to_all | solution.py:709
  97.7 0.0 copy-start.6
  97.7 0.6 copy-done.6
  98.3 4.2 %own_second.1.own_ref = f32[1,8,512]{2,1,0:T(8,128)S(1)} custom-call(f32[8]{0:T(128)S(1)} %copy-done.6, f32[4,8,512]{2,1,0:T(8,128)S(1)} %get-tuple-element.12.refs_1_.refs_2_.loc_ref, f32[4,8,512]{2,1,0:T(8,128)S(1)} %get-tuple-element.16.refs_2_.w_ref), custom_call_target="tpu_custom_call" | custom-call | flops 2000000000 | bytes 1000000 | tf_op jit(solution)/shard_map/own_second/pallas_call | solution.py:635
  102.5 4.1 %all-to-all-done.2.far_hbm_ref = f32[32,8,512]{2,1,0:T(8,128)S(1)} async-done(((f32[32,8,512]{2,1,0:T(8,128)}), f32[32,8,512]{2,1,0:T(8,128)S(1)}, u32[]{:S(2)}, u32[]{:S(2)}) %all-to-all-start.2) | async-done | bytes 524320 | tf_op jit(solution)/shard_map/all_to_all | solution.py:709
  106.7 0.0 copy-start.7
  106.7 0.7 copy-done.7
  107.3 29.6 %cross_second.1 = (f32[4,8,512]{2,1,0:T(8,128)S(1)}, f32[16,16,640]{2,1,0:T(8,128)S(1)}) custom-call(f32[8]{0:T(128)S(1)} %copy-done.7, s32[8,64]{1,0:T(8,128)S(1)} %plan.1.meta_ref, f32[4,8,512]{2,1,0:T(8,128)S(1)} %get-tuple-element.12.refs_1_.refs_2_.loc_ref, f32[4,8,512]{2,1,0:T(8,128)S(1)} %get-tuple-element.16.refs_2_.w_ref, ...), custom_call_target="tpu_custom_call" | custom-call | flops 5000000000 | bytes 60000000 | tf_op jit(solution)/shard_map/cross_second/pallas_call | solution.py:711
  136.9 12.3 %all_to_all.31.got_ref = f32[16,16,640]{2,1,0:T(8,128)S(1)} all-to-all(f32[16,16,640]{2,1,0:T(8,128)S(1)} %get-tuple-element.21), channel_id=1, replica_groups=mesh['row'=8,'col'=16] {'col'}, dimensions={0} | all-to-all | bytes 1310720 | tf_op jit(solution)/shard_map/all_to_all | solution.py:735
  149.2 0.7 dots.1
  149.9 14.3 %all-to-all-start.4 = ((f32[8,1,128]{2,1,0:T(1,128)}), f32[8,1,128]{2,1,0:T(1,128)S(1)}, u32[]{:S(2)}, u32[]{:S(2)}) async-start(f32[8,1,128]{2,1,0:T(1,128)} %bitcast.4), calls=%async_computation.4 | async-start | bytes 8192 | tf_op jit(solution)/shard_map/all_to_all | solution.py:746
  164.2 0.9 gather.1.z_ref
  165.1 3.6 %all-to-all-done.4 = f32[8,1,128]{2,1,0:T(1,128)S(1)} async-done(((f32[8,1,128]{2,1,0:T(1,128)}), f32[8,1,128]{2,1,0:T(1,128)S(1)}, u32[]{:S(2)}, u32[]{:S(2)}) %all-to-all-start.4) | async-done | bytes 4128 | tf_op jit(solution)/shard_map/all_to_all | solution.py:746
  168.7 0.0 copy-done.3
  168.7 1.3 finish.1
Async XLA Ops:
  0.6 168.1 %copy-start.3 = (f32[8]{0:T(128)S(1)}, f32[8]{0:T(128)}, u32[]{:S(2)}) copy-start(f32[8]{0:T(128)} %noise_ref.1) | copy-start | bytes 100
  0.6 0.8 copy-start
  1.4 0.7 copy-start.1
  2.1 0.7 copy-start.2
  4.1 19.1 %all-to-all-start = ((f32[32,8,512]{2,1,0:T(8,128)}), f32[32,8,512]{2,1,0:T(8,128)S(1)}, u32[]{:S(2)}, u32[]{:S(2)}) async-start(f32[32,8,512]{2,1,0:T(8,128)} %get-tuple-element.13), calls=%async_computation | async-start | bytes 1048576 | tf_op jit(solution)/shard_map/all_to_all | solution.py:653
  12.7 0.8 copy-start.8
  13.5 0.7 copy-start.9
  23.2 0.7 copy-start.4
  79.6 12.8 %all-to-all-start.1 = ((f32[32,8,512]{2,1,0:T(8,128)}), f32[32,8,512]{2,1,0:T(8,128)S(1)}, u32[]{:S(2)}, u32[]{:S(2)}) async-start(f32[32,8,512]{2,1,0:T(8,128)} %get-tuple-element.15), calls=%async_computation.1 | async-start | bytes 1048576 | tf_op jit(solution)/shard_map/all_to_all | solution.py:695
  83.3 0.7 copy-start.5
  94.1 12.6 %all-to-all-start.2 = ((f32[32,8,512]{2,1,0:T(8,128)}), f32[32,8,512]{2,1,0:T(8,128)S(1)}, u32[]{:S(2)}, u32[]{:S(2)}) async-start(f32[32,8,512]{2,1,0:T(8,128)} %get-tuple-element.18), calls=%async_computation.2 | async-start | bytes 1048576 | tf_op jit(solution)/shard_map/all_to_all | solution.py:709
  97.7 0.7 copy-start.6
  106.7 0.7 copy-start.7
  149.9 18.8 %all-to-all-start.4 = ((f32[8,1,128]{2,1,0:T(1,128)}), f32[8,1,128]{2,1,0:T(1,128)S(1)}, u32[]{:S(2)}, u32[]{:S(2)}) async-start(f32[8,1,128]{2,1,0:T(1,128)} %bitcast.4), calls=%async_computation.4 | async-start | bytes 8192 | tf_op jit(solution)/shard_map/all_to_all | solution.py:746

commit v4 on v3

--- a/solution.py
+++ b/solution.py
@@ -11,6 +11,7 @@
 LANES = 128
 CHUNK = 16
 DOTS = 5
+APART = 2
 F32 = jnp.float32
 BF16 = jnp.bfloat16
 VMEM = pltpu.VMEM
@@ -52,9 +53,10 @@
     return value & (size - 1) if size & (size - 1) == 0 else value % size
 
 
-def order_kernel(pts_hbm, tgt_hbm, order_hbm, loc_ref, send_ref, pts_ref, tgt_ref, order_ref, sems):
+def order_kernel(scale_ref, pts_hbm, tgt_hbm, order_hbm, loc_ref, send_ref, slope_ref, pts_ref, tgt_ref, order_ref, sems):
     for copy in start_copies((pts_hbm, tgt_hbm, order_hbm), (pts_ref, tgt_ref, order_ref), sems):
         copy.wait()
+    slope_ref[...] = CREST / per_system(scale_ref)
     total = pts_ref.shape[1]
     pieces = total // LANES
     per = BLOCK // LANES
@@ -205,9 +207,8 @@
 CREST = 4.0**0.2
 
 
-def slope_of(scale):
-    one = CREST / jnp.full((8, LANES), scale, F32)
-    return jnp.concatenate([one] * (CHUNK // 8), axis=0)
+def slope_of(slope_ref, l):
+    return jnp.broadcast_to(slope_ref[pl.ds(l, 1), :], (CHUNK, LANES))
 
 
 def kernel_value(dist, slope):
@@ -256,7 +257,7 @@
     def two(t, _):
         back = [jnp.zeros((8, BLOCK), F32) for _ in range(2)]
         ids = [2 * t, 2 * t + 1]
-        slopes = [slope_of(ls_ref[l]) for l in ids]
+        slopes = [slope_of(ls_ref, l) for l in ids]
         for part in range(parts):
             low = part * LANES
             width = BLOCK - low
@@ -294,38 +295,43 @@
     lax.fori_loop(0, turns, two, 0)
 
 
-def own_kernel(common, ls_hbm, loc_ref, vec_ref, out_ref, coord_ref, col_ref, dist_ref, forward_ref, ls_ref, sems):
-    (ls_copy,) = start_copies((ls_hbm,), (ls_ref,), sems)
-    columns = spread_columns(loc_ref[0])
-    for k in range(4):
-        coord_ref[k] = columns[k]
-    if common:
-        coord_ref[3] = rounded(columns[3])
-    else:
-        columns = spread_columns(vec_ref[0])
-        for l in range(LS):
-            col_ref[l] = columns[l]
-    ls_copy.wait()
-    own_tiles(common, 0, ls_ref, loc_ref, vec_ref, coord_ref, col_ref, dist_ref, forward_ref.at[0], out_ref.at[0])
-    out_ref[0] = out_ref[0] + fold_forward(forward_ref, 0)
+def own_kernel(common, ls_ref, loc_ref, vec_ref, out_ref, coord_ref, col_ref, dist_ref, forward_ref):
+    def block(s, _):
+        columns = spread_columns(loc_ref[s])
+        for k in range(4):
+            coord_ref[k] = columns[k]
+        if common:
+            coord_ref[3] = rounded(columns[3])
+        else:
+            columns = spread_columns(vec_ref[s])
+            for l in range(LS):
+                col_ref[l] = columns[l]
+        own_tiles(
+            common, s, ls_ref, loc_ref, vec_ref, coord_ref, col_ref, dist_ref, forward_ref.at[0], out_ref.at[s]
+        )
+        out_ref[s] = out_ref[s] + fold_forward(forward_ref, 0)
+        return 0
+
+    lax.fori_loop(0, APART, block, 0)
 
 
 def first_kernel(
-    ls_hbm, meta_ref, loc_ref, far_hbm_ref,
+    ls_ref, meta_ref, loc_ref, far_hbm_ref,
     out_ref, back_ref, tiles_ref,
-    coord_ref, dist_ref, forward_ref, stage_ref, far_ref, ls_ref, sem_ref, far_sem,
+    coord_ref, dist_ref, forward_ref, stage_ref, far_ref, sem_ref, far_sem,
 ):
     count = loc_ref.shape[0]
     pair_count = meta_ref[5, 0]
     steps = BLOCK // CHUNK
-    far_copy, ls_copy = start_copies((far_hbm_ref, ls_hbm), (far_ref, ls_ref), far_sem)
+    (far_copy,) = start_copies((far_hbm_ref,), (far_ref,), far_sem)
     for s in range(count):
         columns = spread_columns(loc_ref[s])
         for k in range(3):
             coord_ref[s, k] = columns[k]
         coord_ref[s, 3] = rounded(columns[3])
-    forward_ref[0] = jnp.zeros(forward_ref.shape[1:], F32)
-    out_ref[0] = jnp.zeros(out_ref.shape[1:], F32)
+    for s in range(APART):
+        forward_ref[s] = jnp.zeros(forward_ref.shape[1:], F32)
+        out_ref[s] = jnp.zeros(out_ref.shape[1:], F32)
 
     def own(s, _):
         own_tiles(
@@ -333,8 +339,7 @@
         )
         return 0
 
-    ls_copy.wait()
-    lax.fori_loop(1, count, own, 0)
+    lax.fori_loop(APART, count, own, 0)
     far_copy.wait()
 
     def store_copy(slot, number):
@@ -357,7 +362,7 @@
         back_ref[q] = jnp.zeros((LS, BLOCK), F32)
 
         def sweep(ids, number):
-            slopes = [slope_of(ls_ref[l]) for l in ids]
+            slopes = [slope_of(ls_ref, l) for l in ids]
             slots = [(number + n) % 4 for n in range(len(ids))]
             for n in range(len(ids)):
                 @pl.when(number + n >= 4)
@@ -408,7 +413,8 @@
     count = loc_ref.shape[0]
     slots = got_ref.shape[0]
     w_ref[...] = fwd_ref[...]
-    w_ref[0] = w_ref[0] + own_ref[0]
+    for s in range(APART):
+        w_ref[s] = w_ref[s] + own_ref[s]
     for q in range(slots):
         where = meta_ref[4, q]
 
@@ -435,18 +441,16 @@
 
 
 def second_kernel(
-    ls_hbm, meta_ref, loc_ref, w_ref, own_ref, dots_ref, far_pts_hbm_ref, far_hbm_ref, tiles_ref,
+    ls_ref, meta_ref, loc_ref, w_ref, own_ref, dots_ref, far_pts_hbm_ref, far_hbm_ref, tiles_ref,
     out_ref, back_ref,
     list_ref, coord_ref, col_ref, dist_ref, forward_ref, wz_ref, yz_ref, stage_ref, far_pts_ref, far_ref,
-    ls_ref, sem_ref, far_sem,
+    sem_ref, far_sem,
 ):
     count = w_ref.shape[0]
     pair_count = meta_ref[5, 0]
     steps = BLOCK // CHUNK
     depth = stage_ref.shape[0]
-    *copies, ls_copy = start_copies(
-        (far_pts_hbm_ref, far_hbm_ref, ls_hbm), (far_pts_ref, far_ref, ls_ref), far_sem
-    )
+    copies = start_copies((far_pts_hbm_ref, far_hbm_ref), (far_pts_ref, far_ref), far_sem)
 
     def list_pair(p, number):
         reach = meta_ref[2, p]
@@ -480,8 +484,9 @@
         columns = spread_columns(w_ref[s])
         for l in range(LS):
             col_ref[s, l] = columns[l]
-    forward_ref[0] = jnp.zeros(forward_ref.shape[1:], F32)
-    out_ref[0] = own_ref[0]
+    for s in range(APART):
+        forward_ref[s] = jnp.zeros(forward_ref.shape[1:], F32)
+        out_ref[s] = own_ref[s]
 
     def own(s, _):
         columns = spread_columns(loc_ref[s])
@@ -492,8 +497,7 @@
         )
         return 0
 
-    ls_copy.wait()
-    lax.fori_loop(1, count, own, 0)
+    lax.fori_loop(APART, count, own, 0)
     for copy in copies:
         copy.wait()
     wz_ref[...] = jnp.zeros(wz_ref.shape, F32)
@@ -614,14 +618,15 @@
     most = (cols - 1) * CAP * LS
     field = jax.ShapeDtypeStruct((count, LS, BLOCK), F32)
 
-    loc, send = pl.pallas_call(
+    loc, send, slopes = pl.pallas_call(
         order_kernel,
         out_shape=(
             jax.ShapeDtypeStruct((count, 8, BLOCK), F32),
             jax.ShapeDtypeStruct((cols * (count // 2), 8, BLOCK), F32),
+            jax.ShapeDtypeStruct((LS, LANES), F32),
         ),
-        in_specs=[hbm_spec()] * 3,
-        out_specs=(vmem_spec(),) * 2,
+        in_specs=[smem_spec()] + [hbm_spec()] * 3,
+        out_specs=(vmem_spec(),) * 3,
         scratch_shapes=[
             VMEM((3, total), F32),
             VMEM((1, total), F32),
@@ -630,25 +635,23 @@
         ],
         compiler_params=params(8),
         name="order",
-    )(points, targets.reshape(1, total), kd_order.reshape(1, total))
+    )(lengthscales, points, targets.reshape(1, total), kd_order.reshape(1, total))
     def own(vec, common):
         return pl.pallas_call(
             lambda *refs: own_kernel(common, *refs),
-            out_shape=jax.ShapeDtypeStruct((1, LS, BLOCK), F32),
-            in_specs=[hbm_spec(), vmem_spec(), vmem_spec()],
+            out_shape=jax.ShapeDtypeStruct((APART, LS, BLOCK), F32),
+            in_specs=[vmem_spec(), vmem_spec(), vmem_spec()],
             out_specs=vmem_spec(),
             scratch_shapes=[
                 VMEM((4, BLOCK, LANES), F32),
                 VMEM((LS, BLOCK, LANES), F32),
                 VMEM((BLOCK, BLOCK), F32),
                 VMEM((1, LS, BLOCK, LANES), F32),
-                SMEM((LS,), F32),
-                pltpu.SemaphoreType.DMA((1,)),
             ],
             compiler_params=params(16),
             cost_estimate=pl.CostEstimate(flops=2 * 10**9, bytes_accessed=10**6, transcendentals=0),
             name="own_first" if common else "own_second",
-        )(lengthscales, loc, vec)
+        )(slopes, loc, vec)
 
     far = lax.all_to_all(send, "col", split_axis=0, concat_axis=0, tiled=True)
     meta = pl.pallas_call(
@@ -676,7 +679,7 @@
             jax.ShapeDtypeStruct((slots, LS, BLOCK), F32),
             jax.ShapeDtypeStruct((most, BLOCK, BLOCK), BF16),
         ),
-        in_specs=[hbm_spec(), smem_spec(), vmem_spec(), any_spec()],
+        in_specs=[vmem_spec(), smem_spec(), vmem_spec(), any_spec()],
         out_specs=(vmem_spec(), vmem_spec(), any_spec()),
         scratch_shapes=[
             VMEM((count, 4, BLOCK, LANES), F32),
@@ -684,14 +687,13 @@
             VMEM((count, LS, BLOCK, LANES), F32),
             VMEM((4, BLOCK, BLOCK), BF16),
             VMEM((slots, LS, BLOCK), F32),
-            SMEM((LS,), F32),
             pltpu.SemaphoreType.DMA((4,)),
-            pltpu.SemaphoreType.DMA((2,)),
+            pltpu.SemaphoreType.DMA((1,)),
         ],
         compiler_params=params(28),
         cost_estimate=pl.CostEstimate(flops=10**10, bytes_accessed=6 * 10**7, transcendentals=0),
         name="cross_first",
-    )(lengthscales, meta, loc, far)
+    )(slopes, meta, loc, far)
     got_one = lax.all_to_all(back_one, "col", split_axis=0, concat_axis=0, tiled=True)
 
     w, send_w, dots_one = pl.pallas_call(
@@ -711,7 +713,7 @@
     fwd_two, back_two = pl.pallas_call(
         second_kernel,
         out_shape=(field, jax.ShapeDtypeStruct((cols, CAP * LS, BLOCK + LANES), F32)),
-        in_specs=[hbm_spec(), smem_spec()] + [vmem_spec()] * 4 + [any_spec()] * 3,
+        in_specs=[vmem_spec(), smem_spec()] + [vmem_spec()] * 4 + [any_spec()] * 3,
         out_specs=(vmem_spec(),) * 2,
         scratch_shapes=[
             SMEM((most,), jnp.int32),
@@ -724,14 +726,13 @@
             VMEM((8, BLOCK, BLOCK), BF16),
             VMEM((slots, LS, BLOCK), F32),
             VMEM((slots, LS, BLOCK), F32),
-            SMEM((LS,), F32),
             pltpu.SemaphoreType.DMA((8,)),
-            pltpu.SemaphoreType.DMA((3,)),
+            pltpu.SemaphoreType.DMA((2,)),
         ],
         compiler_params=params(40),
         cost_estimate=pl.CostEstimate(flops=5 * 10**9, bytes_accessed=6 * 10**7, transcendentals=0),
         name="cross_second",
-    )(lengthscales, meta, loc, w, own_two, dots_one, far, far_w, tiles)
+    )(slopes, meta, loc, w, own_two, dots_one, far, far_w, tiles)
     got_two = lax.all_to_all(back_two, "col", split_axis=0, concat_axis=0, tiled=True)
 
     dots_two = pl.pallas_call(

time: 171 us -> 166 us (0.971); the launches traced: 170 us -> 167 us
  waiting for transfers between devices: 14.1 us -> 9.4 us
  starting transfers between devices: 30.2 us -> 34.4 us
  Pallas kernels: 106 us -> 103 us
  blocking collectives: 12.3 us -> 15.3 us
  local copies, waits for them, and re-layouts: 6.2 us -> 4.24 us
    pallas_call x2, Pallas kernels: 7.9 us -> 14.1 us  [own(): pl.pallas_call(lambda *refs: own_kernel(common, *refs), out_shape=jax.Sha...]
    pallas_call x1, Pallas kernels: 55.7 us -> 49.9 us  [on_device(): pl.pallas_call(first_kernel, out_shape=(field, jax.ShapeDtypeStruct((slot...]
    pallas_call x1, Pallas kernels: 29.6 us -> 25.6 us  [on_device(): pl.pallas_call(second_kernel, out_shape=(field, jax.ShapeDtypeStruct((col...]
    all_to_all x1, blocking collectives: 12.3 us -> 15.3 us  [on_device(): lax.all_to_all(back_two, 'col', split_axis=0, concat_axis=0, tiled=True)]
    all_to_all x1, waiting for transfers between devices: 4.13 us -> 1.62 us  [on_device(): lax.all_to_all(send_w, 'col', split_axis=0, concat_axis=0, tiled=True)]
    all_to_all x1, waiting for transfers between devices: 4.75 us -> 2.4 us  [on_device(): lax.all_to_all(back_one, 'col', split_axis=0, concat_axis=0, tiled=True)]
    unnamed x20 -> x14, local copies, waits for them, and re-layouts: 6.2 us -> 4.24 us
    all_to_all x1, starting transfers between devices: 14.3 us -> 16.2 us  [on_device(): lax.all_to_all(dots_two, 'row', split_axis=0, concat_axis=0, tiled=True)]
  transfers between devices with their start and end apart: 4 -> 4, of which waited for: 4 -> 4; matrix products, arithmetic and copies ran while one was open for 0% -> 0% of each run, Pallas kernels for 10% -> 13%
where the time goes in v4:
time: 166 us; the launch traced here: 167 us
  Pallas kernels  103 us (62%)
  starting transfers between devices  34.4 us (21%)
  blocking collectives  15.3 us (9%)
  waiting for transfers between devices  9.4 us (6%)
  local copies, waits for them, and re-layouts  4.24 us (3%)
    pallas_call x1, Pallas kernels, on_device(): pl.pallas_call(first_kernel, out_shape=(field, jax.ShapeDtypeStruct((slot...  49.9 us
    pallas_call x1, Pallas kernels, on_device(): pl.pallas_call(second_kernel, out_shape=(field, jax.ShapeDtypeStruct((col...  25.6 us
    all_to_all x1, starting transfers between devices, on_device(): lax.all_to_all(dots_two, 'row', split_axis=0, concat_axis=0, tiled=True)  16.2 us
    all_to_all x1, blocking collectives, on_device(): lax.all_to_all(back_two, 'col', split_axis=0, concat_axis=0, tiled=True)  15.3 us
    pallas_call x2, Pallas kernels, own(): pl.pallas_call(lambda *refs: own_kernel(common, *refs), out_shape=jax.Sha...  14.1 us
    all_to_all x1, starting transfers between devices, on_device(): far = lax.all_to_all(send, 'col', split_axis=0, concat_axis=0, tiled=True)  8.61 us
    pallas_call x1, Pallas kernels, on_device(): pl.pallas_call(lambda *refs: plan_kernel(cols, count, pairs_dev, *refs),...  7.29 us
    all_to_all x1, starting transfers between devices, on_device(): lax.all_to_all(back_one, 'col', split_axis=0, concat_axis=0, tiled=True)  5.34 us
  transfers between devices with their start and end apart: 4, of which 4 were waited for; matrix products, arithmetic and copies ran while one was open for 0% of the time, Pallas kernels for 13%

profile of v4, /device:TPU:1, one launch (start us, length us, event | category | flops | bytes accessed | tf_op | source)
XLA Modules:
  0.0 167.5 jit_solution(13864381095465996829)
XLA Ops:
  0.6 0.0 copy-start.4
  0.6 0.0 copy-start
  0.7 0.8 copy-done
  1.4 0.0 copy-start.1
  1.4 0.7 copy-done.1
  2.1 0.0 copy-start.2
  2.1 0.7 copy-done.2
  2.8 0.0 copy-start.3
  2.8 0.7 copy-done.3
  3.5 1.9 %order.1 = (f32[4,8,512]{2,1,0:T(8,128)S(1)}, f32[32,8,512]{2,1,0:T(8,128)}, f32[8,128]{1,0:T(8,128)S(1)}) custom-call(f32[8]{0:T(128)S(1)} %copy-done.3, f32[3,2048]{1,0:T(4,128)S(1)} %copy-done, f32[1,2048]{1,0:T(1,128)S(1)} %bitcast.8, s32[1,2048]{1,0:T(1,128)S(1)} %bitcast.9), custom_call_target="tpu_custom_call" | custom-call | tf_op jit(solution)/shard_map/order/pallas_call | solution.py:621
  5.3 8.6 %all-to-all-start = ((f32[32,8,512]{2,1,0:T(8,128)}), f32[32,8,512]{2,1,0:T(8,128)S(1)}, u32[]{:S(2)}, u32[]{:S(2)}) async-start(f32[32,8,512]{2,1,0:T(8,128)} %get-tuple-element.15), calls=%async_computation | async-start | bytes 1048576 | tf_op jit(solution)/shard_map/all_to_all | solution.py:656
  14.0 0.0 copy-start.5
  14.0 0.7 copy-done.5
  14.7 0.0 copy-start.6
  14.7 0.7 copy-done.6
  15.4 7.3 %plan.1.meta_ref = s32[8,64]{1,0:T(8,128)S(1)} custom-call(s32[1]{0:T(128)} %bitcast.2.refs_0_, s32[512]{0:T(512)S(1)} %copy-done.6, s32[3,2048]{1,0:T(4,128)S(1)} %copy-done.5), custom_call_target="tpu_custom_call" | custom-call | flops 1000000000 | bytes 1000000 | tf_op jit(solution)/shard_map/plan/pallas_call | solution.py:657
  22.7 1.8 %all-to-all-done.far_hbm_ref.far_pts_hbm_ref = f32[32,8,512]{2,1,0:T(8,128)S(1)} async-done(((f32[32,8,512]{2,1,0:T(8,128)}), f32[32,8,512]{2,1,0:T(8,128)S(1)}, u32[]{:S(2)}, u32[]{:S(2)}) %all-to-all-start) | async-done | bytes 524320 | tf_op jit(solution)/shard_map/all_to_all | solution.py:656
  24.5 49.9 %cross_first.1 = (f32[4,8,512]{2,1,0:T(8,128)S(1)}, f32[32,8,512]{2,1,0:T(8,128)}, bf16[240,512,512]{2,1,0:T(8,128)(2,1)}) custom-call(f32[8,128]{1,0:T(8,128)S(1)} %get-tuple-element.14.refs_0_.ls_ref, s32[8,64]{1,0:T(8,128)S(1)} %plan.1.meta_ref, f32[4,8,512]{2,1,0:T(8,128)S(1)} %get-tuple-element.13.refs_1_.refs_2_.loc_ref, ...), custom_call_target="tpu_custom_call" | custom-call | flops 10000000000 | bytes 60000000 | tf_op jit(solution)/shard_map/cross_first/pallas_call | solution.py:675
  74.4 5.3 %all-to-all-start.1 = ((f32[32,8,512]{2,1,0:T(8,128)}), f32[32,8,512]{2,1,0:T(8,128)S(1)}, u32[]{:S(2)}, u32[]{:S(2)}) async-start(f32[32,8,512]{2,1,0:T(8,128)} %get-tuple-element.17), calls=%async_computation.1 | async-start | bytes 1048576 | tf_op jit(solution)/shard_map/all_to_all | solution.py:697
  79.7 6.6 %own_first.1.own_ref = f32[2,8,512]{2,1,0:T(8,128)S(1)} custom-call(f32[8,128]{1,0:T(8,128)S(1)} %get-tuple-element.14.refs_0_.ls_ref, f32[4,8,512]{2,1,0:T(8,128)S(1)} %get-tuple-element.13.refs_1_.refs_2_.loc_ref, f32[4,8,512]{2,1,0:T(8,128)S(1)} %get-tuple-element.13.refs_1_.refs_2_.loc_ref), custom_call_target="tpu_custom_call" | custom-call | flops 2000000000 | bytes 1000000 | tf_op jit(solution)/shard_map/own_first/pallas_call | solution.py:640
  86.3 2.4 %all-to-all-done.1.got_ref = f32[32,8,512]{2,1,0:T(8,128)S(1)} async-done(((f32[32,8,512]{2,1,0:T(8,128)}), f32[32,8,512]{2,1,0:T(8,128)S(1)}, u32[]{:S(2)}, u32[]{:S(2)}) %all-to-all-start.1) | async-done | bytes 524320 | tf_op jit(solution)/shard_map/all_to_all | solution.py:697
  88.7 1.7 %combine.1 = (f32[4,8,512]{2,1,0:T(8,128)S(1)}, f32[32,8,512]{2,1,0:T(8,128)}, f32[8,128]{1,0:T(8,128)S(1)}) custom-call(s32[8,64]{1,0:T(8,128)S(1)} %plan.1.meta_ref, f32[4,8,512]{2,1,0:T(8,128)S(1)} %get-tuple-element.13.refs_1_.refs_2_.loc_ref, f32[2,8,512]{2,1,0:T(8,128)S(1)} %own_first.1.own_ref, f32[4,8,512]{2,1,0:T(8,128)S(1)} %get-tuple-element.16.fwd_ref, ...), custom_call_target="tpu_custom_call" | custom-call | tf_op jit(solution)/shard_map/combine/pallas_call | solution.py:699
  90.4 4.3 %all-to-all-start.2 = ((f32[32,8,512]{2,1,0:T(8,128)}), f32[32,8,512]{2,1,0:T(8,128)S(1)}, u32[]{:S(2)}, u32[]{:S(2)}) async-start(f32[32,8,512]{2,1,0:T(8,128)} %get-tuple-element.20), calls=%async_computation.2 | async-start | bytes 1048576 | tf_op jit(solution)/shard_map/all_to_all | solution.py:711
  94.7 7.5 %own_second.1.own_ref = f32[2,8,512]{2,1,0:T(8,128)S(1)} custom-call(f32[8,128]{1,0:T(8,128)S(1)} %get-tuple-element.14.refs_0_.ls_ref, f32[4,8,512]{2,1,0:T(8,128)S(1)} %get-tuple-element.13.refs_1_.refs_2_.loc_ref, f32[4,8,512]{2,1,0:T(8,128)S(1)} %get-tuple-element.18.refs_2_.w_ref), custom_call_target="tpu_custom_call" | custom-call | flops 2000000000 | bytes 1000000 | tf_op jit(solution)/shard_map/own_second/pallas_call | solution.py:640
  102.3 1.6 all-to-all-done.2.far_hbm_ref
  103.9 25.6 %cross_second.1 = (f32[4,8,512]{2,1,0:T(8,128)S(1)}, f32[16,16,640]{2,1,0:T(8,128)S(1)}) custom-call(f32[8,128]{1,0:T(8,128)S(1)} %get-tuple-element.14.refs_0_.ls_ref, s32[8,64]{1,0:T(8,128)S(1)} %plan.1.meta_ref, f32[4,8,512]{2,1,0:T(8,128)S(1)} %get-tuple-element.13.refs_1_.refs_2_.loc_ref, f32[4,8,512]{2,1,0:T(8,128)S(1)} %get-tuple-element.18.refs_2_.w_ref, ...), custom_call_target="tpu_custom_call" | custom-call | flops 5000000000 | bytes 60000000 | tf_op jit(solution)/shard_map/cross_second/pallas_call | solution.py:713
  129.5 15.3 %all_to_all.31.got_ref = f32[16,16,640]{2,1,0:T(8,128)S(1)} all-to-all(f32[16,16,640]{2,1,0:T(8,128)S(1)} %get-tuple-element.23), channel_id=1, replica_groups=mesh['row'=8,'col'=16] {'col'}, dimensions={0} | all-to-all | bytes 1310720 | tf_op jit(solution)/shard_map/all_to_all | solution.py:736
  144.8 0.7 dots.1
  145.5 16.2 %all-to-all-start.4 = ((f32[8,1,128]{2,1,0:T(1,128)}), f32[8,1,128]{2,1,0:T(1,128)S(1)}, u32[]{:S(2)}, u32[]{:S(2)}) async-start(f32[8,1,128]{2,1,0:T(1,128)} %bitcast.4), calls=%async_computation.4 | async-start | bytes 8192 | tf_op jit(solution)/shard_map/all_to_all | solution.py:747
  161.7 0.9 gather.1.z_ref
  162.6 3.6 %all-to-all-done.4 = f32[8,1,128]{2,1,0:T(1,128)S(1)} async-done(((f32[8,1,128]{2,1,0:T(1,128)}), f32[8,1,128]{2,1,0:T(1,128)S(1)}, u32[]{:S(2)}, u32[]{:S(2)}) %all-to-all-start.4) | async-done | bytes 4128 | tf_op jit(solution)/shard_map/all_to_all | solution.py:747
  166.2 0.0 copy-done.4
  166.2 1.3 finish.1
Async XLA Ops:
  0.6 165.6 %copy-start.4 = (f32[8]{0:T(128)S(1)}, f32[8]{0:T(128)}, u32[]{:S(2)}) copy-start(f32[8]{0:T(128)} %noise_ref.1) | copy-start | bytes 100
  0.6 0.8 copy-start
  1.4 0.7 copy-start.1
  2.1 0.7 copy-start.2
  2.8 0.7 copy-start.3
  5.3 19.1 %all-to-all-start = ((f32[32,8,512]{2,1,0:T(8,128)}), f32[32,8,512]{2,1,0:T(8,128)S(1)}, u32[]{:S(2)}, u32[]{:S(2)}) async-start(f32[32,8,512]{2,1,0:T(8,128)} %get-tuple-element.15), calls=%async_computation | async-start | bytes 1048576 | tf_op jit(solution)/shard_map/all_to_all | solution.py:656
  14.0 0.8 copy-start.5
  14.7 0.7 copy-start.6
  74.4 14.3 %all-to-all-start.1 = ((f32[32,8,512]{2,1,0:T(8,128)}), f32[32,8,512]{2,1,0:T(8,128)S(1)}, u32[]{:S(2)}, u32[]{:S(2)}) async-start(f32[32,8,512]{2,1,0:T(8,128)} %get-tuple-element.17), calls=%async_computation.1 | async-start | bytes 1048576 | tf_op jit(solution)/shard_map/all_to_all | solution.py:697
  90.4 13.4 %all-to-all-start.2 = ((f32[32,8,512]{2,1,0:T(8,128)}), f32[32,8,512]{2,1,0:T(8,128)S(1)}, u32[]{:S(2)}, u32[]{:S(2)}) async-start(f32[32,8,512]{2,1,0:T(8,128)} %get-tuple-element.20), calls=%async_computation.2 | async-start | bytes 1048576 | tf_op jit(solution)/shard_map/all_to_all | solution.py:711
  145.5 20.7 %all-to-all-start.4 = ((f32[8,1,128]{2,1,0:T(1,128)}), f32[8,1,128]{2,1,0:T(1,128)S(1)}, u32[]{:S(2)}, u32[]{:S(2)}) async-start(f32[8,1,128]{2,1,0:T(1,128)} %bitcast.4), calls=%async_computation.4 | async-start | bytes 8192 | tf_op jit(solution)/shard_map/all_to_all | solution.py:747

commit v5 on v4

--- a/solution.py
+++ b/solution.py
@@ -358,7 +358,7 @@
             dist_ref[at, :] = distance([coord_ref[a, k, at, :] for k in range(3)], rows, BLOCK)
             return 0
 
-        lax.fori_loop(0, steps, measure, 0, unroll=8)
+        lax.fori_loop(0, steps, measure, 0, unroll=32)
         back_ref[q] = jnp.zeros((LS, BLOCK), F32)
 
         def sweep(ids, number):
@@ -383,7 +383,7 @@
                 return tuple(fresh)
 
             held = tuple(jnp.zeros((8, BLOCK), F32) for _ in ids)
-            held = lax.fori_loop(0, steps, step, held, unroll=8)
+            held = lax.fori_loop(0, steps, step, held, unroll=16)
             for n in range(len(ids)):
                 back_ref[q, pl.ds(ids[n], 1), :] = jnp.sum(held[n], axis=0, keepdims=True)
                 store_copy(slots[n], number + n).start()

time: 166 us -> 164 us (0.988)
  starting transfers between devices: 34.4 us -> 30.1 us
  waiting for transfers between devices: 9.4 us -> 11.1 us
    all_to_all x1, starting transfers between devices: 16.2 us -> 10.7 us  [on_device(): lax.all_to_all(dots_two, 'row', split_axis=0, concat_axis=0, tiled=True)]
    all_to_all x1, starting transfers between devices: 5.34 us -> 7.25 us  [on_device(): lax.all_to_all(back_one, 'col', split_axis=0, concat_axis=0, tiled=True)]
  transfers between devices with their start and end apart: 4 -> 4, of which waited for: 4 -> 4; matrix products, arithmetic and copies ran while one was open for 0% -> 0% of each run, Pallas kernels for 13% -> 14%
where the time goes in v5:
time: 164 us
  Pallas kernels  103 us (63%)
  starting transfers between devices  30.1 us (18%)
  blocking collectives  14.8 us (9%)
  waiting for transfers between devices  11.1 us (7%)
  local copies, waits for them, and re-layouts  4.24 us (3%)
    pallas_call x1, Pallas kernels, on_device(): pl.pallas_call(first_kernel, out_shape=(field, jax.ShapeDtypeStruct((slot...  48.9 us
    pallas_call x1, Pallas kernels, on_device(): pl.pallas_call(second_kernel, out_shape=(field, jax.ShapeDtypeStruct((col...  26.2 us
    all_to_all x1, blocking collectives, on_device(): lax.all_to_all(back_two, 'col', split_axis=0, concat_axis=0, tiled=True)  14.8 us
    pallas_call x2, Pallas kernels, own(): pl.pallas_call(lambda *refs: own_kernel(common, *refs), out_shape=jax.Sha...  14.1 us
    all_to_all x1, starting transfers between devices, on_device(): lax.all_to_all(dots_two, 'row', split_axis=0, concat_axis=0, tiled=True)  10.7 us
    all_to_all x1, starting transfers between devices, on_device(): far = lax.all_to_all(send, 'col', split_axis=0, concat_axis=0, tiled=True)  8.61 us
    all_to_all x1, starting transfers between devices, on_device(): lax.all_to_all(back_one, 'col', split_axis=0, concat_axis=0, tiled=True)  7.25 us
    pallas_call x1, Pallas kernels, on_device(): pl.pallas_call(lambda *refs: plan_kernel(cols, count, pairs_dev, *refs),...  7.24 us
  transfers between devices with their start and end apart: 4, of which 4 were waited for; matrix products, arithmetic and copies ran while one was open for 0% of the time, Pallas kernels for 14%

profile of v5, /device:TPU:1, one launch (start us, length us, event | category | flops | bytes accessed | tf_op | source)
XLA Modules:
  0.0 163.9 jit_solution(745071874617208777)
XLA Ops:
  0.6 0.0 copy-start.4
  0.6 0.0 copy-start
  0.7 0.8 copy-done
  1.4 0.0 copy-start.1
  1.4 0.7 copy-done.1
  2.1 0.0 copy-start.2
  2.1 0.7 copy-done.2
  2.8 0.0 copy-start.3
  2.8 0.7 copy-done.3
  3.5 1.9 %order.1 = (f32[4,8,512]{2,1,0:T(8,128)S(1)}, f32[32,8,512]{2,1,0:T(8,128)}, f32[8,128]{1,0:T(8,128)S(1)}) custom-call(f32[8]{0:T(128)S(1)} %copy-done.3, f32[3,2048]{1,0:T(4,128)S(1)} %copy-done, f32[1,2048]{1,0:T(1,128)S(1)} %bitcast.8, s32[1,2048]{1,0:T(1,128)S(1)} %bitcast.9), custom_call_target="tpu_custom_call" | custom-call | tf_op jit(solution)/shard_map/order/pallas_call | solution.py:621
  5.3 8.6 %all-to-all-start = ((f32[32,8,512]{2,1,0:T(8,128)}), f32[32,8,512]{2,1,0:T(8,128)S(1)}, u32[]{:S(2)}, u32[]{:S(2)}) async-start(f32[32,8,512]{2,1,0:T(8,128)} %get-tuple-element.15), calls=%async_computation | async-start | bytes 1048576 | tf_op jit(solution)/shard_map/all_to_all | solution.py:656
  14.0 0.0 copy-start.5
  14.0 0.7 copy-done.5
  14.7 0.0 copy-start.6
  14.7 0.7 copy-done.6
  15.4 7.2 %plan.1.meta_ref = s32[8,64]{1,0:T(8,128)S(1)} custom-call(s32[1]{0:T(128)} %bitcast.2.refs_0_, s32[512]{0:T(512)S(1)} %copy-done.6, s32[3,2048]{1,0:T(4,128)S(1)} %copy-done.5), custom_call_target="tpu_custom_call" | custom-call | flops 1000000000 | bytes 1000000 | tf_op jit(solution)/shard_map/plan/pallas_call | solution.py:657
  22.6 1.8 %all-to-all-done.far_hbm_ref.far_pts_hbm_ref = f32[32,8,512]{2,1,0:T(8,128)S(1)} async-done(((f32[32,8,512]{2,1,0:T(8,128)}), f32[32,8,512]{2,1,0:T(8,128)S(1)}, u32[]{:S(2)}, u32[]{:S(2)}) %all-to-all-start) | async-done | bytes 524320 | tf_op jit(solution)/shard_map/all_to_all | solution.py:656
  24.5 48.9 %cross_first.1 = (f32[4,8,512]{2,1,0:T(8,128)S(1)}, f32[32,8,512]{2,1,0:T(8,128)}, bf16[240,512,512]{2,1,0:T(8,128)(2,1)}) custom-call(f32[8,128]{1,0:T(8,128)S(1)} %get-tuple-element.14.refs_0_.ls_ref, s32[8,64]{1,0:T(8,128)S(1)} %plan.1.meta_ref, f32[4,8,512]{2,1,0:T(8,128)S(1)} %get-tuple-element.13.refs_1_.refs_2_.loc_ref, ...), custom_call_target="tpu_custom_call" | custom-call | flops 10000000000 | bytes 60000000 | tf_op jit(solution)/shard_map/cross_first/pallas_call | solution.py:675
  73.4 7.3 %all-to-all-start.1 = ((f32[32,8,512]{2,1,0:T(8,128)}), f32[32,8,512]{2,1,0:T(8,128)S(1)}, u32[]{:S(2)}, u32[]{:S(2)}) async-start(f32[32,8,512]{2,1,0:T(8,128)} %get-tuple-element.17), calls=%async_computation.1 | async-start | bytes 1048576 | tf_op jit(solution)/shard_map/all_to_all | solution.py:697
  80.6 6.6 %own_first.1.own_ref = f32[2,8,512]{2,1,0:T(8,128)S(1)} custom-call(f32[8,128]{1,0:T(8,128)S(1)} %get-tuple-element.14.refs_0_.ls_ref, f32[4,8,512]{2,1,0:T(8,128)S(1)} %get-tuple-element.13.refs_1_.refs_2_.loc_ref, f32[4,8,512]{2,1,0:T(8,128)S(1)} %get-tuple-element.13.refs_1_.refs_2_.loc_ref), custom_call_target="tpu_custom_call" | custom-call | flops 2000000000 | bytes 1000000 | tf_op jit(solution)/shard_map/own_first/pallas_call | solution.py:640
  87.2 3.8 %all-to-all-done.1.got_ref = f32[32,8,512]{2,1,0:T(8,128)S(1)} async-done(((f32[32,8,512]{2,1,0:T(8,128)}), f32[32,8,512]{2,1,0:T(8,128)S(1)}, u32[]{:S(2)}, u32[]{:S(2)}) %all-to-all-start.1) | async-done | bytes 524320 | tf_op jit(solution)/shard_map/all_to_all | solution.py:697
  91.0 1.7 %combine.1 = (f32[4,8,512]{2,1,0:T(8,128)S(1)}, f32[32,8,512]{2,1,0:T(8,128)}, f32[8,128]{1,0:T(8,128)S(1)}) custom-call(s32[8,64]{1,0:T(8,128)S(1)} %plan.1.meta_ref, f32[4,8,512]{2,1,0:T(8,128)S(1)} %get-tuple-element.13.refs_1_.refs_2_.loc_ref, f32[2,8,512]{2,1,0:T(8,128)S(1)} %own_first.1.own_ref, f32[4,8,512]{2,1,0:T(8,128)S(1)} %get-tuple-element.16.fwd_ref, ...), custom_call_target="tpu_custom_call" | custom-call | tf_op jit(solution)/shard_map/combine/pallas_call | solution.py:699
  92.7 3.6 %all-to-all-start.2 = ((f32[32,8,512]{2,1,0:T(8,128)}), f32[32,8,512]{2,1,0:T(8,128)S(1)}, u32[]{:S(2)}, u32[]{:S(2)}) async-start(f32[32,8,512]{2,1,0:T(8,128)} %get-tuple-element.20), calls=%async_computation.2 | async-start | bytes 1048576 | tf_op jit(solution)/shard_map/all_to_all | solution.py:711
  96.3 7.5 %own_second.1.own_ref = f32[2,8,512]{2,1,0:T(8,128)S(1)} custom-call(f32[8,128]{1,0:T(8,128)S(1)} %get-tuple-element.14.refs_0_.ls_ref, f32[4,8,512]{2,1,0:T(8,128)S(1)} %get-tuple-element.13.refs_1_.refs_2_.loc_ref, f32[4,8,512]{2,1,0:T(8,128)S(1)} %get-tuple-element.18.refs_2_.w_ref), custom_call_target="tpu_custom_call" | custom-call | flops 2000000000 | bytes 1000000 | tf_op jit(solution)/shard_map/own_second/pallas_call | solution.py:640
  103.8 1.9 %all-to-all-done.2.far_hbm_ref = f32[32,8,512]{2,1,0:T(8,128)S(1)} async-done(((f32[32,8,512]{2,1,0:T(8,128)}), f32[32,8,512]{2,1,0:T(8,128)S(1)}, u32[]{:S(2)}, u32[]{:S(2)}) %all-to-all-start.2) | async-done | bytes 524320 | tf_op jit(solution)/shard_map/all_to_all | solution.py:711
  105.7 26.2 %cross_second.1 = (f32[4,8,512]{2,1,0:T(8,128)S(1)}, f32[16,16,640]{2,1,0:T(8,128)S(1)}) custom-call(f32[8,128]{1,0:T(8,128)S(1)} %get-tuple-element.14.refs_0_.ls_ref, s32[8,64]{1,0:T(8,128)S(1)} %plan.1.meta_ref, f32[4,8,512]{2,1,0:T(8,128)S(1)} %get-tuple-element.13.refs_1_.refs_2_.loc_ref, f32[4,8,512]{2,1,0:T(8,128)S(1)} %get-tuple-element.18.refs_2_.w_ref, ...), custom_call_target="tpu_custom_call" | custom-call | flops 5000000000 | bytes 60000000 | tf_op jit(solution)/shard_map/cross_second/pallas_call | solution.py:713
  131.9 14.8 %all_to_all.31.got_ref = f32[16,16,640]{2,1,0:T(8,128)S(1)} all-to-all(f32[16,16,640]{2,1,0:T(8,128)S(1)} %get-tuple-element.23), channel_id=1, replica_groups=mesh['row'=8,'col'=16] {'col'}, dimensions={0} | all-to-all | bytes 1310720 | tf_op jit(solution)/shard_map/all_to_all | solution.py:736
  146.7 0.7 dots.1
  147.4 10.7 %all-to-all-start.4 = ((f32[8,1,128]{2,1,0:T(1,128)}), f32[8,1,128]{2,1,0:T(1,128)S(1)}, u32[]{:S(2)}, u32[]{:S(2)}) async-start(f32[8,1,128]{2,1,0:T(1,128)} %bitcast.4), calls=%async_computation.4 | async-start | bytes 8192 | tf_op jit(solution)/shard_map/all_to_all | solution.py:747
  158.1 0.9 gather.1.z_ref
  159.0 3.6 %all-to-all-done.4 = f32[8,1,128]{2,1,0:T(1,128)S(1)} async-done(((f32[8,1,128]{2,1,0:T(1,128)}), f32[8,1,128]{2,1,0:T(1,128)S(1)}, u32[]{:S(2)}, u32[]{:S(2)}) %all-to-all-start.4) | async-done | bytes 4128 | tf_op jit(solution)/shard_map/all_to_all | solution.py:747
  162.6 0.0 copy-done.4
  162.6 1.3 finish.1
Async XLA Ops:
  0.6 162.0 %copy-start.4 = (f32[8]{0:T(128)S(1)}, f32[8]{0:T(128)}, u32[]{:S(2)}) copy-start(f32[8]{0:T(128)} %noise_ref.1) | copy-start | bytes 100
  0.6 0.8 copy-start
  1.4 0.7 copy-start.1
  2.1 0.7 copy-start.2
  2.8 0.7 copy-start.3
  5.3 19.1 %all-to-all-start = ((f32[32,8,512]{2,1,0:T(8,128)}), f32[32,8,512]{2,1,0:T(8,128)S(1)}, u32[]{:S(2)}, u32[]{:S(2)}) async-start(f32[32,8,512]{2,1,0:T(8,128)} %get-tuple-element.15), calls=%async_computation | async-start | bytes 1048576 | tf_op jit(solution)/shard_map/all_to_all | solution.py:656
  14.0 0.8 copy-start.5
  14.7 0.7 copy-start.6
  73.4 17.6 %all-to-all-start.1 = ((f32[32,8,512]{2,1,0:T(8,128)}), f32[32,8,512]{2,1,0:T(8,128)S(1)}, u32[]{:S(2)}, u32[]{:S(2)}) async-start(f32[32,8,512]{2,1,0:T(8,128)} %get-tuple-element.17), calls=%async_computation.1 | async-start | bytes 1048576 | tf_op jit(solution)/shard_map/all_to_all | solution.py:697
  92.7 13.0 %all-to-all-start.2 = ((f32[32,8,512]{2,1,0:T(8,128)}), f32[32,8,512]{2,1,0:T(8,128)S(1)}, u32[]{:S(2)}, u32[]{:S(2)}) async-start(f32[32,8,512]{2,1,0:T(8,128)} %get-tuple-element.20), calls=%async_computation.2 | async-start | bytes 1048576 | tf_op jit(solution)/shard_map/all_to_all | solution.py:711
  147.4 15.2 %all-to-all-start.4 = ((f32[8,1,128]{2,1,0:T(1,128)}), f32[8,1,128]{2,1,0:T(1,128)S(1)}, u32[]{:S(2)}, u32[]{:S(2)}) async-start(f32[8,1,128]{2,1,0:T(1,128)} %bitcast.4), calls=%async_computation.4 | async-start | bytes 8192 | tf_op jit(solution)/shard_map/all_to_all | solution.py:747

commit v6 on v5

--- a/solution.py
+++ b/solution.py
@@ -383,7 +383,7 @@
                 return tuple(fresh)
 
             held = tuple(jnp.zeros((8, BLOCK), F32) for _ in ids)
-            held = lax.fori_loop(0, steps, step, held, unroll=16)
+            held = lax.fori_loop(0, steps, step, held, unroll=32)
             for n in range(len(ids)):
                 back_ref[q, pl.ds(ids[n], 1), :] = jnp.sum(held[n], axis=0, keepdims=True)
                 store_copy(slots[n], number + n).start()

time: 164 us -> 164 us (level)
  no operation moved by 1% of the time
where the time goes in v6:
time: 164 us
  Pallas kernels  104 us (63%)
  starting transfers between devices  28.9 us (18%)
  blocking collectives  15.7 us (10%)
  waiting for transfers between devices  10.3 us (6%)
  local copies, waits for them, and re-layouts  4.24 us (3%)
    pallas_call x1, Pallas kernels, on_device(): pl.pallas_call(first_kernel, out_shape=(field, jax.ShapeDtypeStruct((slot...  49.3 us
    pallas_call x1, Pallas kernels, on_device(): pl.pallas_call(second_kernel, out_shape=(field, jax.ShapeDtypeStruct((col...  26.4 us
    all_to_all x1, blocking collectives, on_device(): lax.all_to_all(back_two, 'col', split_axis=0, concat_axis=0, tiled=True)  15.7 us
    pallas_call x2, Pallas kernels, own(): pl.pallas_call(lambda *refs: own_kernel(common, *refs), out_shape=jax.Sha...  14.1 us
    all_to_all x1, starting transfers between devices, on_device(): lax.all_to_all(dots_two, 'row', split_axis=0, concat_axis=0, tiled=True)  10.5 us
    all_to_all x1, starting transfers between devices, on_device(): far = lax.all_to_all(send, 'col', split_axis=0, concat_axis=0, tiled=True)  8.61 us
    pallas_call x1, Pallas kernels, on_device(): pl.pallas_call(lambda *refs: plan_kernel(cols, count, pairs_dev, *refs),...  7.29 us
    all_to_all x1, starting transfers between devices, on_device(): lax.all_to_all(back_one, 'col', split_axis=0, concat_axis=0, tiled=True)  6.21 us
  transfers between devices with their start and end apart: 4, of which 4 were waited for; matrix products, arithmetic and copies ran while one was open for 0% of the time, Pallas kernels for 14%

profile of v6, /device:TPU:1, one launch (start us, length us, event | category | flops | bytes accessed | tf_op | source)
XLA Modules:
  0.0 163.5 jit_solution(12472810512451263229)
XLA Ops:
  0.6 0.0 copy-start.4
  0.6 0.0 copy-start
  0.7 0.8 copy-done
  1.4 0.0 copy-start.1
  1.4 0.7 copy-done.1
  2.1 0.0 copy-start.2
  2.1 0.7 copy-done.2
  2.8 0.0 copy-start.3
  2.8 0.7 copy-done.3
  3.5 1.9 %order.1 = (f32[4,8,512]{2,1,0:T(8,128)S(1)}, f32[32,8,512]{2,1,0:T(8,128)}, f32[8,128]{1,0:T(8,128)S(1)}) custom-call(f32[8]{0:T(128)S(1)} %copy-done.3, f32[3,2048]{1,0:T(4,128)S(1)} %copy-done, f32[1,2048]{1,0:T(1,128)S(1)} %bitcast.8, s32[1,2048]{1,0:T(1,128)S(1)} %bitcast.9), custom_call_target="tpu_custom_call" | custom-call | tf_op jit(solution)/shard_map/order/pallas_call | solution.py:621
  5.3 8.6 %all-to-all-start = ((f32[32,8,512]{2,1,0:T(8,128)}), f32[32,8,512]{2,1,0:T(8,128)S(1)}, u32[]{:S(2)}, u32[]{:S(2)}) async-start(f32[32,8,512]{2,1,0:T(8,128)} %get-tuple-element.15), calls=%async_computation | async-start | bytes 1048576 | tf_op jit(solution)/shard_map/all_to_all | solution.py:656
  14.0 0.0 copy-start.5
  14.0 0.7 copy-done.5
  14.7 0.0 copy-start.6
  14.7 0.7 copy-done.6
  15.4 7.3 %plan.1.meta_ref = s32[8,64]{1,0:T(8,128)S(1)} custom-call(s32[1]{0:T(128)} %bitcast.2.refs_0_, s32[512]{0:T(512)S(1)} %copy-done.6, s32[3,2048]{1,0:T(4,128)S(1)} %copy-done.5), custom_call_target="tpu_custom_call" | custom-call | flops 1000000000 | bytes 1000000 | tf_op jit(solution)/shard_map/plan/pallas_call | solution.py:657
  22.7 1.8 %all-to-all-done.far_hbm_ref.far_pts_hbm_ref = f32[32,8,512]{2,1,0:T(8,128)S(1)} async-done(((f32[32,8,512]{2,1,0:T(8,128)}), f32[32,8,512]{2,1,0:T(8,128)S(1)}, u32[]{:S(2)}, u32[]{:S(2)}) %all-to-all-start) | async-done | bytes 524320 | tf_op jit(solution)/shard_map/all_to_all | solution.py:656
  24.5 49.3 %cross_first.1 = (f32[4,8,512]{2,1,0:T(8,128)S(1)}, f32[32,8,512]{2,1,0:T(8,128)}, bf16[240,512,512]{2,1,0:T(8,128)(2,1)}) custom-call(f32[8,128]{1,0:T(8,128)S(1)} %get-tuple-element.14.refs_0_.ls_ref, s32[8,64]{1,0:T(8,128)S(1)} %plan.1.meta_ref, f32[4,8,512]{2,1,0:T(8,128)S(1)} %get-tuple-element.13.refs_1_.refs_2_.loc_ref, ...), custom_call_target="tpu_custom_call" | custom-call | flops 10000000000 | bytes 60000000 | tf_op jit(solution)/shard_map/cross_first/pallas_call | solution.py:675
  73.7 6.2 %all-to-all-start.1 = ((f32[32,8,512]{2,1,0:T(8,128)}), f32[32,8,512]{2,1,0:T(8,128)S(1)}, u32[]{:S(2)}, u32[]{:S(2)}) async-start(f32[32,8,512]{2,1,0:T(8,128)} %get-tuple-element.17), calls=%async_computation.1 | async-start | bytes 1048576 | tf_op jit(solution)/shard_map/all_to_all | solution.py:697
  80.0 6.6 %own_first.1.own_ref = f32[2,8,512]{2,1,0:T(8,128)S(1)} custom-call(f32[8,128]{1,0:T(8,128)S(1)} %get-tuple-element.14.refs_0_.ls_ref, f32[4,8,512]{2,1,0:T(8,128)S(1)} %get-tuple-element.13.refs_1_.refs_2_.loc_ref, f32[4,8,512]{2,1,0:T(8,128)S(1)} %get-tuple-element.13.refs_1_.refs_2_.loc_ref), custom_call_target="tpu_custom_call" | custom-call | flops 2000000000 | bytes 1000000 | tf_op jit(solution)/shard_map/own_first/pallas_call | solution.py:640
  86.6 3.3 %all-to-all-done.1.got_ref = f32[32,8,512]{2,1,0:T(8,128)S(1)} async-done(((f32[32,8,512]{2,1,0:T(8,128)}), f32[32,8,512]{2,1,0:T(8,128)S(1)}, u32[]{:S(2)}, u32[]{:S(2)}) %all-to-all-start.1) | async-done | bytes 524320 | tf_op jit(solution)/shard_map/all_to_all | solution.py:697
  89.9 1.7 %combine.1 = (f32[4,8,512]{2,1,0:T(8,128)S(1)}, f32[32,8,512]{2,1,0:T(8,128)}, f32[8,128]{1,0:T(8,128)S(1)}) custom-call(s32[8,64]{1,0:T(8,128)S(1)} %plan.1.meta_ref, f32[4,8,512]{2,1,0:T(8,128)S(1)} %get-tuple-element.13.refs_1_.refs_2_.loc_ref, f32[2,8,512]{2,1,0:T(8,128)S(1)} %own_first.1.own_ref, f32[4,8,512]{2,1,0:T(8,128)S(1)} %get-tuple-element.16.fwd_ref, ...), custom_call_target="tpu_custom_call" | custom-call | tf_op jit(solution)/shard_map/combine/pallas_call | solution.py:699
  91.6 3.6 %all-to-all-start.2 = ((f32[32,8,512]{2,1,0:T(8,128)}), f32[32,8,512]{2,1,0:T(8,128)S(1)}, u32[]{:S(2)}, u32[]{:S(2)}) async-start(f32[32,8,512]{2,1,0:T(8,128)} %get-tuple-element.20), calls=%async_computation.2 | async-start | bytes 1048576 | tf_op jit(solution)/shard_map/all_to_all | solution.py:711
  95.2 7.5 %own_second.1.own_ref = f32[2,8,512]{2,1,0:T(8,128)S(1)} custom-call(f32[8,128]{1,0:T(8,128)S(1)} %get-tuple-element.14.refs_0_.ls_ref, f32[4,8,512]{2,1,0:T(8,128)S(1)} %get-tuple-element.13.refs_1_.refs_2_.loc_ref, f32[4,8,512]{2,1,0:T(8,128)S(1)} %get-tuple-element.18.refs_2_.w_ref), custom_call_target="tpu_custom_call" | custom-call | flops 2000000000 | bytes 1000000 | tf_op jit(solution)/shard_map/own_second/pallas_call | solution.py:640
  102.7 1.6 %all-to-all-done.2.far_hbm_ref = f32[32,8,512]{2,1,0:T(8,128)S(1)} async-done(((f32[32,8,512]{2,1,0:T(8,128)}), f32[32,8,512]{2,1,0:T(8,128)S(1)}, u32[]{:S(2)}, u32[]{:S(2)}) %all-to-all-start.2) | async-done | bytes 524320 | tf_op jit(solution)/shard_map/all_to_all | solution.py:711
  104.4 26.4 %cross_second.1 = (f32[4,8,512]{2,1,0:T(8,128)S(1)}, f32[16,16,640]{2,1,0:T(8,128)S(1)}) custom-call(f32[8,128]{1,0:T(8,128)S(1)} %get-tuple-element.14.refs_0_.ls_ref, s32[8,64]{1,0:T(8,128)S(1)} %plan.1.meta_ref, f32[4,8,512]{2,1,0:T(8,128)S(1)} %get-tuple-element.13.refs_1_.refs_2_.loc_ref, f32[4,8,512]{2,1,0:T(8,128)S(1)} %get-tuple-element.18.refs_2_.w_ref, ...), custom_call_target="tpu_custom_call" | custom-call | flops 5000000000 | bytes 60000000 | tf_op jit(solution)/shard_map/cross_second/pallas_call | solution.py:713
  130.8 15.7 %all_to_all.31.got_ref = f32[16,16,640]{2,1,0:T(8,128)S(1)} all-to-all(f32[16,16,640]{2,1,0:T(8,128)S(1)} %get-tuple-element.23), channel_id=1, replica_groups=mesh['row'=8,'col'=16] {'col'}, dimensions={0} | all-to-all | bytes 1310720 | tf_op jit(solution)/shard_map/all_to_all | solution.py:736
  146.5 0.7 dots.1
  147.2 10.5 %all-to-all-start.4 = ((f32[8,1,128]{2,1,0:T(1,128)}), f32[8,1,128]{2,1,0:T(1,128)S(1)}, u32[]{:S(2)}, u32[]{:S(2)}) async-start(f32[8,1,128]{2,1,0:T(1,128)} %bitcast.4), calls=%async_computation.4 | async-start | bytes 8192 | tf_op jit(solution)/shard_map/all_to_all | solution.py:747
  157.7 0.9 gather.1.z_ref
  158.6 3.6 %all-to-all-done.4 = f32[8,1,128]{2,1,0:T(1,128)S(1)} async-done(((f32[8,1,128]{2,1,0:T(1,128)}), f32[8,1,128]{2,1,0:T(1,128)S(1)}, u32[]{:S(2)}, u32[]{:S(2)}) %all-to-all-start.4) | async-done | bytes 4128 | tf_op jit(solution)/shard_map/all_to_all | solution.py:747
  162.2 0.0 copy-done.4
  162.2 1.3 finish.1
Async XLA Ops:
  0.6 161.6 %copy-start.4 = (f32[8]{0:T(128)S(1)}, f32[8]{0:T(128)}, u32[]{:S(2)}) copy-start(f32[8]{0:T(128)} %noise_ref.1) | copy-start | bytes 100
  0.6 0.8 copy-start
  1.4 0.7 copy-start.1
  2.1 0.7 copy-start.2
  2.8 0.7 copy-start.3
  5.3 19.1 %all-to-all-start = ((f32[32,8,512]{2,1,0:T(8,128)}), f32[32,8,512]{2,1,0:T(8,128)S(1)}, u32[]{:S(2)}, u32[]{:S(2)}) async-start(f32[32,8,512]{2,1,0:T(8,128)} %get-tuple-element.15), calls=%async_computation | async-start | bytes 1048576 | tf_op jit(solution)/shard_map/all_to_all | solution.py:656
  14.0 0.8 copy-start.5
  14.7 0.7 copy-start.6
  73.7 16.1 %all-to-all-start.1 = ((f32[32,8,512]{2,1,0:T(8,128)}), f32[32,8,512]{2,1,0:T(8,128)S(1)}, u32[]{:S(2)}, u32[]{:S(2)}) async-start(f32[32,8,512]{2,1,0:T(8,128)} %get-tuple-element.17), calls=%async_computation.1 | async-start | bytes 1048576 | tf_op jit(solution)/shard_map/all_to_all | solution.py:697
  91.6 12.8 %all-to-all-start.2 = ((f32[32,8,512]{2,1,0:T(8,128)}), f32[32,8,512]{2,1,0:T(8,128)S(1)}, u32[]{:S(2)}, u32[]{:S(2)}) async-start(f32[32,8,512]{2,1,0:T(8,128)} %get-tuple-element.20), calls=%async_computation.2 | async-start | bytes 1048576 | tf_op jit(solution)/shard_map/all_to_all | solution.py:711
  147.2 15.0 %all-to-all-start.4 = ((f32[8,1,128]{2,1,0:T(1,128)}), f32[8,1,128]{2,1,0:T(1,128)S(1)}, u32[]{:S(2)}, u32[]{:S(2)}) async-start(f32[8,1,128]{2,1,0:T(1,128)} %bitcast.4), calls=%async_computation.4 | async-start | bytes 8192 | tf_op jit(solution)/shard_map/all_to_all | solution.py:747
